TPU v7x, 32 devices: a whole 2x2x4 slice. The times are simulated.
32 devices in a mesh: tm: 16 (over z, x, core), mode: 2 (over y).
Axes of the slice: x: 2, y: 2, z: 4, core: 2. Of those that a mesh axis runs over, the one named last changes fastest.
Arguments:
- fields: float32 [16, 2, 1024, 1024], P('tm', None, 'mode'), may hold values from -2.5 to 2.5
- offsets: int32 [16, 2], P('tm'), may hold values from 1 to 4
Outputs:
- products: float32 [16, 2, 2, 1024, 1024], P('tm', None, None, 'mode')
- correlators: float32 [16, 2], P('tm')
All inputs are finite; a program needn't handle non-finite values.
Results may differ from a plain program's by a relative error of at most 0.0003.
Values sent between devices are 32-bit elements; how exact they have to be, the bound alone decides.
No kernel may reach another device: no remote copies, remote signals or barrier semaphores. Data moves between devices by JAX's collectives and lax.ppermute only.
A program may use at most 128 MiB of HBM per device.

v0:
```python
import jax
import jax.numpy as jnp
from jax import lax
from jax.sharding import PartitionSpec as P


def passed_along(block, axis, distance):
    devices = range(lax.axis_size(axis))
    route = [((i - distance) % len(devices), i) for i in devices]
    return lax.ppermute(block, axis, route)


def body(fields, offsets):
    hi = lax.Precision.HIGHEST
    own = fields[0]
    pairs = offsets.shape[1]
    width = own.shape[2]
    candidates = []
    for reach_step in range(1, 5):
        candidates.append(passed_along(fields, "tm", -reach_step))
    chosen = []
    for pair_index in range(pairs):
        picked = jnp.zeros_like(own)
        for reach_step in range(1, 5):
            picked = jnp.where(
                offsets[0, pair_index] == reach_step, candidates[reach_step - 1][0], picked
            )
        chosen.append(picked)
    sinks = jnp.stack(chosen)
    piece = lax.all_gather(sinks, "mode", axis=2, tiled=True)
    left_re = own[0]
    left_im = own[1]
    real = jnp.einsum("rc,kcn->krn", left_re, piece[:, 0], precision=hi) - jnp.einsum(
        "rc,kcn->krn", left_im, piece[:, 1], precision=hi
    )
    imag = jnp.einsum("rc,kcn->krn", left_re, piece[:, 1], precision=hi) + jnp.einsum(
        "rc,kcn->krn", left_im, piece[:, 0], precision=hi
    )
    forward = jnp.stack([real, imag], axis=1)
    piece = lax.all_gather(own, "mode", axis=1, tiled=True)
    left_re = sinks[:, 0]
    left_im = sinks[:, 1]
    real = jnp.einsum("krc,cn->krn", left_re, piece[0], precision=hi) - jnp.einsum(
        "krc,cn->krn", left_im, piece[1], precision=hi
    )
    imag = jnp.einsum("krc,cn->krn", left_re, piece[1], precision=hi) + jnp.einsum(
        "krc,cn->krn", left_im, piece[0], precision=hi
    )
    partner = jnp.stack([real, imag], axis=1)
    partial_trace = jnp.sum(forward * partner, axis=(1, 2, 3)) / jnp.float32(width)
    traces = lax.psum(partial_trace, "mode")
    return (forward[None], traces[None])


def solution(mesh):
    in_specs = (P("tm", None, "mode", None), P("tm", None))
    out_specs = (P("tm", None, None, "mode", None), P("tm", None))
    return jax.shard_map(body, mesh=mesh, in_specs=in_specs, out_specs=out_specs, check_vma=False)
```

profile of v0, /device:TPU:0, one launch (start us, length us, event | category | flops | bytes accessed | tf_op | source)
XLA Modules:
  0.0 634.8 jit_solution(8443417480938746181)
XLA Ops:
  7.2 0.0 all-gather.6.cloned.1.call-start
  7.2 0.7 all-gather.6.cloned.1.call-update
  7.9 0.0 copy-start.9
  7.9 0.0 all-gather.4.cloned.1.call-start
  8.0 5.4 copy.4
  13.3 5.0 collective-permute-start
  18.4 0.0 collective-permute-start.1
  18.4 1.4 collective-permute-start.2
  19.8 1.3 collective-permute-start.3
  21.1 0.0 copy-done.9
  21.1 0.6 fusion.34
  26.5 83.2 %collective-permute-done = f32[1,2,512,1024]{2,3,0,1:T(8,128)S(1)} collective-permute-done((f32[1,2,512,1024]{2,3,0,1:T(8,128)}, f32[1,2,512,1024]{2,3,0,1:T(8,128)S(1)}, u32[]{:S(2)}, u32[]{:S(2)}) %collective-permute-start) | collective-permute-done | bytes 4194336 | tf_op jit(solution)/shard_map/ppermute | solution.py:10
  109.7 89.9 %collective-permute-done.1 = f32[1,2,512,1024]{2,3,0,1:T(8,128)S(1)} collective-permute-done((f32[1,2,512,1024]{2,3,0,1:T(8,128)}, f32[1,2,512,1024]{2,3,0,1:T(8,128)S(1)}, u32[]{:S(2)}, u32[]{:S(2)}) %collective-permute-start.1) | collective-permute-done | bytes 4194336 | tf_op jit(solution)/shard_map/ppermute | solution.py:10
  199.6 88.7 %collective-permute-done.2 = f32[1,2,512,1024]{2,3,0,1:T(8,128)S(1)} collective-permute-done((f32[1,2,512,1024]{2,3,0,1:T(8,128)}, f32[1,2,512,1024]{2,3,0,1:T(8,128)S(1)}, u32[]{:S(2)}, u32[]{:S(2)}) %collective-permute-start.2) | collective-permute-done | bytes 4194336 | tf_op jit(solution)/shard_map/ppermute | solution.py:10
  288.3 44.9 %collective-permute-done.3 = f32[1,2,512,1024]{2,3,0,1:T(8,128)S(1)} collective-permute-done((f32[1,2,512,1024]{2,3,0,1:T(8,128)}, f32[1,2,512,1024]{2,3,0,1:T(8,128)S(1)}, u32[]{:S(2)}, u32[]{:S(2)}) %collective-permute-start.3) | collective-permute-done | bytes 4194336 | tf_op jit(solution)/shard_map/ppermute | solution.py:10
  333.2 2.1 select_select_fusion.1
  335.4 0.0 copy-start
  335.4 0.0 copy-start.2
  335.4 2.0 copy-done
  337.4 1.3 copy-done.2
  338.6 4.4 pad_maximum_fusion
  343.0 0.0 all-gather.4.cloned.1.call-update
  343.0 0.0 all-gather.6.cloned.1.call-done
  343.0 0.0 copy-start.1
  343.0 0.0 copy-start.3
  343.1 0.0 copy-start.6
  343.1 16.8 %fusion.13 = f32[2,512,1024]{1,2,0:T(8,128)S(1)} fusion(f32[1,2,1024,1024]{3,2,1,0:T(8,128)} %all-gather.6.cloned.1.call-done, f32[1,2,512,1024]{2,3,0,1:T(8,128)} %copy-done, f32[1,2,512,1024]{2,3,0,1:T(8,128)} %copy-done.2), kind=kOutput, calls=%fused_computation.30 | convolution fusion | flops 12885950464 | bytes 16777216 | tf_op jit(solution)/shard_map/krc,cn->krn/dot_general | solution.py:43
  359.9 0.0 copy-done.1
  359.9 0.0 copy-done.3
  359.9 0.0 copy-done.6
  359.9 14.7 %fusion.10 = f32[2,512,1024]{1,2,0:T(8,128)S(1)} fusion(f32[1,2,1024,1024]{3,2,1,0:T(8,128)S(1)} %copy-done.6, f32[1,2,512,1024]{2,3,0,1:T(8,128)S(1)} %copy-done.1, f32[1,2,512,1024]{2,3,0,1:T(8,128)S(1)} %copy-done.3), kind=kOutput, calls=%fused_computation.27 | convolution fusion | flops 12885950464 | bytes 16777216 | tf_op jit(solution)/shard_map/krc,cn->krn/dot_general | solution.py:46
  374.7 15.3 %subtract_bitcast_fusion = f32[2,1,512,1024]{2,3,0,1:T(8,128)} fusion(f32[2,512,1024]{1,2,0:T(8,128)S(1)} %fusion.13, f32[1,2,1024,1024]{3,2,1,0:T(8,128)S(1)} %copy-done.6, f32[1,2,512,1024]{2,3,0,1:T(8,128)S(1)} %copy-done.1, f32[1,2,512,1024]{2,3,0,1:T(8,128)S(1)} %copy-done.3), kind=kOutput, calls=%fused_computation.22 | convolution fusion | flops 12886999040 | bytes 20971520 | tf_op jit(solution)/shard_map/krc,cn->krn/dot_general | solution.py:43
  390.0 15.5 %add_bitcast_fusion = f32[2,1,512,1024]{2,3,0,1:T(8,128)} fusion(f32[2,512,1024]{1,2,0:T(8,128)S(1)} %fusion.10, f32[1,2,1024,1024]{3,2,1,0:T(8,128)S(1)} %copy-done.6, f32[1,2,512,1024]{2,3,0,1:T(8,128)S(1)} %copy-done.1, f32[1,2,512,1024]{2,3,0,1:T(8,128)S(1)} %copy-done.3), kind=kOutput, calls=%fused_computation.21 | convolution fusion | flops 12886999040 | bytes 20971520 | tf_op jit(solution)/shard_map/krc,cn->krn/dot_general | solution.py:46
  405.5 137.8 %all-gather.4.cloned.1.call-done = f32[2,2,1024,1024]{2,3,0,1:T(8,128)} async-done(((f32[2,2,512,1024]{2,3,0,1:T(8,128)}), f32[2,2,1024,1024]{2,3,0,1:T(8,128)}) %all-gather.4.cloned.1.call-update) | async-done | bytes 16777232 | tf_op jit(solution)/shard_map/all_gather | solution.py:30
  543.3 0.0 copy-start.4
  543.3 0.0 copy-start.5
  543.3 17.0 %fusion.4 = f32[2,1024,512]{2,1,0:T(8,128)S(1)} fusion(f32[2,2,1024,1024]{2,3,0,1:T(8,128)} %all-gather.4.cloned.1.call-done, f32[1,2,512,1024]{3,2,1,0:T(8,128)} %param.2), kind=kOutput, calls=%fused_computation.13 | convolution fusion | flops 12884901888 | bytes 14680064 | tf_op jit(solution)/shard_map/rc,kcn->krn/dot_general | solution.py:33
  560.3 0.0 copy-done.4
  560.3 15.9 %fusion.1 = f32[2,1024,512]{2,1,0:T(8,128)S(1)} fusion(f32[2,2,1024,1024]{2,3,0,1:T(8,128)} %all-gather.4.cloned.1.call-done, f32[1,2,512,1024]{3,2,1,0:T(8,128)S(1)} %copy-done.4), kind=kOutput, calls=%fused_computation.10 | convolution fusion | flops 12884901888 | bytes 14680064 | tf_op jit(solution)/shard_map/rc,kcn->krn/dot_general | solution.py:36
  576.2 0.0 copy-done.5
  576.2 15.4 %subtract_bitcast_fusion.1 = f32[2,1,512,1024]{2,3,0,1:T(8,128)} fusion(f32[2,1024,512]{2,1,0:T(8,128)S(1)} %fusion.4, f32[1,2,512,1024]{3,2,1,0:T(8,128)S(1)} %copy-done.4, f32[2,2,1024,1024]{2,3,0,1:T(8,128)S(1)} %copy-done.5), kind=kOutput, calls=%fused_computation.24 | convolution fusion | flops 12885950464 | bytes 18874368 | tf_op jit(solution)/shard_map/rc,kcn->krn/dot_general | solution.py:33
  591.6 0.0 copy-start.7
  591.6 15.4 %add_bitcast_fusion.1 = f32[2,1,512,1024]{2,3,0,1:T(8,128)} fusion(f32[2,1024,512]{2,1,0:T(8,128)S(1)} %fusion.1, f32[1,2,512,1024]{3,2,1,0:T(8,128)S(1)} %copy-done.4, f32[2,2,1024,1024]{2,3,0,1:T(8,128)S(1)} %copy-done.5), kind=kOutput, calls=%fused_computation.23 | convolution fusion | flops 12885950464 | bytes 18874368 | tf_op jit(solution)/shard_map/rc,kcn->krn/dot_general | solution.py:36
  607.0 0.0 copy-done.7
  607.0 0.0 copy-done.8
  607.0 6.7 %fusion = (f32[2]{0:T(128)S(1)}, f32[1,2,2,512,1024]{3,4,1,2,0:T(8,128)}) fusion(f32[2,1,512,1024]{2,3,0,1:T(8,128)S(1)} %copy-done.8, f32[2,1,512,1024]{2,3,0,1:T(8,128)S(1)} %copy-done.7, f32[2,1,512,1024]{2,3,0,1:T(8,128)} %add_bitcast_fusion.1, f32[2,1,512,1024]{2,3,0,1:T(8,128)} %subtract_bitcast_fusion.1), kind=kLoop, calls=%fused_computation.9 | loop fusion | flops 8388606 | bytes 25165832 | tf_op jit(solution)/shard_map/reduce_sum | solution.py:50
  613.6 8.7 %copy.16 = f32[1,2,2,512,1024]{4,3,2,1,0:T(8,128)} copy(f32[1,2,2,512,1024]{3,4,1,2,0:T(8,128)} %get-tuple-element.7) | data formatting | bytes 16777216
  622.3 5.4 psum.7
  (2 shorter events, 0.0 us)
Async XLA Ops:
  7.2 335.9 %all-gather.6.cloned.1.call-start = ((), (), s32[]{:S(2)}) async-start(), calls=%async_computation.1 | async-start | bytes 12582912 | tf_op jit(solution)/shard_map/all_gather | solution.py:40
  7.9 13.2 %copy-start.9 = (s32[1,2]{1,0:T(1,128)S(1)}, s32[1,2]{1,0:T(1,128)}, u32[]{:S(2)}) copy-start(s32[1,2]{1,0:T(1,128)} %param.3) | copy-start | bytes 28
  7.9 535.4 %all-gather.4.cloned.1.call-start = ((), (), s32[]{:S(2)}) async-start(), calls=%async_computation | async-start | bytes 25165824 | tf_op jit(solution)/shard_map/all_gather | solution.py:30
  13.3 96.3 %collective-permute-start = (f32[1,2,512,1024]{2,3,0,1:T(8,128)}, f32[1,2,512,1024]{2,3,0,1:T(8,128)S(1)}, u32[]{:S(2)}, u32[]{:S(2)}) collective-permute-start(f32[1,2,512,1024]{2,3,0,1:T(8,128)} %copy.4), channel_id=1, source_target_pairs={{8,0},{10,2},{12,4},{14,6},{16,8},{18,10},{20,12},{22,14},{24,16},... | collective-permute-start | bytes 12582920 | tf_op jit(solution)/shard_map/ppermute | solution.py:10
  18.4 181.2 %collective-permute-start.1 = (f32[1,2,512,1024]{2,3,0,1:T(8,128)}, f32[1,2,512,1024]{2,3,0,1:T(8,128)S(1)}, u32[]{:S(2)}, u32[]{:S(2)}) collective-permute-start(f32[1,2,512,1024]{2,3,0,1:T(8,128)} %copy.4), channel_id=1, source_target_pairs={{6,0},{8,2},{10,4},{12,6},{14,8},{16,10},{18,12},{20,14},{22,16},{... | collective-permute-start | bytes 12582920 | tf_op jit(solution)/shard_map/ppermute | solution.py:10
  18.4 269.9 %collective-permute-start.2 = (f32[1,2,512,1024]{2,3,0,1:T(8,128)}, f32[1,2,512,1024]{2,3,0,1:T(8,128)S(1)}, u32[]{:S(2)}, u32[]{:S(2)}) collective-permute-start(f32[1,2,512,1024]{2,3,0,1:T(8,128)} %copy.4), channel_id=1, source_target_pairs={{4,0},{6,2},{8,4},{10,6},{12,8},{14,10},{16,12},{18,14},{20,16},{2... | collective-permute-start | bytes 12582920 | tf_op jit(solution)/shard_map/ppermute | solution.py:10
  19.8 313.4 %collective-permute-start.3 = (f32[1,2,512,1024]{2,3,0,1:T(8,128)}, f32[1,2,512,1024]{2,3,0,1:T(8,128)S(1)}, u32[]{:S(2)}, u32[]{:S(2)}) collective-permute-start(f32[1,2,512,1024]{2,3,0,1:T(8,128)} %copy.4), channel_id=1, source_target_pairs={{2,0},{4,2},{6,4},{8,6},{10,8},{12,10},{14,12},{16,14},{18,16},{20... | collective-permute-start | bytes 12582920 | tf_op jit(solution)/shard_map/ppermute | solution.py:10
  335.4 2.0 copy-start
  335.4 3.2 copy-start.2
  343.0 16.9 %copy-start.1 = (f32[1,2,512,1024]{2,3,0,1:T(8,128)S(1)}, f32[1,2,512,1024]{2,3,0,1:T(8,128)}, u32[]{:S(2)}) copy-start(f32[1,2,512,1024]{2,3,0,1:T(8,128)} %copy-done) | copy-start | bytes 12582916
  343.0 16.9 %copy-start.3 = (f32[1,2,512,1024]{2,3,0,1:T(8,128)S(1)}, f32[1,2,512,1024]{2,3,0,1:T(8,128)}, u32[]{:S(2)}) copy-start(f32[1,2,512,1024]{2,3,0,1:T(8,128)} %copy-done.2) | copy-start | bytes 12582916
  343.1 16.9 %copy-start.6 = (f32[1,2,1024,1024]{3,2,1,0:T(8,128)S(1)}, f32[1,2,1024,1024]{3,2,1,0:T(8,128)}, u32[]{:S(2)}) copy-start(f32[1,2,1024,1024]{3,2,1,0:T(8,128)} %all-gather.6.cloned.1.call-done) | copy-start | bytes 25165828
  543.3 17.0 %copy-start.4 = (f32[1,2,512,1024]{3,2,1,0:T(8,128)S(1)}, f32[1,2,512,1024]{3,2,1,0:T(8,128)}, u32[]{:S(2)}) copy-start(f32[1,2,512,1024]{3,2,1,0:T(8,128)} %param.2) | copy-start | bytes 12582916
  543.3 32.9 %copy-start.5 = (f32[2,2,1024,1024]{2,3,0,1:T(8,128)S(1)}, f32[2,2,1024,1024]{2,3,0,1:T(8,128)}, u32[]{:S(2)}) copy-start(f32[2,2,1024,1024]{2,3,0,1:T(8,128)} %all-gather.4.cloned.1.call-done) | copy-start | bytes 50331652
  591.6 15.4 %copy-start.7 = (f32[2,1,512,1024]{2,3,0,1:T(8,128)S(1)}, f32[2,1,512,1024]{2,3,0,1:T(8,128)}, u32[]{:S(2)}) copy-start(f32[2,1,512,1024]{2,3,0,1:T(8,128)} %subtract_bitcast_fusion) | copy-start | bytes 12582916
  591.6 15.4 %copy-start.8 = (f32[2,1,512,1024]{2,3,0,1:T(8,128)S(1)}, f32[2,1,512,1024]{2,3,0,1:T(8,128)}, u32[]{:S(2)}) copy-start(f32[2,1,512,1024]{2,3,0,1:T(8,128)} %add_bitcast_fusion) | copy-start | bytes 12582916
Sparse Core Ops, SparseCore 0:
  9.5 106.6 all-gather.5
  343.1 200.1 all-gather.3
where the time goes:
time: 643 us; the launch traced here: 635 us
  waiting for transfers between devices  445 us (69%)
  matrix products  126 us (20%)
  between operations  19.3 us (3%)
  local copies, waits for them, and re-layouts  17.8 us (3%)
  other arithmetic  13.2 us (2%)
  starting transfers between devices  7.85 us (1%)
    ppermute x4, waiting for transfers between devices, passed_along(): return lax.ppermute(block, axis, route)  307 us
    all_gather x1, waiting for transfers between devices, body(): piece = lax.all_gather(sinks, 'mode', axis=2, tiled=True)  138 us
    unnamed x22, local copies, waits for them, and re-layouts  17.3 us
    dot_general x1, matrix products, body(): jnp.einsum('rc,kcn->krn', left_im, piece[:, 1], precision=hi)  17 us
    dot_general x1, matrix products, body(): jnp.einsum('krc,cn->krn', left_im, piece[1], precision=hi)  16.8 us
    dot_general x1, matrix products, body(): jnp.einsum('rc,kcn->krn', left_im, piece[:, 0], precision=hi)  15.9 us
    dot_general x1, matrix products, body(): jnp.einsum('krc,cn->krn', left_re, piece[1], precision=hi)  15.5 us
    dot_general x1, matrix products, body(): jnp.einsum('rc,kcn->krn', left_re, piece[:, 0], precision=hi)  15.4 us
  transfers between devices with their start and end apart: 6, of which 5 were waited for; matrix products, arithmetic and copies ran while one was open for 12% of the time, Pallas kernels for 0%

commit v1 on v0

v1 whole, which is shorter than its diff:
```python
import functools

import jax
import jax.numpy as jnp
from jax import lax
from jax.experimental import pallas as pl
from jax.experimental.pallas import tpu as pltpu
from jax.sharding import PartitionSpec as P

F32 = jnp.float32
BF16 = jnp.bfloat16
VMEM_LIMIT = 54 * 1024 * 1024
ROUTE_LIMIT = 54 * 1024 * 1024
TILE = 512
SPLIT_TILE = 256
CHUNKS = 4
GATE = pl.CostEstimate(flops=1, bytes_accessed=1, transcendentals=0)
SMALL = pl.CostEstimate(flops=1, bytes_accessed=1, transcendentals=0)
TOKEN = jax.ShapeDtypeStruct((8, 128), F32)
ANY = pl.BlockSpec(memory_space=pl.ANY)
IN_VMEM = pl.BlockSpec(memory_space=pltpu.VMEM)


def held(x):
    return pltpu.with_memory_space_constraint(x, pltpu.VMEM)


def route_kernel(plan, chosen, count, *refs):
    meta = refs[0]
    ins, refs = refs[chosen : chosen + count], refs[chosen + count :]
    outs, (_, sems) = refs[: len(plan)], refs[len(plan) :]
    moves = []
    for out, pieces in zip(outs, plan):
        for dst, rows, selector, options in pieces:
            step = rows // CHUNKS
            for c in range(CHUNKS):
                made = [
                    pltpu.make_async_copy(
                        ins[i].at[:, pl.ds(row + c * step, step), :],
                        out.at[:, pl.ds(dst + c * step, step), :],
                        sems.at[len(moves)],
                    )
                    for i, row in options
                ]
                moves.append((selector, made))
    for selector, made in moves:
        if selector is None:
            made[0].start()
        else:
            for value, copy in enumerate(made):
                pl.when(meta[selector] == value)(copy.start)
    for _, made in moves:
        made[0].wait()


def route(meta, outputs, after, in_vmem):
    arrays, place = [], {}
    plan = []
    for pieces in outputs:
        listed = []
        for dst, rows, selector, options in pieces:
            numbered = []
            for array, row in options:
                if id(array) not in place:
                    place[id(array)] = len(arrays)
                    arrays.append(array)
                numbered.append((place[id(array)], row))
            listed.append((dst, rows, selector, numbered))
        plan.append(listed)
    width = arrays[0].shape[2]
    heights = [sum(piece[1] for piece in pieces) for pieces in plan]
    arrays += after
    shape_of = pltpu.VMEM if in_vmem else jax.ShapeDtypeStruct
    chosen = any(piece[2] is not None for pieces in plan for piece in pieces)
    return pl.pallas_call(
        functools.partial(route_kernel, plan, int(chosen), len(arrays)),
        in_specs=[pl.BlockSpec(memory_space=pltpu.SMEM)] * chosen + [ANY] * len(arrays),
        out_specs=[pl.BlockSpec(memory_space=pltpu.VMEM)] * len(plan) + [ANY],
        out_shape=[shape_of((2, h, width), F32) for h in heights] + [TOKEN],
        scratch_shapes=[pltpu.SemaphoreType.DMA((CHUNKS * sum(len(p) for p in plan),))],
        compiler_params=pltpu.CompilerParams(vmem_limit_bytes=ROUTE_LIMIT),
        cost_estimate=GATE,
    )(*[meta] * chosen, *arrays)


def split(x):
    hi = x.astype(BF16)
    return hi, (x - hi.astype(F32)).astype(BF16)


def parts_of(re, im):
    out = []
    for x in (re, im, re + im):
        out.extend(split(x))
    return out


def split_kernel(x_ref, out, _):
    for index, value in enumerate(parts_of(x_ref[0], x_ref[1])):
        out[index] = value


def split_block(x):
    _, rows, width = x.shape
    return pl.pallas_call(
        split_kernel,
        grid=(width // SPLIT_TILE,),
        in_specs=[pl.BlockSpec((2, rows, SPLIT_TILE), lambda n: (0, 0, n))],
        out_specs=[pl.BlockSpec((6, rows, SPLIT_TILE), lambda n: (0, 0, n)), ANY],
        out_shape=[jax.ShapeDtypeStruct((6, rows, width), BF16), TOKEN],
        compiler_params=pltpu.CompilerParams(vmem_limit_bytes=VMEM_LIMIT),
        cost_estimate=SMALL,
    )(x)


def fetch_start(meta, places, sources, raw, sems, k, t):
    part = raw.shape[2] // len(places[0])
    cols = pl.ds(t * TILE, TILE)
    for c in range(4):

        @pl.when(meta[k] == c)
        def _():
            for p, (index, row) in enumerate(places[c]):
                source = sources[index].at[:, pl.ds(row, part), cols]
                spot = raw.at[k, :, pl.ds(p * part, part), cols]
                pltpu.make_async_copy(source, spot, sems.at[k, p, t]).start()


def fetch_wait(places, raw, sems, k, t, cols):
    part = raw.shape[2] // len(places[0])
    for p in range(len(places[0])):
        spot = raw.at[k, :, pl.ds(p * part, part), cols]
        pltpu.make_async_copy(spot, spot, sems.at[k, p, t]).wait()


def tile_at(t):
    return pl.ds(pl.multiple_of(t * TILE, TILE), TILE)


def own_columns(own6, left6, sem, block, total):
    cols = pl.ds(pl.multiple_of(block * total, total), total)
    return pltpu.make_async_copy(own6.at[:, :, cols], left6, sem.at[0])


def lay_left(left6, left):
    total = left6.shape[2]
    for which in range(3):
        for slot, index in enumerate((2 * which, 2 * which, 2 * which + 1)):
            left[which, :, pl.ds(slot * total, total)] = left6[index]


def lay_right(right, which, high, low):
    total = high.shape[0]
    for slot, value in enumerate((high, low, high)):
        right[which, pl.ds(slot * total, total), :] = value


def products(left, right, sums):
    rows = left.shape[1]
    for which in range(3):
        sums[which, pl.ds(0, rows), :] = jnp.dot(left[which], right[which], preferred_element_type=F32)


def both_kernel(places, count, has_sum, planes, group, groups, meta, own6, *refs):
    sources, refs = refs[:count], refs[count:]
    blocks, refs = (own6, *refs[: planes - 1]), refs[planes - 1 :]
    if has_sum:
        f_in, refs = refs[0], refs[1:]
    f_out, p_out, _, raw, left6, left, *refs = refs
    (rights, sums), (parts, held, f_held, p_held, *sems) = (refs[:2], refs[2:4]), refs[4:]
    raw_sems, left_sem, block_sems, in_sems, out_sems, p_sems = sems
    pairs, _, total, width = raw.shape
    rows = left.shape[1]
    tiles = width // TILE
    plane = meta[pairs]

    def load_sum(t, k):
        spot = (k, slice(None), slice(None), tile_at(t))
        return pltpu.make_async_copy(f_in.at[spot], f_held.at[spot], in_sems.at[t, k])

    def give_sum(t, k):
        spot = (k, slice(None), slice(None), tile_at(t))
        return pltpu.make_async_copy(f_held.at[spot], f_out.at[spot], out_sems.at[t, k])

    def load_block(j, t):
        return pltpu.make_async_copy(blocks[j].at[:, :, tile_at(t)], held.at[j, :, :, tile_at(t)], block_sems.at[j, t])

    def give_partner(t):
        spot = (slice(None), slice(None), slice(None), tile_at(t))
        return pltpu.make_async_copy(p_held.at[spot], p_out.at[spot], p_sems.at[t])

    load_left = own_columns(own6, left6, left_sem, plane * groups + group, total)
    load_left.start()
    for t in range(tiles):
        for k in range(pairs):
            fetch_start(meta, places, sources, raw, raw_sems, k, t)
            if has_sum:
                load_sum(t, k).start()
    for t in range(tiles):
        for j in range(planes):
            load_block(j, t).start()
    load_left.wait()
    lay_left(left6, left)

    def lay(t, k):
        cols, band = tile_at(t), pl.ds(k * total, total)
        fetch_wait(places, raw, raw_sems, k, t, cols)
        re, im = raw[k, 0, :, cols], raw[k, 1, :, cols]
        for which, value in enumerate((re, im, re + im)):
            high, low = split(value)
            lay_right(rights[k % 2], which, high, low)
            parts[2 * which, band, cols] = high
            parts[2 * which + 1, band, cols] = low

    def finish(t, k):
        cols = tile_at(t)
        t0, t1, t2 = (sums[k % 2][which, pl.ds(0, rows), :] for which in range(3))
        fr, fi = t0 - t1, t2 - t0 - t1
        if has_sum:
            fr, fi = fr + f_held[k, 0, :, cols], fi + f_held[k, 1, :, cols]
        f_held[k, 0, :, cols] = fr
        f_held[k, 1, :, cols] = fi

    def forward(t, carry):
        if has_sum:
            for k in range(pairs):
                load_sum(t, k).wait()
        lay(t, 0)
        for k in range(pairs):
            if k + 1 < pairs:
                lay(t, k + 1)
            products(left, rights[k % 2], sums[k % 2])
            if k > 0:
                finish(t, k - 1)
        finish(t, pairs - 1)
        for k in range(pairs):
            give_sum(t, k).start()
        return carry

    lax.fori_loop(0, tiles, forward, 0)

    def partner(t, carry):
        cols = tile_at(t)
        for j in range(planes):
            load_block(j, t).wait()

        for i in range(3):
            term = None
            for j in range(planes):
                at = pl.multiple_of(lax.rem(plane + j, planes) * rows, rows)
                ah, al = parts[2 * i, :, pl.ds(at, rows)], parts[2 * i + 1, :, pl.ds(at, rows)]
                bh, bl = held[j, 2 * i, :, cols], held[j, 2 * i + 1, :, cols]
                for a, b in ((ah, bh), (ah, bl), (al, bh)):
                    more = jnp.dot(a, b, preferred_element_type=F32)
                    term = more if term is None else term + more
            sums[0][i, pl.ds(0, pairs * total), :] = term
        for k in range(pairs):
            t0, t1, t2 = (sums[0][i, pl.ds(k * total, total), :] for i in range(3))
            p_held[k, 0, :, cols] = t0 - t1
            p_held[k, 1, :, cols] = t2 - t0 - t1
        give_partner(t).start()
        return carry

    lax.fori_loop(0, tiles, partner, 0)
    for t in range(tiles):
        for k in range(pairs):
            give_sum(t, k).wait()
        give_partner(t).wait()


def more_kernel(places, count, partners, planes, shift, group, groups, meta, own6, *refs):
    sources, refs = refs[:count], refs[count:]
    f_in, refs = refs[0], refs[1:]
    p_refs, refs = refs[:partners], refs[partners:]
    f_out, refs = refs[0], refs[1:]
    if partners:
        tr_out, refs = refs[0], refs[1:]
    raw, left6, left, *refs = refs
    (rights, sums), (f_held, raw_sems, left_sem, sems, *p_held) = (refs[:2], refs[2:4]), refs[4:]
    pairs, _, total, width = raw.shape
    rows = left.shape[1]
    tiles = width // TILE

    def load_sum(t, k):
        spot = (k, slice(None), slice(None), tile_at(t))
        return pltpu.make_async_copy(f_in.at[spot], f_held.at[spot], sems.at[0, t, k])

    def give_sum(t, k):
        spot = (k, slice(None), slice(None), tile_at(t))
        return pltpu.make_async_copy(f_held.at[spot], f_out.at[spot], sems.at[1, t, k])

    def load_partners(t, k):
        copies, row = [], 0
        for index, p_ref in enumerate(p_refs):
            high = p_ref.shape[2]
            there = p_held[0].at[k, :, pl.ds(row, high), tile_at(t)]
            copies.append(pltpu.make_async_copy(p_ref.at[k, :, :, tile_at(t)], there, sems.at[2 + index, t, k]))
            row += high
        return copies

    load_left = own_columns(own6, left6, left_sem, lax.rem(meta[pairs] + shift, planes) * groups + group, total)
    load_left.start()
    for t in range(tiles):
        for k in range(pairs):
            fetch_start(meta, places, sources, raw, raw_sems, k, t)
            load_sum(t, k).start()
            for copy in load_partners(t, k):
                copy.start()
    if partners:
        tr_out[...] = jnp.zeros_like(tr_out)
    load_left.wait()
    lay_left(left6, left)

    def lay(t, k):
        cols = tile_at(t)
        fetch_wait(places, raw, raw_sems, k, t, cols)
        re, im = raw[k, 0, :, cols], raw[k, 1, :, cols]
        for which, value in enumerate((re, im, re + im)):
            lay_right(rights[k % 2], which, *split(value))

    def finish(t, k):
        cols = tile_at(t)
        t0, t1, t2 = (sums[k % 2][which, pl.ds(0, rows), :] for which in range(3))
        fr, fi = t0 - t1 + f_held[k, 0, :, cols], t2 - t0 - t1 + f_held[k, 1, :, cols]
        f_held[k, 0, :, cols] = fr
        f_held[k, 1, :, cols] = fi
        if partners:
            term = fr * p_held[0][k, 0, :, cols] + fi * p_held[0][k, 1, :, cols]
            term = jnp.sum(term.reshape(rows // 8, 8, TILE), axis=0)
            tr_out[k] += sum(term[:, c * 128 : (c + 1) * 128] for c in range(TILE // 128))

    def forward(t, carry):
        lay(t, 0)
        for k in range(pairs):
            load_sum(t, k).wait()
            for copy in load_partners(t, k):
                copy.wait()
            if k + 1 < pairs:
                lay(t, k + 1)
            products(left, rights[k % 2], sums[k % 2])
            if k > 0:
                finish(t, k - 1)
        finish(t, pairs - 1)
        for k in range(pairs):
            give_sum(t, k).start()
        return carry

    lax.fori_loop(0, tiles, forward, 0)
    for t in range(tiles):
        for k in range(pairs):
            give_sum(t, k).wait()


def placed(groups_of_cands):
    sources, places = [], []
    for cands in groups_of_cands:
        listed = []
        for pieces in cands:
            entry = []
            for array, row in pieces:
                known = [i for i, s in enumerate(sources) if s is array]
                if not known:
                    sources.append(array)
                entry.append((known[0] if known else len(sources) - 1, row))
            listed.append(entry)
        places.append(listed)
    return sources, places


def fetch_scratch(pairs, total, width, pieces):
    return pltpu.VMEM((pairs, 2, total, width), F32), pltpu.SemaphoreType.DMA((pairs, pieces, width // TILE))


def operand_scratch(rows, total, high):
    return [
        pltpu.VMEM((6, rows, total), BF16),
        pltpu.VMEM((3, rows, 3 * total), BF16),
        *[pltpu.VMEM((3, 3 * total, TILE), BF16)] * 2,
        *[pltpu.VMEM((3, high, TILE), F32)] * 2,
    ]


def both_call(meta, own6, others6, cands, f, group, groups):
    pairs = f_pairs(meta)
    planes = 1 + len(others6)
    _, rows, width = own6.shape
    total = rows // groups
    tiles = width // TILE
    sources, (places,) = placed([cands])
    raw, raw_sems = fetch_scratch(pairs, total, width, len(places[0]))
    args = [meta, own6, *sources, *others6]
    aliases = {}
    if f is not None:
        aliases = {len(args): 0}
        args.append(f)
    return pl.pallas_call(
        functools.partial(both_kernel, places, len(sources), f is not None, planes, group, groups),
        in_specs=[pl.BlockSpec(memory_space=pltpu.SMEM)] + [ANY] * (len(args) - 1),
        out_specs=[ANY] * 3,
        out_shape=[
            jax.ShapeDtypeStruct((pairs, 2, rows, width), F32),
            jax.ShapeDtypeStruct((pairs, 2, total, width), F32),
            TOKEN,
        ],
        scratch_shapes=[
            raw,
            *operand_scratch(rows, total, max(rows, pairs * total)),
            pltpu.VMEM((6, pairs * total, width), BF16),
            pltpu.VMEM((planes, 6, rows, width), BF16),
            pltpu.VMEM((pairs, 2, rows, width), F32),
            pltpu.VMEM((pairs, 2, total, width), F32),
            raw_sems,
            pltpu.SemaphoreType.DMA((1,)),
            pltpu.SemaphoreType.DMA((planes, tiles)),
            pltpu.SemaphoreType.DMA((tiles, pairs)),
            pltpu.SemaphoreType.DMA((tiles, pairs)),
            pltpu.SemaphoreType.DMA((tiles,)),
        ],
        input_output_aliases=aliases,
        compiler_params=pltpu.CompilerParams(vmem_limit_bytes=VMEM_LIMIT),
        cost_estimate=SMALL,
    )(*args)


def more_call(meta, own6, cands, f, partners, shift, group, groups):
    pairs = f_pairs(meta)
    _, rows, width = own6.shape
    planes = width // rows
    total = rows // groups
    tiles = width // TILE
    sources, (places,) = placed([cands])
    raw, raw_sems = fetch_scratch(pairs, total, width, len(places[0]))
    out_specs = [ANY]
    out_shape = [jax.ShapeDtypeStruct((pairs, 2, rows, width), F32)]
    scratch = [raw, *operand_scratch(rows, total, rows), pltpu.VMEM((pairs, 2, rows, width), F32), raw_sems]
    scratch += [pltpu.SemaphoreType.DMA((1,)), pltpu.SemaphoreType.DMA((2 + len(partners), tiles, pairs))]
    if partners:
        out_specs.append(IN_VMEM)
        out_shape.append(jax.ShapeDtypeStruct((pairs, 8, 128), F32))
        scratch.append(pltpu.VMEM((pairs, 2, rows, width), F32))
    args = [meta, own6, *sources, f, *partners]
    return pl.pallas_call(
        functools.partial(more_kernel, places, len(sources), len(partners), planes, shift, group, groups),
        in_specs=[pl.BlockSpec(memory_space=pltpu.SMEM)] + [ANY] * (len(args) - 1),
        out_specs=out_specs,
        out_shape=out_shape,
        scratch_shapes=scratch,
        input_output_aliases={2 + len(sources): 0},
        compiler_params=pltpu.CompilerParams(vmem_limit_bytes=VMEM_LIMIT),
        cost_estimate=SMALL,
    )(*args)


def f_pairs(meta):
    return meta.shape[0] - 3


STEPS = {
    2: (
        ([("z", 0, 0)], [], []),
        ([("z", 0, 1)], [], []),
        ([("x", 0, 0), ("z", 0, 2)], [("own", 0)], []),
        ([("x", 0, 1), ("z", 0, 3)], [], []),
        ([("x", 0, 2)], [], []),
        ([("x", 0, 3), ("z", 1, 0), ("z", 1, 2), ("zy", 1, 1), ("c", 0, 0)], [("other", 0)], [("x", 0, 2)]),
        ([("x", 1, 0), ("z", 1, 3), ("xy", 1, 1), ("c", 0, 1)], [], [("z", 1, 1)]),
        ([("x", 1, 2), ("xy", 1, 3), ("c", 1, 0)], [("both", 0)], []),
        ([("c", 1, 1)], [("both", 1)], []),
    ),
    1: (
        ([("z", 0, 0)], [], []),
        ([("z", 0, 1)], [], []),
        ([("x", 0, 0)], [("own", 0)], []),
        ([("x", 0, 1), ("z", 1, 0), ("zy", 1, 1)], [], []),
        ([("x", 1, 0), ("c", 0, 0), ("xy", 1, 1)], [("other", 0)], []),
        ([("c", 1, 0)], [("both", 0)], []),
    ),
}


def body(fields, offsets):
    own = fields[0]
    pairs = offsets.shape[1]
    _, rows, width = own.shape
    steps = lax.axis_size("tm")
    planes = lax.axis_size("mode")
    me = lax.axis_index("tm")
    lane = lax.rem(me, 2)
    odd_chip = lax.rem(lax.div(me, 2), 2)
    groups = 2 if rows >= 512 else 1
    part = rows // groups // 2

    distance = offsets[0]
    place = jnp.where((lane == 1) & (distance % 2 == 1), 3 - distance, distance - 1)
    meta = jnp.concatenate([place, jnp.stack([lax.axis_index("mode"), odd_chip, lane])]).astype(jnp.int32)
    odd_at, lane_at = pairs + 1, pairs + 2

    def from_later(x):
        return lax.ppermute(x, "tm", [((i + 4) % steps, i) for i in range(steps)])

    def from_plane(x, shift):
        return lax.ppermute(x, "mode", [((i + shift) % planes, i) for i in range(planes)])

    def across_chips(x):
        return lax.ppermute(x, "tm", [(i ^ 2, i) for i in range(steps)])

    def across_cores(x):
        return lax.ppermute(x, "tm", [(i ^ 1, i) for i in range(steps)])

    got = {}

    def here(j, q):
        if j == 0:
            return own, q * part
        return got["y", j], q * part

    def operand(kind, j, q):
        if kind == "z":
            return [(0, part, None, [here(j, q)])]
        if kind in ("zy", "xy"):
            return [(0, part, None, [(got[kind[0], 0, q], 0)])]
        if kind == "x":
            arrived = held(got["z", j, q]) if planes == 2 else got["z", j, q]
            return [(0, part, odd_at, [(arrived, 0), here(j, q)])]
        pieces = (2 * q, 2 * q + 1)
        out = [(i * part, part, None, [(got["x", j, p], 0)]) for i, p in enumerate(pieces)]
        return out + [
            ((i + 2) * part, part, lane_at, [(got["z", j, p], 0), here(j, p)]) for i, p in enumerate(pieces)
        ]

    def send(kind, j, q, x):
        if kind in ("zy", "xy"):
            return from_plane(x, j)
        if kind == "z":
            return from_later(x)
        if kind == "x":
            return across_chips(x)
        return across_cores(x)

    def candidates(j, group, near=False):
        picks = (2 * group, 2 * group + 1)
        swapped = held(got["c", j, group]) if near else got["c", j, group]
        cross4 = [(swapped, 2 * part), (swapped, 3 * part)]
        cross2 = [(swapped, 0), (swapped, part)]
        return [
            cross4,
            [(got["x", j, q], 0) for q in picks],
            cross2,
            [(got["z", j, q], 0) for q in picks],
        ]

    f, own6, others6, partners = None, None, [], []

    for j in range(1, planes):
        got["y", j] = from_plane(own, j)
    written = []
    for step, work, there in STEPS[groups]:
        tasks, after = [], list(written[-1:])
        for kind, other, q in step:
            tasks += [(kind, j, q) for j in (range(1, planes) if other else [0])]
        after += [got[kind, j, q] for kind, other, q in there for j in (range(1, planes) if other else [0])]
        for kind, g in work:
            if kind == "own":
                own6, done = split_block(own)
                after.append(done)
            elif kind == "other":
                for j in range(1, planes):
                    block6, done = split_block(got["y", j])
                    others6.append(block6)
                    after.append(done)
            else:
                f, partner, done = both_call(meta, own6, others6, candidates(0, g), f, g, groups)
                partners.append(partner)
                after.append(done)
        written = route(meta, [operand(*task) for task in tasks], after, planes == 2)
        for (kind, j, q), x in zip(tasks, written[:-1]):
            got[kind[0], j, q] = send(kind, j, q, x)

    for g in range(groups):
        for j in range(1, planes):
            last = g == groups - 1 and j == planes - 1
            out = more_call(meta, own6, candidates(j, g, last and planes == 2), f, partners if last else [], j, g, groups)
            f = out[0]
    partial_trace = jnp.sum(out[1], axis=(1, 2)) / F32(width)
    if planes == 2:
        traces = partial_trace + from_plane(partial_trace, 1)
    else:
        traces = lax.psum(partial_trace, "mode")
    return (f[None], traces[None])


def solution(mesh):
    in_specs = (P("tm", None, "mode", None), P("tm", None))
    out_specs = (P("tm", None, None, "mode", None), P("tm", None))
    return jax.shard_map(body, mesh=mesh, in_specs=in_specs, out_specs=out_specs, check_vma=False)
```

time: 643 us -> 248 us (0.39); the launches traced: 635 us -> 247 us
  waiting for transfers between devices: 445 us -> 94.6 us
  matrix products: 126 us -> 0 us
  Pallas kernels: 0 us -> 112 us
  starting transfers between devices: 7.85 us -> 32 us
  between operations: 19.3 us -> 0.92 us
  local copies, waits for them, and re-layouts: 17.8 us -> 5.81 us
  other arithmetic: 13.2 us -> 1.98 us
    ppermute x4 -> x22, waiting for transfers between devices: 307 us -> 94.6 us  [the longest x7 48.8 us: from_later(): return lax.ppermute(x, 'tm', [((i + 4) % steps, i) for i in range(steps)])]
    all_gather x2 -> x0, waiting for transfers between devices: 138 us -> none  [the longest x1 138 us: body(): piece = lax.all_gather(sinks, 'mode', axis=2, tiled=True)]
    dot_general x8 -> x0, matrix products: 126 us -> none  [the longest x1 17 us: body(): jnp.einsum('rc,kcn->krn', left_im, piece[:, 1], precision=hi)]
    pallas_call x0 -> x15, Pallas kernels: none -> 112 us  [the longest x2 44.2 us: both_call(): pl.pallas_call(functools.partial(both_kernel, places, len(sources), f is...]
    ppermute x4 -> x22, starting transfers between devices: 7.78 us -> 32 us  [the longest x7 15.2 us: from_later(): return lax.ppermute(x, 'tm', [((i + 4) % steps, i) for i in range(steps)])]
    unnamed x22 -> x36, local copies, waits for them, and re-layouts: 17.3 us -> 5.81 us
  transfers between devices with their start and end apart: 6 -> 22, of which waited for: 5 -> 12; matrix products, arithmetic and copies ran while one was open for 12% -> 0% of each run, Pallas kernels for 0% -> 37%
where the time goes in v1:
time: 248 us; the launch traced here: 247 us
  Pallas kernels  112 us (45%)
  waiting for transfers between devices  94.6 us (38%)
  starting transfers between devices  32 us (13%)
  local copies, waits for them, and re-layouts  5.81 us (2%)
    ppermute x7, waiting for transfers between devices, from_later(): return lax.ppermute(x, 'tm', [((i + 4) % steps, i) for i in range(steps)])  48.8 us
    pallas_call x2, Pallas kernels, both_call(): pl.pallas_call(functools.partial(both_kernel, places, len(sources), f is...  44.2 us
    ppermute x6, waiting for transfers between devices, across_chips(): return lax.ppermute(x, 'tm', [(i ^ 2, i) for i in range(steps)])  30.5 us
    pallas_call x9, Pallas kernels, route(): pl.pallas_call(functools.partial(route_kernel, plan, int(chosen), len(arr...  28.9 us
    pallas_call x2, Pallas kernels, more_call(): pl.pallas_call(functools.partial(more_kernel, places, len(sources), len(p...  27 us
    ppermute x7, starting transfers between devices, from_later(): return lax.ppermute(x, 'tm', [((i + 4) % steps, i) for i in range(steps)])  15.2 us
    ppermute x5, waiting for transfers between devices, from_plane(): lax.ppermute(x, 'mode', [((i + shift) % planes, i) for i in range(planes)])  15.2 us
    pallas_call x2, Pallas kernels, split_block(): pl.pallas_call(split_kernel, grid=(width // SPLIT_TILE,), in_specs=[pl.Bl...  11.5 us
  transfers between devices with their start and end apart: 22, of which 12 were waited for; matrix products, arithmetic and copies ran while one was open for 0% of the time, Pallas kernels for 37%

profile of v1, /device:TPU:0, one launch (start us, length us, event | category | flops | bytes accessed | tf_op | source)
XLA Modules:
  0.0 246.9 jit_solution(523376359047701964)
XLA Ops:
  0.6 3.0 %collective-permute-start.3 = (f32[2,512,1024]{2,1,0:T(8,128)}, f32[2,512,1024]{2,1,0:T(8,128)}, u32[]{:S(2)}, u32[]{:S(2)}) collective-permute-start(f32[2,512,1024]{2,1,0:T(8,128)} %bitcast.15), channel_id=1, source_target_pairs={{1,0},{0,1},{3,2},{2,3},{5,4},{4,5},{7,6},{6,7},{9,8},{8,9},{11,10... | collective-permute-start | bytes 12582920 | tf_op jit(solution)/shard_map/ppermute | solution.py:502
  3.7 2.2 shard_map.42
  5.9 3.7 %collective-permute-start.1 = (f32[2,128,1024]{2,1,0:T(8,128)}, f32[2,128,1024]{2,1,0:T(8,128)S(1)}, u32[]{:S(2)}, u32[]{:S(2)}) collective-permute-start(f32[2,128,1024]{2,1,0:T(8,128)} %get-tuple-element.45), channel_id=1, source_target_pairs={{8,0},{10,2},{12,4},{14,6},{16,8},{18,10},{20,12},{22,14},{24,16},... | collective-permute-start | bytes 3145736 | tf_op jit(solution)/shard_map/ppermute | solution.py:499
  9.5 1.2 shard_map.43
  11.3 0.7 pad_add_fusion.refs_0_.meta
  11.9 5.7 %shard_map.41 = (bf16[6,512,1024]{2,1,0:T(8,128)(2,1)}, f32[8,128]{1,0:T(8,128)}) custom-call(f32[2,512,1024]{2,1,0:T(8,128)} %bitcast.18), custom_call_target="tpu_custom_call" | custom-call | flops 1 | bytes 1 | tf_op jit(solution)/shard_map/pallas_call | solution.py:105
  17.7 15.8 %collective-permute-done.1.refs_1_.refs_7_.refs_3_ = f32[2,128,1024]{2,1,0:T(8,128)S(1)} collective-permute-done((f32[2,128,1024]{2,1,0:T(8,128)}, f32[2,128,1024]{2,1,0:T(8,128)S(1)}, u32[]{:S(2)}, u32[]{:S(2)}) %collective-permute-start.1) | collective-permute-done | bytes 1048608 | tf_op jit(solution)/shard_map/ppermute | solution.py:499
  33.4 2.0 shard_map.44
  35.5 4.2 %collective-permute-start.6 = (f32[2,128,1024]{2,1,0:T(8,128)S(1)}, f32[2,128,1024]{2,1,0:T(8,128)S(1)}, u32[]{:S(2)}, u32[]{:S(2)}) collective-permute-start(f32[2,128,1024]{2,1,0:T(8,128)S(1)} %get-tuple-element.52), channel_id=1, source_target_pairs={{8,0},{10,2},{12,4},{14,6},{16,8},{18,10},{20,12},{22,14},{24,16},... | collective-permute-start | bytes 3145736 | tf_op jit(solution)/shard_map/ppermute | solution.py:499
  39.7 1.7 collective-permute-start.4
  41.4 14.4 %collective-permute-done.refs_1_.refs_4_ = f32[2,128,1024]{2,1,0:T(8,128)S(1)} collective-permute-done((f32[2,128,1024]{2,1,0:T(8,128)S(1)}, f32[2,128,1024]{2,1,0:T(8,128)S(1)}, u32[]{:S(2)}, u32[]{:S(2)}) %collective-permute-start) | collective-permute-done | bytes 1048608 | tf_op jit(solution)/shard_map/ppermute | solution.py:499
  55.8 2.0 shard_map.45
  57.8 4.3 %collective-permute-start.2 = (f32[2,128,1024]{2,1,0:T(8,128)S(1)}, f32[2,128,1024]{2,1,0:T(8,128)S(1)}, u32[]{:S(2)}, u32[]{:S(2)}) collective-permute-start(f32[2,128,1024]{2,1,0:T(8,128)S(1)} %get-tuple-element.49), channel_id=1, source_target_pairs={{8,0},{10,2},{12,4},{14,6},{16,8},{18,10},{20,12},{22,14},{24,16},... | collective-permute-start | bytes 3145736 | tf_op jit(solution)/shard_map/ppermute | solution.py:499
  62.2 1.7 collective-permute-start.5
  63.9 14.4 %collective-permute-done.6.refs_1_.refs_6_.refs_3_ = f32[2,128,1024]{2,1,0:T(8,128)S(1)} collective-permute-done((f32[2,128,1024]{2,1,0:T(8,128)S(1)}, f32[2,128,1024]{2,1,0:T(8,128)S(1)}, u32[]{:S(2)}, u32[]{:S(2)}) %collective-permute-start.6) | collective-permute-done | bytes 1048608 | tf_op jit(solution)/shard_map/ppermute | solution.py:499
  78.3 0.8 shard_map.46
  79.1 2.6 %collective-permute-start.7 = (f32[2,128,1024]{2,1,0:T(8,128)S(1)}, f32[2,128,1024]{2,1,0:T(8,128)S(1)}, u32[]{:S(2)}, u32[]{:S(2)}) collective-permute-start(f32[2,128,1024]{2,1,0:T(8,128)S(1)} %get-tuple-element.55), channel_id=1, source_target_pairs={{4,0},{6,2},{0,4},{2,6},{12,8},{14,10},{8,12},{10,14},{20,16},{22,... | collective-permute-start | bytes 3145736 | tf_op jit(solution)/shard_map/ppermute | solution.py:505
  81.8 12.8 %collective-permute-done.3.x_ref.refs_3_.refs_2_.refs_4_ = f32[2,512,1024]{2,1,0:T(8,128)} collective-permute-done((f32[2,512,1024]{2,1,0:T(8,128)}, f32[2,512,1024]{2,1,0:T(8,128)}, u32[]{:S(2)}, u32[]{:S(2)}) %collective-permute-start.3) | collective-permute-done | bytes 4194336 | tf_op jit(solution)/shard_map/ppermute | solution.py:502
  94.6 5.8 %shard_map.47 = (bf16[6,512,1024]{2,1,0:T(8,128)(2,1)}, f32[8,128]{1,0:T(8,128)}) custom-call(f32[2,512,1024]{2,1,0:T(8,128)} %collective-permute-done.3.x_ref.refs_3_.refs_2_.refs_4_), custom_call_target="tpu_custom_call" | custom-call | flops 1 | bytes 1 | tf_op jit(solution)/shard_map/pallas_call | solution.py:105
  100.4 6.2 %collective-permute-done.7.refs_9_.refs_4_.refs_1_ = f32[2,128,1024]{2,1,0:T(8,128)S(1)} collective-permute-done((f32[2,128,1024]{2,1,0:T(8,128)S(1)}, f32[2,128,1024]{2,1,0:T(8,128)S(1)}, u32[]{:S(2)}, u32[]{:S(2)}) %collective-permute-start.7) | collective-permute-done | bytes 1048608 | tf_op jit(solution)/shard_map/ppermute | solution.py:505
  106.6 1.0 copy-done.10
  107.6 6.1 %shard_map.48 = (f32[2,128,1024]{2,1,0:T(8,128)S(1)}, f32[2,128,1024]{2,1,0:T(8,128)S(1)}, f32[2,128,1024]{2,1,0:T(8,128)S(1)}, f32[2,128,1024]{2,1,0:T(8,128)S(...) custom-call(s32[5]{0:T(128)} %pad_add_fusion.refs_0_.meta, ...), custom_call_target="tpu_custom_call" | custom-call | flops 1 | bytes 1 | tf_op jit(solution)/shard_map/pallas_call | solution.py:75
  113.8 1.0 copy-done.6
  114.7 1.9 collective-permute-start.9
  117.0 0.5 collective-permute-start.11
  117.5 23.0 %collective-permute-done.9.refs_5_.refs_3_.refs_2_ = f32[2,128,1024]{2,1,0:T(8,128)S(1)} collective-permute-done((f32[2,128,1024]{2,1,0:T(8,128)S(1)}, f32[2,128,1024]{2,1,0:T(8,128)S(1)}, u32[]{:S(2)}, u32[]{:S(2)}) %collective-permute-start.9) | collective-permute-done | bytes 1048608 | tf_op jit(solution)/shard_map/ppermute | solution.py:505
  140.5 1.5 collective-permute-done.10.refs_1_.refs_6_.refs_3_
  142.0 1.1 copy-done.8
  143.1 5.9 %shard_map.49 = (f32[2,128,1024]{2,1,0:T(8,128)S(1)}, f32[2,128,1024]{2,1,0:T(8,128)S(1)}, f32[2,128,1024]{2,1,0:T(8,128)S(1)}, f32[2,512,1024]{2,1,0:T(8,128)}, f32[8,128]{1,0:T(8,128)}) custom-call(s32[5]{0:T(128)} %pad_add_fusion.refs_0_.meta, f32[2,128,1024]{2,1,0:T(8,128)S(1)} %collective-permute-done.10.refs_1_.refs_6_.refs_3_, ...), custom_call_target="tpu_custom_call" | custom-call | flops 1 | bytes 1 | tf_op jit(solution)/shard_map/pallas_call | solution.py:75
  149.1 2.1 collective-permute-start.8
  151.2 0.5 collective-permute-start.12
  151.7 0.5 collective-permute-start.13
  152.3 20.0 %shard_map.50 = (f32[2,2,512,1024]{3,2,1,0:T(8,128)}, f32[2,2,256,1024]{3,2,1,0:T(8,128)}, f32[8,128]{1,0:T(8,128)}) custom-call(s32[5]{0:T(128)} %pad_add_fusion.refs_0_.meta, bf16[6,512,1024]{2,1,0:T(8,128)(2,1)} %get-tuple-element.42.own6, f32[2,512,1024]{2,1,0:T(8,128)} %collective-permute-done.14.refs_0_, ...), custom_call_target="tpu_custom_call" | custom-call | flops 1 | bytes 1 | tf_op jit(solution)/shard_map/pallas_call | solution.py:396
  172.3 2.8 %collective-permute-done.8.refs_1_.refs_3_ = f32[2,128,1024]{2,1,0:T(8,128)S(1)} collective-permute-done((f32[2,128,1024]{2,1,0:T(8,128)S(1)}, f32[2,128,1024]{2,1,0:T(8,128)S(1)}, u32[]{:S(2)}, u32[]{:S(2)}) %collective-permute-start.8) | collective-permute-done | bytes 1048608 | tf_op jit(solution)/shard_map/ppermute | solution.py:499
  175.1 1.3 collective-permute-done.12.refs_4_.refs_1_
  176.7 0.8 copy-done.13
  177.8 5.7 %shard_map.51 = (f32[2,128,1024]{2,1,0:T(8,128)S(1)}, f32[2,128,1024]{2,1,0:T(8,128)S(1)}, f32[2,512,1024]{2,1,0:T(8,128)}, f32[8,128]{1,0:T(8,128)}) custom-call(s32[5]{0:T(128)} %pad_add_fusion.refs_0_.meta, f32[2,128,1024]{2,1,0:T(8,128)S(1)} %collective-permute-done.8.refs_1_.refs_3_, ...), custom_call_target="tpu_custom_call" | custom-call | flops 1 | bytes 1 | tf_op jit(solution)/shard_map/pallas_call | solution.py:75
  183.5 1.5 collective-permute-start.15
  185.5 24.2 %shard_map.52 = (f32[2,2,512,1024]{3,2,1,0:T(8,128)}, f32[2,2,256,1024]{3,2,1,0:T(8,128)}, f32[8,128]{1,0:T(8,128)}) custom-call(s32[5]{0:T(128)} %pad_add_fusion.refs_0_.meta, bf16[6,512,1024]{2,1,0:T(8,128)(2,1)} %get-tuple-element.42.own6, f32[2,512,1024]{2,1,0:T(8,128)} %collective-permute-done.18.refs_0_, ...), custom_call_target="tpu_custom_call", output_to_operand_aliasing={{0}: (8, {})} | custom-call | flops 1 | bytes 1 | tf_op jit(solution)/shard_map/pallas_call | solution.py:396
  209.9 0.9 copy-done.12
  211.5 2.9 %shard_map.53 = (f32[2,512,1024]{2,1,0:T(8,128)S(1)}, f32[8,128]{1,0:T(8,128)}) custom-call(s32[5]{0:T(128)} %pad_add_fusion.refs_0_.meta, f32[2,128,1024]{2,1,0:T(8,128)} %copy-done.15, f32[2,128,1024]{2,1,0:T(8,128)} %copy-done.16, f32[2,128,1024]{2,1,0:T(8,128)} %copy-done, f32[2,512,1024]{2,1,0:T(8,128)} %collective-permute-done.3.x_ref.refs_3_.refs_2_.refs_4_, ...), custom_call_target="tpu_custom_call" | custom-call | flops 1 | bytes 1 | tf_op jit(solution)/shard_map/pallas_call | solution.py:75
  214.4 0.6 collective-permute-start.19
  215.0 12.6 %shard_map.54.refs_5_ = f32[2,2,512,1024]{3,2,1,0:T(8,128)} custom-call(s32[5]{0:T(128)} %pad_add_fusion.refs_0_.meta, bf16[6,512,1024]{2,1,0:T(8,128)(2,1)} %get-tuple-element.42.own6, f32[2,512,1024]{2,1,0:T(8,128)} %collective-permute-done.20.refs_0_, f32[2,128,1024]{2,1,0:T(8,128)} %copy-done.13, ...), custom_call_target="tpu_custom_call", output_to_operand_aliasing={{}: (7, {})} | custom-call | flops 1 | bytes 1 | tf_op jit(solution)/shard_map/pallas_call | solution.py:442
  227.6 14.4 %shard_map.55 = (f32[2,2,512,1024]{3,2,1,0:T(8,128)}, f32[2,8,128]{2,1,0:T(8,128)}) custom-call(s32[5]{0:T(128)} %pad_add_fusion.refs_0_.meta, bf16[6,512,1024]{2,1,0:T(8,128)(2,1)} %get-tuple-element.42.own6, f32[2,512,1024]{2,1,0:T(8,128)S(1)} %collective-permute-done.19.refs_0_, f32[2,128,1024]{2,1,0:T(8,128)} %copy-done.15, ...), custom_call_target="tpu_custom_call", output_to_operand_aliasing={{0}: (7, {})} | custom-call | flops 1 | bytes 1 | tf_op jit(solution)/shard_map/pallas_call | solution.py:442
  242.0 0.8 reduce_sum.9
  242.8 1.4 collective-permute-start.21
  244.2 2.1 collective-permute-done.21
  246.4 0.5 add_bitcast_fusion
  (52 shorter events, 3.0 us)
Async XLA Ops:
  0.6 10.6 %copy-start.17 = (s32[1,2]{1,0:T(1,128)S(1)}, s32[1,2]{1,0:T(1,128)}, u32[]{:S(2)}) copy-start(s32[1,2]{1,0:T(1,128)} %param.3) | copy-start | bytes 28
  0.6 93.9 %collective-permute-start.3 = (f32[2,512,1024]{2,1,0:T(8,128)}, f32[2,512,1024]{2,1,0:T(8,128)}, u32[]{:S(2)}, u32[]{:S(2)}) collective-permute-start(f32[2,512,1024]{2,1,0:T(8,128)} %bitcast.15), channel_id=1, source_target_pairs={{1,0},{0,1},{3,2},{2,3},{5,4},{4,5},{7,6},{6,7},{9,8},{8,9},{11,10... | collective-permute-start | bytes 12582920 | tf_op jit(solution)/shard_map/ppermute | solution.py:502
  5.9 27.6 %collective-permute-start.1 = (f32[2,128,1024]{2,1,0:T(8,128)}, f32[2,128,1024]{2,1,0:T(8,128)S(1)}, u32[]{:S(2)}, u32[]{:S(2)}) collective-permute-start(f32[2,128,1024]{2,1,0:T(8,128)} %get-tuple-element.45), channel_id=1, source_target_pairs={{8,0},{10,2},{12,4},{14,6},{16,8},{18,10},{20,12},{22,14},{24,16},... | collective-permute-start | bytes 3145736 | tf_op jit(solution)/shard_map/ppermute | solution.py:499
  10.8 45.1 %collective-permute-start = (f32[2,128,1024]{2,1,0:T(8,128)S(1)}, f32[2,128,1024]{2,1,0:T(8,128)S(1)}, u32[]{:S(2)}, u32[]{:S(2)}) collective-permute-start(f32[2,128,1024]{2,1,0:T(8,128)S(1)} %get-tuple-element.44), channel_id=1, source_target_pairs={{8,0},{10,2},{12,4},{14,6},{16,8},{18,10},{20,12},{22,14},{24,16},... | collective-permute-start | bytes 3145736 | tf_op jit(solution)/shard_map/ppermute | solution.py:499
  33.4 24.4 %copy-start.1 = (f32[2,128,1024]{2,1,0:T(8,128)}, f32[2,128,1024]{2,1,0:T(8,128)S(1)}, u32[]{:S(2)}) copy-start(f32[2,128,1024]{2,1,0:T(8,128)S(1)} %collective-permute-done.1.refs_1_.refs_7_.refs_3_) | copy-start | bytes 3145732
  35.5 42.8 %collective-permute-start.6 = (f32[2,128,1024]{2,1,0:T(8,128)S(1)}, f32[2,128,1024]{2,1,0:T(8,128)S(1)}, u32[]{:S(2)}, u32[]{:S(2)}) collective-permute-start(f32[2,128,1024]{2,1,0:T(8,128)S(1)} %get-tuple-element.52), channel_id=1, source_target_pairs={{8,0},{10,2},{12,4},{14,6},{16,8},{18,10},{20,12},{22,14},{24,16},... | collective-permute-start | bytes 3145736 | tf_op jit(solution)/shard_map/ppermute | solution.py:499
  39.7 60.6 %collective-permute-start.4 = (f32[2,128,1024]{2,1,0:T(8,128)S(1)}, f32[2,128,1024]{2,1,0:T(8,128)}, u32[]{:S(2)}, u32[]{:S(2)}) collective-permute-start(f32[2,128,1024]{2,1,0:T(8,128)S(1)} %get-tuple-element.50), channel_id=1, source_target_pairs={{4,0},{6,2},{0,4},{2,6},{12,8},{14,10},{8,12},{10,14},{20,16},{22,... | collective-permute-start | bytes 3145736 | tf_op jit(solution)/shard_map/ppermute | solution.py:505
  55.8 23.3 %copy-start.2 = (f32[2,128,1024]{2,1,0:T(8,128)}, f32[2,128,1024]{2,1,0:T(8,128)S(1)}, u32[]{:S(2)}) copy-start(f32[2,128,1024]{2,1,0:T(8,128)S(1)} %collective-permute-done.refs_1_.refs_4_) | copy-start | bytes 3145732
  57.8 42.5 %collective-permute-start.2 = (f32[2,128,1024]{2,1,0:T(8,128)S(1)}, f32[2,128,1024]{2,1,0:T(8,128)S(1)}, u32[]{:S(2)}, u32[]{:S(2)}) collective-permute-start(f32[2,128,1024]{2,1,0:T(8,128)S(1)} %get-tuple-element.49), channel_id=1, source_target_pairs={{8,0},{10,2},{12,4},{14,6},{16,8},{18,10},{20,12},{22,14},{24,16},... | collective-permute-start | bytes 3145736 | tf_op jit(solution)/shard_map/ppermute | solution.py:499
  62.2 38.2 %collective-permute-start.5 = (f32[2,128,1024]{2,1,0:T(8,128)S(1)}, f32[2,128,1024]{2,1,0:T(8,128)S(1)}, u32[]{:S(2)}, u32[]{:S(2)}) collective-permute-start(f32[2,128,1024]{2,1,0:T(8,128)S(1)} %get-tuple-element.51), channel_id=1, source_target_pairs={{4,0},{6,2},{0,4},{2,6},{12,8},{14,10},{8,12},{10,14},{20,16},{22,... | collective-permute-start | bytes 3145736 | tf_op jit(solution)/shard_map/ppermute | solution.py:505
  78.3 22.0 %copy-start.4 = (f32[2,128,1024]{2,1,0:T(8,128)}, f32[2,128,1024]{2,1,0:T(8,128)S(1)}, u32[]{:S(2)}) copy-start(f32[2,128,1024]{2,1,0:T(8,128)S(1)} %collective-permute-done.6.refs_1_.refs_6_.refs_3_) | copy-start | bytes 3145732
  79.1 27.5 %collective-permute-start.7 = (f32[2,128,1024]{2,1,0:T(8,128)S(1)}, f32[2,128,1024]{2,1,0:T(8,128)S(1)}, u32[]{:S(2)}, u32[]{:S(2)}) collective-permute-start(f32[2,128,1024]{2,1,0:T(8,128)S(1)} %get-tuple-element.55), channel_id=1, source_target_pairs={{4,0},{6,2},{0,4},{2,6},{12,8},{14,10},{8,12},{10,14},{20,16},{22,... | collective-permute-start | bytes 3145736 | tf_op jit(solution)/shard_map/ppermute | solution.py:505
  100.3 13.4 %copy-start.5 = (f32[2,128,1024]{2,1,0:T(8,128)}, f32[2,128,1024]{2,1,0:T(8,128)S(1)}, u32[]{:S(2)}) copy-start(f32[2,128,1024]{2,1,0:T(8,128)S(1)} %collective-permute-done.2.refs_1_.refs_8_.refs_4_) | copy-start | bytes 3145732
  100.4 6.3 %copy-start.11 = (f32[2,128,1024]{2,1,0:T(8,128)}, f32[2,128,1024]{2,1,0:T(8,128)S(1)}, u32[]{:S(2)}) copy-start(f32[2,128,1024]{2,1,0:T(8,128)S(1)} %collective-permute-done.5.refs_6_.refs_3_.refs_2_) | copy-start | bytes 3145732
  106.6 1.0 copy-start.10
  113.7 1.0 copy-start.6
  114.7 37.5 %collective-permute-start.14 = (f32[2,512,1024]{2,1,0:T(8,128)}, f32[2,512,1024]{2,1,0:T(8,128)}, u32[]{:S(2)}, u32[]{:S(2)}) collective-permute-start(f32[2,512,1024]{2,1,0:T(8,128)} %get-tuple-element.65), channel_id=1, source_target_pairs={{2,0},{0,2},{6,4},{4,6},{10,8},{8,10},{14,12},{12,14},{18,16},{16,... | collective-permute-start | bytes 12582920 | tf_op jit(solution)/shard_map/ppermute | solution.py:508
  114.7 25.8 %collective-permute-start.9 = (f32[2,128,1024]{2,1,0:T(8,128)S(1)}, f32[2,128,1024]{2,1,0:T(8,128)S(1)}, u32[]{:S(2)}, u32[]{:S(2)}) collective-permute-start(f32[2,128,1024]{2,1,0:T(8,128)S(1)} %get-tuple-element.58), channel_id=1, source_target_pairs={{4,0},{6,2},{0,4},{2,6},{12,8},{14,10},{8,12},{10,14},{20,16},{22,... | collective-permute-start | bytes 3145736 | tf_op jit(solution)/shard_map/ppermute | solution.py:505
  116.7 25.3 %collective-permute-start.10 = (f32[2,128,1024]{2,1,0:T(8,128)S(1)}, f32[2,128,1024]{2,1,0:T(8,128)S(1)}, u32[]{:S(2)}, u32[]{:S(2)}) collective-permute-start(f32[2,128,1024]{2,1,0:T(8,128)S(1)} %get-tuple-element.59), channel_id=1, source_target_pairs={{8,0},{10,2},{12,4},{14,6},{16,8},{18,10},{20,12},{22,14},{24,16},... | collective-permute-start | bytes 3145736 | tf_op jit(solution)/shard_map/ppermute | solution.py:499
  117.0 25.0 %collective-permute-start.11 = (f32[2,128,1024]{2,1,0:T(8,128)S(1)}, f32[2,128,1024]{2,1,0:T(8,128)S(1)}, u32[]{:S(2)}, u32[]{:S(2)}) collective-permute-start(f32[2,128,1024]{2,1,0:T(8,128)S(1)} %get-tuple-element.61), channel_id=1, source_target_pairs={{1,0},{0,1},{3,2},{2,3},{5,4},{4,5},{7,6},{6,7},{9,8},{8,9},{11,10... | collective-permute-start | bytes 3145736 | tf_op jit(solution)/shard_map/ppermute | solution.py:502
  140.5 1.5 copy-start.9
  141.9 7.1 %copy-start.3 = (f32[2,128,1024]{2,1,0:T(8,128)}, f32[2,128,1024]{2,1,0:T(8,128)S(1)}, u32[]{:S(2)}) copy-start(f32[2,128,1024]{2,1,0:T(8,128)S(1)} %collective-permute-done.10.refs_1_.refs_6_.refs_3_) | copy-start | bytes 3145732
  142.0 1.1 copy-start.8
  143.1 6.0 %copy-start.7 = (f32[2,128,1024]{2,1,0:T(8,128)S(1)}, f32[2,128,1024]{2,1,0:T(8,128)}, u32[]{:S(2)}) copy-start(f32[2,128,1024]{2,1,0:T(8,128)} %copy-done.6) | copy-start | bytes 3145732
  149.0 36.5 %collective-permute-start.18 = (f32[2,512,1024]{2,1,0:T(8,128)}, f32[2,512,1024]{2,1,0:T(8,128)}, u32[]{:S(2)}, u32[]{:S(2)}) collective-permute-start(f32[2,512,1024]{2,1,0:T(8,128)} %get-tuple-element.72), channel_id=1, source_target_pairs={{2,0},{0,2},{6,4},{4,6},{10,8},{8,10},{14,12},{12,14},{18,16},{16,... | collective-permute-start | bytes 12582920 | tf_op jit(solution)/shard_map/ppermute | solution.py:508
  149.1 26.0 %collective-permute-start.8 = (f32[2,128,1024]{2,1,0:T(8,128)S(1)}, f32[2,128,1024]{2,1,0:T(8,128)S(1)}, u32[]{:S(2)}, u32[]{:S(2)}) collective-permute-start(f32[2,128,1024]{2,1,0:T(8,128)S(1)} %copy-done.7), channel_id=1, source_target_pairs={{8,0},{10,2},{12,4},{14,6},{16,8},{18,10},{20,12},{22,14},{24,16},... | collective-permute-start | bytes 3145736 | tf_op jit(solution)/shard_map/ppermute | solution.py:499
  151.2 25.2 %collective-permute-start.12 = (f32[2,128,1024]{2,1,0:T(8,128)S(1)}, f32[2,128,1024]{2,1,0:T(8,128)S(1)}, u32[]{:S(2)}, u32[]{:S(2)}) collective-permute-start(f32[2,128,1024]{2,1,0:T(8,128)S(1)} %get-tuple-element.62), channel_id=1, source_target_pairs={{4,0},{6,2},{0,4},{2,6},{12,8},{14,10},{8,12},{10,14},{20,16},{22,... | collective-permute-start | bytes 3145736 | tf_op jit(solution)/shard_map/ppermute | solution.py:505
  151.7 24.9 %collective-permute-start.13 = (f32[2,128,1024]{2,1,0:T(8,128)S(1)}, f32[2,128,1024]{2,1,0:T(8,128)S(1)}, u32[]{:S(2)}, u32[]{:S(2)}) collective-permute-start(f32[2,128,1024]{2,1,0:T(8,128)S(1)} %get-tuple-element.63), channel_id=1, source_target_pairs={{1,0},{0,1},{3,2},{2,3},{5,4},{4,5},{7,6},{6,7},{9,8},{8,9},{11,10... | collective-permute-start | bytes 3145736 | tf_op jit(solution)/shard_map/ppermute | solution.py:502
  152.2 57.6 %collective-permute-start.17 = (f32[2,128,1024]{2,1,0:T(8,128)S(1)}, f32[2,128,1024]{2,1,0:T(8,128)S(1)}, u32[]{:S(2)}, u32[]{:S(2)}) collective-permute-start(f32[2,128,1024]{2,1,0:T(8,128)S(1)} %get-tuple-element.70), channel_id=1, source_target_pairs={{8,0},{10,2},{12,4},{14,6},{16,8},{18,10},{20,12},{22,14},{24,16},... | collective-permute-start | bytes 3145736 | tf_op jit(solution)/shard_map/ppermute | solution.py:499
  175.1 8.3 %copy-start = (f32[2,128,1024]{2,1,0:T(8,128)}, f32[2,128,1024]{2,1,0:T(8,128)S(1)}, u32[]{:S(2)}) copy-start(f32[2,128,1024]{2,1,0:T(8,128)S(1)} %collective-permute-done.8.refs_1_.refs_3_) | copy-start | bytes 3145732
  176.4 1.0 copy-start.13
  176.6 1.1 copy-start.14
  183.5 26.3 %collective-permute-start.15 = (f32[2,128,1024]{2,1,0:T(8,128)S(1)}, f32[2,128,1024]{2,1,0:T(8,128)S(1)}, u32[]{:S(2)}, u32[]{:S(2)}) collective-permute-start(f32[2,128,1024]{2,1,0:T(8,128)S(1)} %get-tuple-element.68), channel_id=1, source_target_pairs={{4,0},{6,2},{0,4},{2,6},{12,8},{14,10},{8,12},{10,14},{20,16},{22,... | collective-permute-start | bytes 3145736 | tf_op jit(solution)/shard_map/ppermute | solution.py:505
  185.0 24.8 %collective-permute-start.16 = (f32[2,128,1024]{2,1,0:T(8,128)S(1)}, f32[2,128,1024]{2,1,0:T(8,128)S(1)}, u32[]{:S(2)}, u32[]{:S(2)}) collective-permute-start(f32[2,128,1024]{2,1,0:T(8,128)S(1)} %get-tuple-element.69), channel_id=1, source_target_pairs={{1,0},{0,1},{3,2},{2,3},{5,4},{4,5},{7,6},{6,7},{9,8},{8,9},{11,10... | collective-permute-start | bytes 3145736 | tf_op jit(solution)/shard_map/ppermute | solution.py:502
  185.5 29.5 %collective-permute-start.20 = (f32[2,512,1024]{2,1,0:T(8,128)}, f32[2,512,1024]{2,1,0:T(8,128)}, u32[]{:S(2)}, u32[]{:S(2)}) collective-permute-start(f32[2,512,1024]{2,1,0:T(8,128)} %get-tuple-element.76), channel_id=1, source_target_pairs={{2,0},{0,2},{6,4},{4,6},{10,8},{8,10},{14,12},{12,14},{18,16},{16,... | collective-permute-start | bytes 12582920 | tf_op jit(solution)/shard_map/ppermute | solution.py:508
  209.8 1.0 copy-start.12
  209.8 1.3 copy-start.15
  209.8 1.6 copy-start.16
  214.4 13.2 %collective-permute-start.19 = (f32[2,512,1024]{2,1,0:T(8,128)S(1)}, f32[2,512,1024]{2,1,0:T(8,128)S(1)}, u32[]{:S(2)}, u32[]{:S(2)}) collective-permute-start(f32[2,512,1024]{2,1,0:T(8,128)S(1)} %get-tuple-element.75), channel_id=1, source_target_pairs={{2,0},{0,2},{6,4},{4,6},{10,8},{8,10},{14,12},{12,14},{18,16},{16,... | collective-permute-start | bytes 12582920 | tf_op jit(solution)/shard_map/ppermute | solution.py:508
  242.8 3.6 %collective-permute-start.21 = (f32[2]{0:T(128)S(1)}, f32[2]{0:T(128)S(1)}, u32[]{:S(2)}, u32[]{:S(2)}) collective-permute-start(f32[2]{0:T(128)S(1)} %broadcast_multiply_fusion), channel_id=1, source_target_pairs={{1,0},{0,1},{3,2},{2,3},{5,4},{4,5},{7,6},{6,7},{9,8},{8,9},{11,10... | collective-permute-start | bytes 32 | tf_op jit(solution)/shard_map/ppermute | solution.py:502

commit v2 on v1

--- a/solution.py
+++ b/solution.py
@@ -53,7 +53,7 @@
         made[0].wait()
 
 
-def route(meta, outputs, after, in_vmem):
+def route(meta, outputs, after, near):
     arrays, place = [], {}
     plan = []
     for pieces in outputs:
@@ -70,13 +70,15 @@
     width = arrays[0].shape[2]
     heights = [sum(piece[1] for piece in pieces) for pieces in plan]
     arrays += after
-    shape_of = pltpu.VMEM if in_vmem else jax.ShapeDtypeStruct
     chosen = any(piece[2] is not None for pieces in plan for piece in pieces)
     return pl.pallas_call(
         functools.partial(route_kernel, plan, int(chosen), len(arrays)),
         in_specs=[pl.BlockSpec(memory_space=pltpu.SMEM)] * chosen + [ANY] * len(arrays),
         out_specs=[pl.BlockSpec(memory_space=pltpu.VMEM)] * len(plan) + [ANY],
-        out_shape=[shape_of((2, h, width), F32) for h in heights] + [TOKEN],
+        out_shape=[
+            (pltpu.VMEM if n else jax.ShapeDtypeStruct)((2, h, width), F32) for n, h in zip(near, heights)
+        ]
+        + [TOKEN],
         scratch_shapes=[pltpu.SemaphoreType.DMA((CHUNKS * sum(len(p) for p in plan),))],
         compiler_params=pltpu.CompilerParams(vmem_limit_bytes=ROUTE_LIMIT),
         cost_estimate=GATE,
@@ -272,7 +274,7 @@
     sources, refs = refs[:count], refs[count:]
     f_in, refs = refs[0], refs[1:]
     p_refs, refs = refs[:partners], refs[partners:]
-    f_out, refs = refs[0], refs[1:]
+    f_out, _, refs = refs[0], refs[1], refs[2:]
     if partners:
         tr_out, refs = refs[0], refs[1:]
     raw, left6, left, *refs = refs
@@ -430,8 +432,8 @@
     tiles = width // TILE
     sources, (places,) = placed([cands])
     raw, raw_sems = fetch_scratch(pairs, total, width, len(places[0]))
-    out_specs = [ANY]
-    out_shape = [jax.ShapeDtypeStruct((pairs, 2, rows, width), F32)]
+    out_specs = [ANY, ANY]
+    out_shape = [jax.ShapeDtypeStruct((pairs, 2, rows, width), F32), TOKEN]
     scratch = [raw, *operand_scratch(rows, total, rows), pltpu.VMEM((pairs, 2, rows, width), F32), raw_sems]
     scratch += [pltpu.SemaphoreType.DMA((1,)), pltpu.SemaphoreType.DMA((2 + len(partners), tiles, pairs))]
     if partners:
@@ -462,10 +464,10 @@
         ([("x", 0, 0), ("z", 0, 2)], [("own", 0)], []),
         ([("x", 0, 1), ("z", 0, 3)], [], []),
         ([("x", 0, 2)], [], []),
-        ([("x", 0, 3), ("z", 1, 0), ("z", 1, 2), ("zy", 1, 1), ("c", 0, 0)], [("other", 0)], [("x", 0, 2)]),
-        ([("x", 1, 0), ("z", 1, 3), ("xy", 1, 1), ("c", 0, 1)], [], [("z", 1, 1)]),
-        ([("x", 1, 2), ("xy", 1, 3), ("c", 1, 0)], [("both", 0)], []),
-        ([("c", 1, 1)], [("both", 1)], []),
+        ([("x", 0, 3), ("z", 1, 0), ("z", 1, 2), ("zy", 1, 1), ("c", 0, 0), ("d", 0, 1)], [("other", 0)], []),
+        ([("x", 1, 0), ("z", 1, 3), ("xy", 1, 1), ("xy", 1, 3), ("e", 0, 3)], [("both", 0)], [("z", 1, 1)]),
+        ([("x", 1, 2), ("c", 1, 0)], [("both", 1)], []),
+        ([("c", 1, 1)], [("more", 0)], []),
     ),
     1: (
         ([("z", 0, 0)], [], []),
@@ -517,15 +519,16 @@
     def operand(kind, j, q):
         if kind == "z":
             return [(0, part, None, [here(j, q)])]
-        if kind in ("zy", "xy"):
-            return [(0, part, None, [(got[kind[0], 0, q], 0)])]
+        if kind in ("zy", "xy", "e"):
+            return [(0, part, None, [(got["x" if kind == "e" else kind[0], 0, q], 0)])]
         if kind == "x":
             arrived = held(got["z", j, q]) if planes == 2 else got["z", j, q]
             return [(0, part, odd_at, [(arrived, 0), here(j, q)])]
         pieces = (2 * q, 2 * q + 1)
-        out = [(i * part, part, None, [(got["x", j, p], 0)]) for i, p in enumerate(pieces)]
+        pieces_x = pieces[:1] if kind == "d" else pieces
+        out = [(i * part, part, None, [(got["x", j, p], 0)]) for i, p in enumerate(pieces_x)]
         return out + [
-            ((i + 2) * part, part, lane_at, [(got["z", j, p], 0), here(j, p)]) for i, p in enumerate(pieces)
+            ((i + len(pieces_x)) * part, part, lane_at, [(got["z", j, p], 0), here(j, p)]) for i, p in enumerate(pieces)
         ]
 
     def send(kind, j, q, x):
@@ -539,9 +542,14 @@
 
     def candidates(j, group, near=False):
         picks = (2 * group, 2 * group + 1)
-        swapped = held(got["c", j, group]) if near else got["c", j, group]
-        cross4 = [(swapped, 2 * part), (swapped, 3 * part)]
-        cross2 = [(swapped, 0), (swapped, part)]
+        if ("c", j, group) in got:
+            swapped = held(got["c", j, group]) if near else got["c", j, group]
+            cross4 = [(swapped, 2 * part), (swapped, 3 * part)]
+            cross2 = [(swapped, 0), (swapped, part)]
+        else:
+            swapped = got["d", j, group]
+            cross4 = [(swapped, part), (swapped, 2 * part)]
+            cross2 = [(swapped, 0), (got["e", j, picks[1]], 0)]
         return [
             cross4,
             [(got["x", j, q], 0) for q in picks],
@@ -568,20 +576,26 @@
                     block6, done = split_block(got["y", j])
                     others6.append(block6)
                     after.append(done)
+            elif kind == "more":
+                for j in range(1, planes):
+                    f, done = more_call(meta, own6, candidates(j, g), f, [], j, g, groups)
+                    after.append(done)
             else:
                 f, partner, done = both_call(meta, own6, others6, candidates(0, g), f, g, groups)
                 partners.append(partner)
                 after.append(done)
-        written = route(meta, [operand(*task) for task in tasks], after, planes == 2)
+        written = route(
+            meta, [operand(*task) for task in tasks], after, [planes == 2 and task[0] != "d" for task in tasks]
+        )
         for (kind, j, q), x in zip(tasks, written[:-1]):
             got[kind[0], j, q] = send(kind, j, q, x)
 
-    for g in range(groups):
-        for j in range(1, planes):
-            last = g == groups - 1 and j == planes - 1
-            out = more_call(meta, own6, candidates(j, g, last and planes == 2), f, partners if last else [], j, g, groups)
-            f = out[0]
-    partial_trace = jnp.sum(out[1], axis=(1, 2)) / F32(width)
+    for j in range(1, planes):
+        near, last = planes == 2, j == planes - 1
+        cands = candidates(j, groups - 1, near)
+        out = more_call(meta, own6, cands, f, partners if last else [], j, groups - 1, groups)
+        f = out[0]
+    partial_trace = jnp.sum(out[2], axis=(1, 2)) / F32(width)
     if planes == 2:
         traces = partial_trace + from_plane(partial_trace, 1)
     else:

time: 248 us -> 240 us (0.968)
  waiting for transfers between devices: 94.6 us -> 86.4 us
  local copies, waits for them, and re-layouts: 5.81 us -> 9.95 us
  Pallas kernels: 112 us -> 108 us
    ppermute x6, waiting for transfers between devices: 30.5 us -> 5.41 us  [across_chips(): return lax.ppermute(x, 'tm', [(i ^ 2, i) for i in range(steps)])]
    ppermute x4 -> x5, waiting for transfers between devices: 0.01 us -> 15.7 us  [across_cores(): return lax.ppermute(x, 'tm', [(i ^ 1, i) for i in range(steps)])]
    ppermute x5, waiting for transfers between devices: 15.2 us -> 19.5 us  [from_plane(): lax.ppermute(x, 'mode', [((i + shift) % planes, i) for i in range(planes)])]
    unnamed x36 -> x40, local copies, waits for them, and re-layouts: 5.81 us -> 9.95 us
    pallas_call x9, Pallas kernels: 28.9 us -> 25.4 us  [route(): pl.pallas_call(functools.partial(route_kernel, plan, int(chosen), len(arr...]
    ppermute x7, waiting for transfers between devices: 48.8 us -> 45.8 us  [from_later(): return lax.ppermute(x, 'tm', [((i + 4) % steps, i) for i in range(steps)])]
  transfers between devices with their start and end apart: 22 -> 23, of which waited for: 12 -> 12; matrix products, arithmetic and copies ran while one was open for 0% -> 0% of each run, Pallas kernels for 37% -> 33%
where the time goes in v2:
time: 240 us
  Pallas kernels  108 us (45%)
  waiting for transfers between devices  86.4 us (36%)
  starting transfers between devices  32.2 us (13%)
  local copies, waits for them, and re-layouts  9.95 us (4%)
    ppermute x7, waiting for transfers between devices, from_later(): return lax.ppermute(x, 'tm', [((i + 4) % steps, i) for i in range(steps)])  45.8 us
    pallas_call x2, Pallas kernels, both_call(): pl.pallas_call(functools.partial(both_kernel, places, len(sources), f is...  44.3 us
    pallas_call x2, Pallas kernels, more_call(): pl.pallas_call(functools.partial(more_kernel, places, len(sources), len(p...  27.2 us
    pallas_call x9, Pallas kernels, route(): pl.pallas_call(functools.partial(route_kernel, plan, int(chosen), len(arr...  25.4 us
    ppermute x5, waiting for transfers between devices, from_plane(): lax.ppermute(x, 'mode', [((i + shift) % planes, i) for i in range(planes)])  19.5 us
    ppermute x5, waiting for transfers between devices, across_cores(): return lax.ppermute(x, 'tm', [(i ^ 1, i) for i in range(steps)])  15.7 us
    ppermute x7, starting transfers between devices, from_later(): return lax.ppermute(x, 'tm', [((i + 4) % steps, i) for i in range(steps)])  13.6 us
    pallas_call x2, Pallas kernels, split_block(): pl.pallas_call(split_kernel, grid=(width // SPLIT_TILE,), in_specs=[pl.Bl...  11.5 us
  transfers between devices with their start and end apart: 23, of which 12 were waited for; matrix products, arithmetic and copies ran while one was open for 0% of the time, Pallas kernels for 33%

profile of v2, /device:TPU:0, one launch (start us, length us, event | category | flops | bytes accessed | tf_op | source)
XLA Modules:
  0.0 239.8 jit_solution(1887285460004800618)
XLA Ops:
  0.6 3.0 %collective-permute-start.3 = (f32[2,512,1024]{2,1,0:T(8,128)}, f32[2,512,1024]{2,1,0:T(8,128)}, u32[]{:S(2)}, u32[]{:S(2)}) collective-permute-start(f32[2,512,1024]{2,1,0:T(8,128)} %bitcast.15), channel_id=1, source_target_pairs={{1,0},{0,1},{3,2},{2,3},{5,4},{4,5},{7,6},{6,7},{9,8},{8,9},{11,10... | collective-permute-start | bytes 12582920 | tf_op jit(solution)/shard_map/ppermute | solution.py:504
  3.7 2.2 shard_map.42
  5.9 3.7 %collective-permute-start.1 = (f32[2,128,1024]{2,1,0:T(8,128)}, f32[2,128,1024]{2,1,0:T(8,128)S(1)}, u32[]{:S(2)}, u32[]{:S(2)}) collective-permute-start(f32[2,128,1024]{2,1,0:T(8,128)} %get-tuple-element.48), channel_id=1, source_target_pairs={{8,0},{10,2},{12,4},{14,6},{16,8},{18,10},{20,12},{22,14},{24,16},... | collective-permute-start | bytes 3145736 | tf_op jit(solution)/shard_map/ppermute | solution.py:501
  9.5 1.2 shard_map.43
  11.3 0.7 pad_add_fusion.refs_0_.meta
  11.9 5.8 %shard_map.41 = (bf16[6,512,1024]{2,1,0:T(8,128)(2,1)}, f32[8,128]{1,0:T(8,128)}) custom-call(f32[2,512,1024]{2,1,0:T(8,128)} %bitcast.18), custom_call_target="tpu_custom_call" | custom-call | flops 1 | bytes 1 | tf_op jit(solution)/shard_map/pallas_call | solution.py:107
  17.7 15.8 %collective-permute-done.1.refs_1_.refs_7_.refs_3_ = f32[2,128,1024]{2,1,0:T(8,128)S(1)} collective-permute-done((f32[2,128,1024]{2,1,0:T(8,128)}, f32[2,128,1024]{2,1,0:T(8,128)S(1)}, u32[]{:S(2)}, u32[]{:S(2)}) %collective-permute-start.1) | collective-permute-done | bytes 1048608 | tf_op jit(solution)/shard_map/ppermute | solution.py:501
  33.4 2.0 shard_map.44
  35.5 4.2 %collective-permute-start.6 = (f32[2,128,1024]{2,1,0:T(8,128)S(1)}, f32[2,128,1024]{2,1,0:T(8,128)S(1)}, u32[]{:S(2)}, u32[]{:S(2)}) collective-permute-start(f32[2,128,1024]{2,1,0:T(8,128)S(1)} %get-tuple-element.55), channel_id=1, source_target_pairs={{8,0},{10,2},{12,4},{14,6},{16,8},{18,10},{20,12},{22,14},{24,16},... | collective-permute-start | bytes 3145736 | tf_op jit(solution)/shard_map/ppermute | solution.py:501
  39.7 1.7 collective-permute-start.4
  41.4 14.4 %collective-permute-done.refs_1_.refs_4_ = f32[2,128,1024]{2,1,0:T(8,128)S(1)} collective-permute-done((f32[2,128,1024]{2,1,0:T(8,128)S(1)}, f32[2,128,1024]{2,1,0:T(8,128)S(1)}, u32[]{:S(2)}, u32[]{:S(2)}) %collective-permute-start) | collective-permute-done | bytes 1048608 | tf_op jit(solution)/shard_map/ppermute | solution.py:501
  55.8 2.0 shard_map.45
  57.8 4.3 %collective-permute-start.2 = (f32[2,128,1024]{2,1,0:T(8,128)S(1)}, f32[2,128,1024]{2,1,0:T(8,128)S(1)}, u32[]{:S(2)}, u32[]{:S(2)}) collective-permute-start(f32[2,128,1024]{2,1,0:T(8,128)S(1)} %get-tuple-element.52), channel_id=1, source_target_pairs={{8,0},{10,2},{12,4},{14,6},{16,8},{18,10},{20,12},{22,14},{24,16},... | collective-permute-start | bytes 3145736 | tf_op jit(solution)/shard_map/ppermute | solution.py:501
  62.2 1.7 collective-permute-start.5
  63.9 14.4 %collective-permute-done.6.refs_1_.refs_9_.refs_4_ = f32[2,128,1024]{2,1,0:T(8,128)S(1)} collective-permute-done((f32[2,128,1024]{2,1,0:T(8,128)S(1)}, f32[2,128,1024]{2,1,0:T(8,128)S(1)}, u32[]{:S(2)}, u32[]{:S(2)}) %collective-permute-start.6) | collective-permute-done | bytes 1048608 | tf_op jit(solution)/shard_map/ppermute | solution.py:501
  78.3 0.8 shard_map.46
  79.1 2.6 %collective-permute-start.7 = (f32[2,128,1024]{2,1,0:T(8,128)S(1)}, f32[2,128,1024]{2,1,0:T(8,128)S(1)}, u32[]{:S(2)}, u32[]{:S(2)}) collective-permute-start(f32[2,128,1024]{2,1,0:T(8,128)S(1)} %get-tuple-element.57), channel_id=1, source_target_pairs={{4,0},{6,2},{0,4},{2,6},{12,8},{14,10},{8,12},{10,14},{20,16},{22,... | collective-permute-start | bytes 3145736 | tf_op jit(solution)/shard_map/ppermute | solution.py:507
  81.8 12.8 %collective-permute-done.3.x_ref.refs_3_.refs_2_.refs_4_ = f32[2,512,1024]{2,1,0:T(8,128)} collective-permute-done((f32[2,512,1024]{2,1,0:T(8,128)}, f32[2,512,1024]{2,1,0:T(8,128)}, u32[]{:S(2)}, u32[]{:S(2)}) %collective-permute-start.3) | collective-permute-done | bytes 4194336 | tf_op jit(solution)/shard_map/ppermute | solution.py:504
  94.6 5.8 %shard_map.47 = (bf16[6,512,1024]{2,1,0:T(8,128)(2,1)}, f32[8,128]{1,0:T(8,128)}) custom-call(f32[2,512,1024]{2,1,0:T(8,128)} %collective-permute-done.3.x_ref.refs_3_.refs_2_.refs_4_), custom_call_target="tpu_custom_call" | custom-call | flops 1 | bytes 1 | tf_op jit(solution)/shard_map/pallas_call | solution.py:107
  100.3 1.0 copy-done
  101.3 5.3 %collective-permute-done.7.refs_8_.refs_1_ = f32[2,128,1024]{2,1,0:T(8,128)S(1)} collective-permute-done((f32[2,128,1024]{2,1,0:T(8,128)S(1)}, f32[2,128,1024]{2,1,0:T(8,128)S(1)}, u32[]{:S(2)}, u32[]{:S(2)}) %collective-permute-start.7) | collective-permute-done | bytes 1048608 | tf_op jit(solution)/shard_map/ppermute | solution.py:507
  106.6 1.0 copy-done.12
  107.6 1.2 copy-done.1
  108.8 7.9 %shard_map.48 = (f32[2,128,1024]{2,1,0:T(8,128)S(1)}, f32[2,128,1024]{2,1,0:T(8,128)S(1)}, f32[2,128,1024]{2,1,0:T(8,128)S(1)}, f32[2,128,1024]{2,1,0:T(8,128)S(...) custom-call(s32[5]{0:T(128)} %pad_add_fusion.refs_0_.meta, f32[2,128,1024]{2,1,0:T(8,128)S(1)} %copy-done.1, ...), custom_call_target="tpu_custom_call" | custom-call | flops 1 | bytes 1 | tf_op jit(solution)/shard_map/pallas_call | solution.py:74
  117.7 2.0 collective-permute-start.10
  120.2 4.2 %collective-permute-done.12.refs_0_ = f32[2,512,1024]{2,1,0:T(8,128)} collective-permute-done((f32[2,512,1024]{2,1,0:T(8,128)}, f32[2,512,1024]{2,1,0:T(8,128)}, u32[]{:S(2)}, u32[]{:S(2)}) %collective-permute-start.12) | collective-permute-done | bytes 4194336 | tf_op jit(solution)/shard_map/ppermute | solution.py:510
  124.3 20.0 %shard_map.49 = (f32[2,2,512,1024]{3,2,1,0:T(8,128)}, f32[2,2,256,1024]{3,2,1,0:T(8,128)}, f32[8,128]{1,0:T(8,128)}) custom-call(s32[5]{0:T(128)} %pad_add_fusion.refs_0_.meta, bf16[6,512,1024]{2,1,0:T(8,128)(2,1)} %get-tuple-element.45.own6, f32[2,512,1024]{2,1,0:T(8,128)} %collective-permute-done.12.refs_0_, ...), custom_call_target="tpu_custom_call" | custom-call | flops 1 | bytes 1 | tf_op jit(solution)/shard_map/pallas_call | solution.py:398
  144.4 1.0 copy-done.13
  145.8 3.2 %shard_map.50 = (f32[2,128,1024]{2,1,0:T(8,128)S(1)}, f32[2,128,1024]{2,1,0:T(8,128)S(1)}, f32[2,128,1024]{2,1,0:T(8,128)S(1)}, f32[2,128,1024]{2,1,0:T(8,128)S(...) custom-call(s32[5]{0:T(128)} %pad_add_fusion.refs_0_.meta, ...), custom_call_target="tpu_custom_call" | custom-call | flops 1 | bytes 1 | tf_op jit(solution)/shard_map/pallas_call | solution.py:74
  149.7 2.2 collective-permute-start.13
  152.4 1.0 copy-done.18
  153.4 24.3 %shard_map.51 = (f32[2,2,512,1024]{3,2,1,0:T(8,128)}, f32[2,2,256,1024]{3,2,1,0:T(8,128)}, f32[8,128]{1,0:T(8,128)}) custom-call(s32[5]{0:T(128)} %pad_add_fusion.refs_0_.meta, bf16[6,512,1024]{2,1,0:T(8,128)(2,1)} %get-tuple-element.45.own6, f32[2,384,1024]{2,1,0:T(8,128)} %collective-permute-done.15.refs_0_, ...), custom_call_target="tpu_custom_call", output_to_operand_aliasing={{0}: (9, {})} | custom-call | flops 1 | bytes 1 | tf_op jit(solution)/shard_map/pallas_call | solution.py:398
  177.8 1.0 copy-done.16
  179.1 3.1 %shard_map.52 = (f32[2,128,1024]{2,1,0:T(8,128)S(1)}, f32[2,512,1024]{2,1,0:T(8,128)S(1)}, f32[8,128]{1,0:T(8,128)}) custom-call(s32[5]{0:T(128)} %pad_add_fusion.refs_0_.meta, f32[2,128,1024]{2,1,0:T(8,128)S(1)} %collective-permute-done.8.refs_1_.refs_3_, f32[2,512,1024]{2,1,0:T(8,128)} %collective-permute-done.3.x_ref.refs_3_.refs_2_.refs_4_, ...), custom_call_target="tpu_custom_call" | custom-call | flops 1 | bytes 1 | tf_op jit(solution)/shard_map/pallas_call | solution.py:74
  182.3 1.6 collective-permute-start.18
  183.9 1.1 collective-permute-start.17
  185.1 4.4 %collective-permute-done.20.refs_0_ = f32[2,512,1024]{2,1,0:T(8,128)S(1)} collective-permute-done((f32[2,512,1024]{2,1,0:T(8,128)S(1)}, f32[2,512,1024]{2,1,0:T(8,128)S(1)}, u32[]{:S(2)}, u32[]{:S(2)}) %collective-permute-start.20) | collective-permute-done | bytes 4194336 | tf_op jit(solution)/shard_map/ppermute | solution.py:510
  189.4 2.1 copy-done.11
  191.5 12.5 %shard_map.53 = (f32[2,2,512,1024]{3,2,1,0:T(8,128)}, f32[8,128]{1,0:T(8,128)}) custom-call(s32[5]{0:T(128)} %pad_add_fusion.refs_0_.meta, bf16[6,512,1024]{2,1,0:T(8,128)(2,1)} %get-tuple-element.45.own6, f32[2,512,1024]{2,1,0:T(8,128)} %copy-done.11, f32[2,128,1024]{2,1,0:T(8,128)} %copy-done.16, ...), custom_call_target="tpu_custom_call", output_to_operand_aliasing={{0}: (7, {})} | custom-call | flops 1 | bytes 1 | tf_op jit(solution)/shard_map/pallas_call | solution.py:444
  204.0 3.8 %collective-permute-done.18.refs_2_ = f32[2,128,1024]{2,1,0:T(8,128)S(1)} collective-permute-done((f32[2,128,1024]{2,1,0:T(8,128)S(1)}, f32[2,128,1024]{2,1,0:T(8,128)S(1)}, u32[]{:S(2)}, u32[]{:S(2)}) %collective-permute-start.18) | collective-permute-done | bytes 1048608 | tf_op jit(solution)/shard_map/ppermute | solution.py:504
  207.9 1.2 collective-permute-done.19.refs_5_.refs_4_
  209.2 0.9 copy-done.15
  210.1 2.9 %shard_map.54 = (f32[2,512,1024]{2,1,0:T(8,128)S(1)}, f32[8,128]{1,0:T(8,128)}) custom-call(s32[5]{0:T(128)} %pad_add_fusion.refs_0_.meta, f32[2,128,1024]{2,1,0:T(8,128)} %collective-permute-done.17.refs_1_, f32[2,128,1024]{2,1,0:T(8,128)} %copy-done.14, f32[2,128,1024]{2,1,0:T(8,128)} %copy-done.6, ...), custom_call_target="tpu_custom_call" | custom-call | flops 1 | bytes 1 | tf_op jit(solution)/shard_map/pallas_call | solution.py:74
  213.2 7.1 %collective-permute-done.21.refs_0_ = f32[2,512,1024]{2,1,0:T(8,128)S(1)} collective-permute-done((f32[2,512,1024]{2,1,0:T(8,128)S(1)}, f32[2,512,1024]{2,1,0:T(8,128)S(1)}, u32[]{:S(2)}, u32[]{:S(2)}) %collective-permute-start.21) | collective-permute-done | bytes 4194336 | tf_op jit(solution)/shard_map/ppermute | solution.py:510
  220.3 14.6 %shard_map.55 = (f32[2,2,512,1024]{3,2,1,0:T(8,128)}, f32[8,128]{1,0:T(8,128)}, f32[2,8,128]{2,1,0:T(8,128)}) custom-call(s32[5]{0:T(128)} %pad_add_fusion.refs_0_.meta, bf16[6,512,1024]{2,1,0:T(8,128)(2,1)} %get-tuple-element.45.own6, f32[2,512,1024]{2,1,0:T(8,128)S(1)} %collective-permute-done.21.refs_0_, ...), custom_call_target="tpu_custom_call", output_to_operand_aliasing={{0}: (7, {})} | custom-call | flops 1 | bytes 1 | tf_op jit(solution)/shard_map/pallas_call | solution.py:444
  235.0 0.8 reduce_sum.9
  235.8 0.7 collective-permute-start.22
  236.4 2.9 %collective-permute-done.22 = f32[2]{0:T(128)S(1)} collective-permute-done((f32[2]{0:T(128)S(1)}, f32[2]{0:T(128)S(1)}, u32[]{:S(2)}, u32[]{:S(2)}) %collective-permute-start.22) | collective-permute-done | bytes 40 | tf_op jit(solution)/shard_map/ppermute | solution.py:504
  (58 shorter events, 4.8 us)
Async XLA Ops:
  0.6 10.6 %copy-start.19 = (s32[1,2]{1,0:T(1,128)S(1)}, s32[1,2]{1,0:T(1,128)}, u32[]{:S(2)}) copy-start(s32[1,2]{1,0:T(1,128)} %param.3) | copy-start | bytes 28
  0.6 93.9 %collective-permute-start.3 = (f32[2,512,1024]{2,1,0:T(8,128)}, f32[2,512,1024]{2,1,0:T(8,128)}, u32[]{:S(2)}, u32[]{:S(2)}) collective-permute-start(f32[2,512,1024]{2,1,0:T(8,128)} %bitcast.15), channel_id=1, source_target_pairs={{1,0},{0,1},{3,2},{2,3},{5,4},{4,5},{7,6},{6,7},{9,8},{8,9},{11,10... | collective-permute-start | bytes 12582920 | tf_op jit(solution)/shard_map/ppermute | solution.py:504
  5.9 27.6 %collective-permute-start.1 = (f32[2,128,1024]{2,1,0:T(8,128)}, f32[2,128,1024]{2,1,0:T(8,128)S(1)}, u32[]{:S(2)}, u32[]{:S(2)}) collective-permute-start(f32[2,128,1024]{2,1,0:T(8,128)} %get-tuple-element.48), channel_id=1, source_target_pairs={{8,0},{10,2},{12,4},{14,6},{16,8},{18,10},{20,12},{22,14},{24,16},... | collective-permute-start | bytes 3145736 | tf_op jit(solution)/shard_map/ppermute | solution.py:501
  10.8 45.1 %collective-permute-start = (f32[2,128,1024]{2,1,0:T(8,128)S(1)}, f32[2,128,1024]{2,1,0:T(8,128)S(1)}, u32[]{:S(2)}, u32[]{:S(2)}) collective-permute-start(f32[2,128,1024]{2,1,0:T(8,128)S(1)} %get-tuple-element.47), channel_id=1, source_target_pairs={{8,0},{10,2},{12,4},{14,6},{16,8},{18,10},{20,12},{22,14},{24,16},... | collective-permute-start | bytes 3145736 | tf_op jit(solution)/shard_map/ppermute | solution.py:501
  33.4 24.4 %copy-start.2 = (f32[2,128,1024]{2,1,0:T(8,128)}, f32[2,128,1024]{2,1,0:T(8,128)S(1)}, u32[]{:S(2)}) copy-start(f32[2,128,1024]{2,1,0:T(8,128)S(1)} %collective-permute-done.1.refs_1_.refs_7_.refs_3_) | copy-start | bytes 3145732
  35.5 42.8 %collective-permute-start.6 = (f32[2,128,1024]{2,1,0:T(8,128)S(1)}, f32[2,128,1024]{2,1,0:T(8,128)S(1)}, u32[]{:S(2)}, u32[]{:S(2)}) collective-permute-start(f32[2,128,1024]{2,1,0:T(8,128)S(1)} %get-tuple-element.55), channel_id=1, source_target_pairs={{8,0},{10,2},{12,4},{14,6},{16,8},{18,10},{20,12},{22,14},{24,16},... | collective-permute-start | bytes 3145736 | tf_op jit(solution)/shard_map/ppermute | solution.py:501
  39.7 60.6 %collective-permute-start.4 = (f32[2,128,1024]{2,1,0:T(8,128)S(1)}, f32[2,128,1024]{2,1,0:T(8,128)}, u32[]{:S(2)}, u32[]{:S(2)}) collective-permute-start(f32[2,128,1024]{2,1,0:T(8,128)S(1)} %get-tuple-element.53), channel_id=1, source_target_pairs={{4,0},{6,2},{0,4},{2,6},{12,8},{14,10},{8,12},{10,14},{20,16},{22,... | collective-permute-start | bytes 3145736 | tf_op jit(solution)/shard_map/ppermute | solution.py:507
  55.8 23.3 %copy-start.3 = (f32[2,128,1024]{2,1,0:T(8,128)}, f32[2,128,1024]{2,1,0:T(8,128)S(1)}, u32[]{:S(2)}) copy-start(f32[2,128,1024]{2,1,0:T(8,128)S(1)} %collective-permute-done.refs_1_.refs_4_) | copy-start | bytes 3145732
  57.8 42.5 %collective-permute-start.2 = (f32[2,128,1024]{2,1,0:T(8,128)S(1)}, f32[2,128,1024]{2,1,0:T(8,128)S(1)}, u32[]{:S(2)}, u32[]{:S(2)}) collective-permute-start(f32[2,128,1024]{2,1,0:T(8,128)S(1)} %get-tuple-element.52), channel_id=1, source_target_pairs={{8,0},{10,2},{12,4},{14,6},{16,8},{18,10},{20,12},{22,14},{24,16},... | collective-permute-start | bytes 3145736 | tf_op jit(solution)/shard_map/ppermute | solution.py:501
  62.2 39.1 %collective-permute-start.5 = (f32[2,128,1024]{2,1,0:T(8,128)S(1)}, f32[2,128,1024]{2,1,0:T(8,128)S(1)}, u32[]{:S(2)}, u32[]{:S(2)}) collective-permute-start(f32[2,128,1024]{2,1,0:T(8,128)S(1)} %get-tuple-element.54), channel_id=1, source_target_pairs={{4,0},{6,2},{0,4},{2,6},{12,8},{14,10},{8,12},{10,14},{20,16},{22,... | collective-permute-start | bytes 3145736 | tf_op jit(solution)/shard_map/ppermute | solution.py:507
  78.3 22.0 %copy-start.4 = (f32[2,128,1024]{2,1,0:T(8,128)}, f32[2,128,1024]{2,1,0:T(8,128)S(1)}, u32[]{:S(2)}) copy-start(f32[2,128,1024]{2,1,0:T(8,128)S(1)} %collective-permute-done.6.refs_1_.refs_9_.refs_4_) | copy-start | bytes 3145732
  79.1 27.5 %collective-permute-start.7 = (f32[2,128,1024]{2,1,0:T(8,128)S(1)}, f32[2,128,1024]{2,1,0:T(8,128)S(1)}, u32[]{:S(2)}, u32[]{:S(2)}) collective-permute-start(f32[2,128,1024]{2,1,0:T(8,128)S(1)} %get-tuple-element.57), channel_id=1, source_target_pairs={{4,0},{6,2},{0,4},{2,6},{12,8},{14,10},{8,12},{10,14},{20,16},{22,... | collective-permute-start | bytes 3145736 | tf_op jit(solution)/shard_map/ppermute | solution.py:507
  100.3 1.0 copy-start
  101.3 5.3 %copy-start.9 = (f32[2,128,1024]{2,1,0:T(8,128)}, f32[2,128,1024]{2,1,0:T(8,128)S(1)}, u32[]{:S(2)}) copy-start(f32[2,128,1024]{2,1,0:T(8,128)S(1)} %collective-permute-done.5.refs_6_.refs_2_.refs_3_) | copy-start | bytes 3145732
  106.6 1.0 copy-start.12
  107.6 1.2 copy-start.1
  116.8 27.6 %copy-start.7 = (f32[2,128,1024]{2,1,0:T(8,128)}, f32[2,128,1024]{2,1,0:T(8,128)S(1)}, u32[]{:S(2)}) copy-start(f32[2,128,1024]{2,1,0:T(8,128)S(1)} %get-tuple-element.60) | copy-start | bytes 3145732
  116.8 7.6 %collective-permute-start.12 = (f32[2,512,1024]{2,1,0:T(8,128)}, f32[2,512,1024]{2,1,0:T(8,128)}, u32[]{:S(2)}, u32[]{:S(2)}) collective-permute-start(f32[2,512,1024]{2,1,0:T(8,128)} %get-tuple-element.65), channel_id=1, source_target_pairs={{2,0},{0,2},{6,4},{4,6},{10,8},{8,10},{14,12},{12,14},{18,16},{16,... | collective-permute-start | bytes 12582920 | tf_op jit(solution)/shard_map/ppermute | solution.py:510
  116.8 35.5 %collective-permute-start.15 = (f32[2,384,1024]{2,1,0:T(8,128)}, f32[2,384,1024]{2,1,0:T(8,128)}, u32[]{:S(2)}, u32[]{:S(2)}) collective-permute-start(f32[2,384,1024]{2,1,0:T(8,128)} %get-tuple-element.71), channel_id=1, source_target_pairs={{2,0},{0,2},{6,4},{4,6},{10,8},{8,10},{14,12},{12,14},{18,16},{16,... | collective-permute-start | bytes 9437192 | tf_op jit(solution)/shard_map/ppermute | solution.py:510
  117.3 27.0 %collective-permute-start.9 = (f32[2,128,1024]{2,1,0:T(8,128)S(1)}, f32[2,128,1024]{2,1,0:T(8,128)S(1)}, u32[]{:S(2)}, u32[]{:S(2)}) collective-permute-start(f32[2,128,1024]{2,1,0:T(8,128)S(1)} %get-tuple-element.61), channel_id=1, source_target_pairs={{8,0},{10,2},{12,4},{14,6},{16,8},{18,10},{20,12},{22,14},{24,16},... | collective-permute-start | bytes 3145736 | tf_op jit(solution)/shard_map/ppermute | solution.py:501
  117.7 26.7 %collective-permute-start.10 = (f32[2,128,1024]{2,1,0:T(8,128)S(1)}, f32[2,128,1024]{2,1,0:T(8,128)S(1)}, u32[]{:S(2)}, u32[]{:S(2)}) collective-permute-start(f32[2,128,1024]{2,1,0:T(8,128)S(1)} %get-tuple-element.62), channel_id=1, source_target_pairs={{4,0},{6,2},{0,4},{2,6},{12,8},{14,10},{8,12},{10,14},{20,16},{22,... | collective-permute-start | bytes 3145736 | tf_op jit(solution)/shard_map/ppermute | solution.py:507
  119.7 24.7 %collective-permute-start.11 = (f32[2,128,1024]{2,1,0:T(8,128)S(1)}, f32[2,128,1024]{2,1,0:T(8,128)S(1)}, u32[]{:S(2)}, u32[]{:S(2)}) collective-permute-start(f32[2,128,1024]{2,1,0:T(8,128)S(1)} %get-tuple-element.64), channel_id=1, source_target_pairs={{1,0},{0,1},{3,2},{2,3},{5,4},{4,5},{7,6},{6,7},{9,8},{8,9},{11,10... | collective-permute-start | bytes 3145736 | tf_op jit(solution)/shard_map/ppermute | solution.py:504
  144.4 4.6 %copy-start.5 = (f32[2,128,1024]{2,1,0:T(8,128)}, f32[2,128,1024]{2,1,0:T(8,128)S(1)}, u32[]{:S(2)}) copy-start(f32[2,128,1024]{2,1,0:T(8,128)S(1)} %collective-permute-done.9.refs_1_.refs_5_.refs_3_) | copy-start | bytes 3145732
  144.4 1.0 copy-start.13
  144.4 1.4 copy-start.10
  145.8 3.4 %copy-start.8 = (f32[2,128,1024]{2,1,0:T(8,128)S(1)}, f32[2,128,1024]{2,1,0:T(8,128)}, u32[]{:S(2)}) copy-start(f32[2,128,1024]{2,1,0:T(8,128)} %copy-done.7) | copy-start | bytes 3145732
  149.0 3.4 %collective-permute-start.16 = (f32[2,128,1024]{2,1,0:T(8,128)S(1)}, f32[2,128,1024]{2,1,0:T(8,128)S(1)}, u32[]{:S(2)}, u32[]{:S(2)}) collective-permute-start(f32[2,128,1024]{2,1,0:T(8,128)S(1)} %get-tuple-element.72), channel_id=1, source_target_pairs={{2,0},{0,2},{6,4},{4,6},{10,8},{8,10},{14,12},{12,14},{18,16},{16,... | collective-permute-start | bytes 3145736 | tf_op jit(solution)/shard_map/ppermute | solution.py:510
  149.2 28.5 %collective-permute-start.8 = (f32[2,128,1024]{2,1,0:T(8,128)S(1)}, f32[2,128,1024]{2,1,0:T(8,128)S(1)}, u32[]{:S(2)}, u32[]{:S(2)}) collective-permute-start(f32[2,128,1024]{2,1,0:T(8,128)S(1)} %copy-done.8), channel_id=1, source_target_pairs={{8,0},{10,2},{12,4},{14,6},{16,8},{18,10},{20,12},{22,14},{24,16},... | collective-permute-start | bytes 3145736 | tf_op jit(solution)/shard_map/ppermute | solution.py:501
  149.7 28.1 %collective-permute-start.13 = (f32[2,128,1024]{2,1,0:T(8,128)S(1)}, f32[2,128,1024]{2,1,0:T(8,128)S(1)}, u32[]{:S(2)}, u32[]{:S(2)}) collective-permute-start(f32[2,128,1024]{2,1,0:T(8,128)S(1)} %get-tuple-element.68), channel_id=1, source_target_pairs={{4,0},{6,2},{0,4},{2,6},{12,8},{14,10},{8,12},{10,14},{20,16},{22,... | collective-permute-start | bytes 3145736 | tf_op jit(solution)/shard_map/ppermute | solution.py:507
  151.9 25.9 %collective-permute-start.14 = (f32[2,128,1024]{2,1,0:T(8,128)S(1)}, f32[2,128,1024]{2,1,0:T(8,128)S(1)}, u32[]{:S(2)}, u32[]{:S(2)}) collective-permute-start(f32[2,128,1024]{2,1,0:T(8,128)S(1)} %get-tuple-element.69), channel_id=1, source_target_pairs={{1,0},{0,1},{3,2},{2,3},{5,4},{4,5},{7,6},{6,7},{9,8},{8,9},{11,10... | collective-permute-start | bytes 3145736 | tf_op jit(solution)/shard_map/ppermute | solution.py:504
  152.4 1.0 copy-start.18
  177.7 4.5 %copy-start.6 = (f32[2,128,1024]{2,1,0:T(8,128)}, f32[2,128,1024]{2,1,0:T(8,128)S(1)}, u32[]{:S(2)}) copy-start(f32[2,128,1024]{2,1,0:T(8,128)S(1)} %collective-permute-done.8.refs_1_.refs_3_) | copy-start | bytes 3145732
  177.8 1.0 copy-start.16
  177.8 1.3 copy-start.17
  182.2 7.2 %collective-permute-start.20 = (f32[2,512,1024]{2,1,0:T(8,128)S(1)}, f32[2,512,1024]{2,1,0:T(8,128)S(1)}, u32[]{:S(2)}, u32[]{:S(2)}) collective-permute-start(f32[2,512,1024]{2,1,0:T(8,128)S(1)} %get-tuple-element.79), channel_id=1, source_target_pairs={{2,0},{0,2},{6,4},{4,6},{10,8},{8,10},{14,12},{12,14},{18,16},{16,... | collective-permute-start | bytes 12582920 | tf_op jit(solution)/shard_map/ppermute | solution.py:510
  182.3 25.6 %collective-permute-start.18 = (f32[2,128,1024]{2,1,0:T(8,128)S(1)}, f32[2,128,1024]{2,1,0:T(8,128)S(1)}, u32[]{:S(2)}, u32[]{:S(2)}) collective-permute-start(f32[2,128,1024]{2,1,0:T(8,128)S(1)} %get-tuple-element.76), channel_id=1, source_target_pairs={{1,0},{0,1},{3,2},{2,3},{5,4},{4,5},{7,6},{6,7},{9,8},{8,9},{11,10... | collective-permute-start | bytes 3145736 | tf_op jit(solution)/shard_map/ppermute | solution.py:504
  183.9 25.2 %collective-permute-start.19 = (f32[2,128,1024]{2,1,0:T(8,128)S(1)}, f32[2,128,1024]{2,1,0:T(8,128)S(1)}, u32[]{:S(2)}, u32[]{:S(2)}) collective-permute-start(f32[2,128,1024]{2,1,0:T(8,128)S(1)} %get-tuple-element.77), channel_id=1, source_target_pairs={{8,0},{10,2},{12,4},{14,6},{16,8},{18,10},{20,12},{22,14},{24,16},... | collective-permute-start | bytes 3145736 | tf_op jit(solution)/shard_map/ppermute | solution.py:501
  183.9 25.3 %collective-permute-start.17 = (f32[2,128,1024]{2,1,0:T(8,128)S(1)}, f32[2,128,1024]{2,1,0:T(8,128)}, u32[]{:S(2)}, u32[]{:S(2)}) collective-permute-start(f32[2,128,1024]{2,1,0:T(8,128)S(1)} %get-tuple-element.75), channel_id=1, source_target_pairs={{4,0},{6,2},{0,4},{2,6},{12,8},{14,10},{8,12},{10,14},{20,16},{22,... | collective-permute-start | bytes 3145736 | tf_op jit(solution)/shard_map/ppermute | solution.py:507
  189.4 2.1 copy-start.11
  207.9 2.3 copy-start.14
  209.1 1.0 copy-start.15
  213.1 7.2 %collective-permute-start.21 = (f32[2,512,1024]{2,1,0:T(8,128)S(1)}, f32[2,512,1024]{2,1,0:T(8,128)S(1)}, u32[]{:S(2)}, u32[]{:S(2)}) collective-permute-start(f32[2,512,1024]{2,1,0:T(8,128)S(1)} %get-tuple-element.82), channel_id=1, source_target_pairs={{2,0},{0,2},{6,4},{4,6},{10,8},{8,10},{14,12},{12,14},{18,16},{16,... | collective-permute-start | bytes 12582920 | tf_op jit(solution)/shard_map/ppermute | solution.py:510
  235.8 3.6 %collective-permute-start.22 = (f32[2]{0:T(128)S(1)}, f32[2]{0:T(128)S(1)}, u32[]{:S(2)}, u32[]{:S(2)}) collective-permute-start(f32[2]{0:T(128)S(1)} %broadcast_multiply_fusion), channel_id=1, source_target_pairs={{1,0},{0,1},{3,2},{2,3},{5,4},{4,5},{7,6},{6,7},{9,8},{8,9},{11,10... | collective-permute-start | bytes 32 | tf_op jit(solution)/shard_map/ppermute | solution.py:504

commit v3 on v2

--- a/solution.py
+++ b/solution.py
@@ -516,19 +516,24 @@
             return own, q * part
         return got["y", j], q * part
 
+    fresh = {"e": [("x", 0, 3)], "c": [("x", 1, 0), ("x", 1, 2), ("x", 1, 3)]}
+
+    def piece(user, *name):
+        return held(got[name]) if planes == 2 and groups == 2 and name in fresh.get(user, []) else got[name]
+
     def operand(kind, j, q):
         if kind == "z":
             return [(0, part, None, [here(j, q)])]
         if kind in ("zy", "xy", "e"):
-            return [(0, part, None, [(got["x" if kind == "e" else kind[0], 0, q], 0)])]
+            return [(0, part, None, [(piece(kind, "x" if kind == "e" else kind[0], 0, q), 0)])]
         if kind == "x":
             arrived = held(got["z", j, q]) if planes == 2 else got["z", j, q]
             return [(0, part, odd_at, [(arrived, 0), here(j, q)])]
         pieces = (2 * q, 2 * q + 1)
         pieces_x = pieces[:1] if kind == "d" else pieces
-        out = [(i * part, part, None, [(got["x", j, p], 0)]) for i, p in enumerate(pieces_x)]
+        out = [(i * part, part, None, [(piece(kind, "x", j, p), 0)]) for i, p in enumerate(pieces_x)]
         return out + [
-            ((i + len(pieces_x)) * part, part, lane_at, [(got["z", j, p], 0), here(j, p)]) for i, p in enumerate(pieces)
+            ((i + len(pieces_x)) * part, part, lane_at, [(piece(kind, "z", j, p), 0), here(j, p)]) for i, p in enumerate(pieces)
         ]
 
     def send(kind, j, q, x):
@@ -549,7 +554,7 @@
         else:
             swapped = got["d", j, group]
             cross4 = [(swapped, part), (swapped, 2 * part)]
-            cross2 = [(swapped, 0), (got["e", j, picks[1]], 0)]
+            cross2 = [(swapped, 0), (held(got["e", j, picks[1]]), 0)]
         return [
             cross4,
             [(got["x", j, q], 0) for q in picks],

time: 240 us -> 236 us (0.983)
  local copies, waits for them, and re-layouts: 9.95 us -> 6.33 us
    unnamed x40, local copies, waits for them, and re-layouts: 9.95 us -> 6.33 us
  transfers between devices with their start and end apart: 23 -> 23, of which waited for: 12 -> 11; matrix products, arithmetic and copies ran while one was open for 0% -> 0% of each run, Pallas kernels for 33% -> 34%
where the time goes in v3:
time: 236 us; the launch traced here: 235 us
  Pallas kernels  107 us (45%)
  waiting for transfers between devices  85.6 us (36%)
  starting transfers between devices  33 us (14%)
  local copies, waits for them, and re-layouts  6.33 us (3%)
    ppermute x7, waiting for transfers between devices, from_later(): return lax.ppermute(x, 'tm', [((i + 4) % steps, i) for i in range(steps)])  46 us
    pallas_call x2, Pallas kernels, both_call(): pl.pallas_call(functools.partial(both_kernel, places, len(sources), f is...  44.4 us
    pallas_call x2, Pallas kernels, more_call(): pl.pallas_call(functools.partial(more_kernel, places, len(sources), len(p...  27.2 us
    pallas_call x9, Pallas kernels, route(): pl.pallas_call(functools.partial(route_kernel, plan, int(chosen), len(arr...  24.2 us
    ppermute x5, waiting for transfers between devices, from_plane(): lax.ppermute(x, 'mode', [((i + shift) % planes, i) for i in range(planes)])  19.1 us
    ppermute x5, waiting for transfers between devices, across_cores(): return lax.ppermute(x, 'tm', [(i ^ 1, i) for i in range(steps)])  15.2 us
    ppermute x7, starting transfers between devices, from_later(): return lax.ppermute(x, 'tm', [((i + 4) % steps, i) for i in range(steps)])  13.5 us
    ppermute x6, starting transfers between devices, across_chips(): return lax.ppermute(x, 'tm', [(i ^ 2, i) for i in range(steps)])  11.9 us
  transfers between devices with their start and end apart: 23, of which 11 were waited for; matrix products, arithmetic and copies ran while one was open for 0% of the time, Pallas kernels for 34%

profile of v3, /device:TPU:0, one launch (start us, length us, event | category | flops | bytes accessed | tf_op | source)
XLA Modules:
  0.0 235.2 jit_solution(3022304176366987035)
XLA Ops:
  0.6 3.0 %collective-permute-start.3 = (f32[2,512,1024]{2,1,0:T(8,128)}, f32[2,512,1024]{2,1,0:T(8,128)}, u32[]{:S(2)}, u32[]{:S(2)}) collective-permute-start(f32[2,512,1024]{2,1,0:T(8,128)} %bitcast.15), channel_id=1, source_target_pairs={{1,0},{0,1},{3,2},{2,3},{5,4},{4,5},{7,6},{6,7},{9,8},{8,9},{11,10... | collective-permute-start | bytes 12582920 | tf_op jit(solution)/shard_map/ppermute | solution.py:504
  3.7 2.2 shard_map.42
  5.9 3.7 %collective-permute-start.1 = (f32[2,128,1024]{2,1,0:T(8,128)}, f32[2,128,1024]{2,1,0:T(8,128)S(1)}, u32[]{:S(2)}, u32[]{:S(2)}) collective-permute-start(f32[2,128,1024]{2,1,0:T(8,128)} %get-tuple-element.48), channel_id=1, source_target_pairs={{8,0},{10,2},{12,4},{14,6},{16,8},{18,10},{20,12},{22,14},{24,16},... | collective-permute-start | bytes 3145736 | tf_op jit(solution)/shard_map/ppermute | solution.py:501
  9.5 1.2 shard_map.43
  10.8 0.5 collective-permute-start
  11.3 0.6 pad_add_fusion.refs_0_.meta
  11.9 5.8 %shard_map.41 = (bf16[6,512,1024]{2,1,0:T(8,128)(2,1)}, f32[8,128]{1,0:T(8,128)}) custom-call(f32[2,512,1024]{2,1,0:T(8,128)} %bitcast.18), custom_call_target="tpu_custom_call" | custom-call | flops 1 | bytes 1 | tf_op jit(solution)/shard_map/pallas_call | solution.py:107
  17.6 15.8 %collective-permute-done.1.refs_1_.refs_7_.refs_3_ = f32[2,128,1024]{2,1,0:T(8,128)S(1)} collective-permute-done((f32[2,128,1024]{2,1,0:T(8,128)}, f32[2,128,1024]{2,1,0:T(8,128)S(1)}, u32[]{:S(2)}, u32[]{:S(2)}) %collective-permute-start.1) | collective-permute-done | bytes 1048608 | tf_op jit(solution)/shard_map/ppermute | solution.py:501
  33.4 2.0 shard_map.44
  35.5 4.2 %collective-permute-start.6 = (f32[2,128,1024]{2,1,0:T(8,128)S(1)}, f32[2,128,1024]{2,1,0:T(8,128)S(1)}, u32[]{:S(2)}, u32[]{:S(2)}) collective-permute-start(f32[2,128,1024]{2,1,0:T(8,128)S(1)} %get-tuple-element.55), channel_id=1, source_target_pairs={{8,0},{10,2},{12,4},{14,6},{16,8},{18,10},{20,12},{22,14},{24,16},... | collective-permute-start | bytes 3145736 | tf_op jit(solution)/shard_map/ppermute | solution.py:501
  39.7 1.7 collective-permute-start.4
  41.4 14.4 %collective-permute-done.refs_1_.refs_4_ = f32[2,128,1024]{2,1,0:T(8,128)S(1)} collective-permute-done((f32[2,128,1024]{2,1,0:T(8,128)S(1)}, f32[2,128,1024]{2,1,0:T(8,128)S(1)}, u32[]{:S(2)}, u32[]{:S(2)}) %collective-permute-start) | collective-permute-done | bytes 1048608 | tf_op jit(solution)/shard_map/ppermute | solution.py:501
  55.8 2.0 shard_map.45
  57.8 4.3 %collective-permute-start.2 = (f32[2,128,1024]{2,1,0:T(8,128)S(1)}, f32[2,128,1024]{2,1,0:T(8,128)S(1)}, u32[]{:S(2)}, u32[]{:S(2)}) collective-permute-start(f32[2,128,1024]{2,1,0:T(8,128)S(1)} %get-tuple-element.52), channel_id=1, source_target_pairs={{8,0},{10,2},{12,4},{14,6},{16,8},{18,10},{20,12},{22,14},{24,16},... | collective-permute-start | bytes 3145736 | tf_op jit(solution)/shard_map/ppermute | solution.py:501
  62.2 1.7 collective-permute-start.5
  63.9 14.4 %collective-permute-done.6.refs_1_.refs_9_.refs_4_ = f32[2,128,1024]{2,1,0:T(8,128)S(1)} collective-permute-done((f32[2,128,1024]{2,1,0:T(8,128)S(1)}, f32[2,128,1024]{2,1,0:T(8,128)S(1)}, u32[]{:S(2)}, u32[]{:S(2)}) %collective-permute-start.6) | collective-permute-done | bytes 1048608 | tf_op jit(solution)/shard_map/ppermute | solution.py:501
  78.3 0.8 shard_map.46
  79.1 2.6 %collective-permute-start.7 = (f32[2,128,1024]{2,1,0:T(8,128)S(1)}, f32[2,128,1024]{2,1,0:T(8,128)S(1)}, u32[]{:S(2)}, u32[]{:S(2)}) collective-permute-start(f32[2,128,1024]{2,1,0:T(8,128)S(1)} %get-tuple-element.57), channel_id=1, source_target_pairs={{4,0},{6,2},{0,4},{2,6},{12,8},{14,10},{8,12},{10,14},{20,16},{22,... | collective-permute-start | bytes 3145736 | tf_op jit(solution)/shard_map/ppermute | solution.py:507
  81.8 12.8 %collective-permute-done.3.x_ref.refs_3_.refs_2_.refs_4_ = f32[2,512,1024]{2,1,0:T(8,128)} collective-permute-done((f32[2,512,1024]{2,1,0:T(8,128)}, f32[2,512,1024]{2,1,0:T(8,128)}, u32[]{:S(2)}, u32[]{:S(2)}) %collective-permute-start.3) | collective-permute-done | bytes 4194336 | tf_op jit(solution)/shard_map/ppermute | solution.py:504
  94.6 5.8 %shard_map.47 = (bf16[6,512,1024]{2,1,0:T(8,128)(2,1)}, f32[8,128]{1,0:T(8,128)}) custom-call(f32[2,512,1024]{2,1,0:T(8,128)} %collective-permute-done.3.x_ref.refs_3_.refs_2_.refs_4_), custom_call_target="tpu_custom_call" | custom-call | flops 1 | bytes 1 | tf_op jit(solution)/shard_map/pallas_call | solution.py:107
  100.3 1.0 copy-done
  101.3 5.3 %collective-permute-done.7.refs_8_.refs_1_ = f32[2,128,1024]{2,1,0:T(8,128)S(1)} collective-permute-done((f32[2,128,1024]{2,1,0:T(8,128)S(1)}, f32[2,128,1024]{2,1,0:T(8,128)S(1)}, u32[]{:S(2)}, u32[]{:S(2)}) %collective-permute-start.7) | collective-permute-done | bytes 1048608 | tf_op jit(solution)/shard_map/ppermute | solution.py:507
  106.6 1.0 copy-done.18
  107.6 1.2 copy-done.1
  108.8 7.9 %shard_map.48 = (f32[2,128,1024]{2,1,0:T(8,128)S(1)}, f32[2,128,1024]{2,1,0:T(8,128)S(1)}, f32[2,128,1024]{2,1,0:T(8,128)S(1)}, f32[2,128,1024]{2,1,0:T(8,128)S(...) custom-call(s32[5]{0:T(128)} %pad_add_fusion.refs_0_.meta, f32[2,128,1024]{2,1,0:T(8,128)S(1)} %copy-done.1, ...), custom_call_target="tpu_custom_call" | custom-call | flops 1 | bytes 1 | tf_op jit(solution)/shard_map/pallas_call | solution.py:74
  117.7 2.0 collective-permute-start.10
  119.7 0.5 collective-permute-start.11
  120.2 4.2 %collective-permute-done.12.refs_0_ = f32[2,512,1024]{2,1,0:T(8,128)} collective-permute-done((f32[2,512,1024]{2,1,0:T(8,128)}, f32[2,512,1024]{2,1,0:T(8,128)}, u32[]{:S(2)}, u32[]{:S(2)}) %collective-permute-start.12) | collective-permute-done | bytes 4194336 | tf_op jit(solution)/shard_map/ppermute | solution.py:510
  124.3 20.1 %shard_map.49 = (f32[2,2,512,1024]{3,2,1,0:T(8,128)}, f32[2,2,256,1024]{3,2,1,0:T(8,128)}, f32[8,128]{1,0:T(8,128)}) custom-call(s32[5]{0:T(128)} %pad_add_fusion.refs_0_.meta, bf16[6,512,1024]{2,1,0:T(8,128)(2,1)} %get-tuple-element.45.own6, f32[2,512,1024]{2,1,0:T(8,128)} %collective-permute-done.12.refs_0_, ...), custom_call_target="tpu_custom_call" | custom-call | flops 1 | bytes 1 | tf_op jit(solution)/shard_map/pallas_call | solution.py:398
  144.5 1.0 copy-done.16
  145.5 2.6 %shard_map.50 = (f32[2,128,1024]{2,1,0:T(8,128)S(1)}, f32[2,128,1024]{2,1,0:T(8,128)S(1)}, f32[2,128,1024]{2,1,0:T(8,128)S(1)}, f32[2,128,1024]{2,1,0:T(8,128)S(...) custom-call(s32[5]{0:T(128)} %pad_add_fusion.refs_0_.meta, ...), custom_call_target="tpu_custom_call" | custom-call | flops 1 | bytes 1 | tf_op jit(solution)/shard_map/pallas_call | solution.py:74
  148.7 2.2 collective-permute-start.13
  151.4 24.3 %shard_map.51 = (f32[2,2,512,1024]{3,2,1,0:T(8,128)}, f32[2,2,256,1024]{3,2,1,0:T(8,128)}, f32[8,128]{1,0:T(8,128)}) custom-call(s32[5]{0:T(128)} %pad_add_fusion.refs_0_.meta, bf16[6,512,1024]{2,1,0:T(8,128)(2,1)} %get-tuple-element.45.own6, f32[2,384,1024]{2,1,0:T(8,128)} %collective-permute-done.15.refs_0_, ...), custom_call_target="tpu_custom_call", output_to_operand_aliasing={{0}: (9, {})} | custom-call | flops 1 | bytes 1 | tf_op jit(solution)/shard_map/pallas_call | solution.py:398
  175.8 3.0 %shard_map.52 = (f32[2,128,1024]{2,1,0:T(8,128)S(1)}, f32[2,512,1024]{2,1,0:T(8,128)S(1)}, f32[8,128]{1,0:T(8,128)}) custom-call(s32[5]{0:T(128)} %pad_add_fusion.refs_0_.meta, f32[2,128,1024]{2,1,0:T(8,128)S(1)} %collective-permute-done.8.refs_1_.refs_3_, f32[2,512,1024]{2,1,0:T(8,128)} %collective-permute-done.3.x_ref.refs_3_.refs_2_.refs_4_, ...), custom_call_target="tpu_custom_call" | custom-call | flops 1 | bytes 1 | tf_op jit(solution)/shard_map/pallas_call | solution.py:74
  178.9 1.6 collective-permute-start.18
  180.6 1.6 collective-permute-start.17
  182.2 3.9 %collective-permute-done.20.refs_0_ = f32[2,512,1024]{2,1,0:T(8,128)S(1)} collective-permute-done((f32[2,512,1024]{2,1,0:T(8,128)S(1)}, f32[2,512,1024]{2,1,0:T(8,128)S(1)}, u32[]{:S(2)}, u32[]{:S(2)}) %collective-permute-start.20) | collective-permute-done | bytes 4194336 | tf_op jit(solution)/shard_map/ppermute | solution.py:510
  186.1 2.1 copy-done.17
  188.1 12.5 %shard_map.53 = (f32[2,2,512,1024]{3,2,1,0:T(8,128)}, f32[8,128]{1,0:T(8,128)}) custom-call(s32[5]{0:T(128)} %pad_add_fusion.refs_0_.meta, bf16[6,512,1024]{2,1,0:T(8,128)(2,1)} %get-tuple-element.45.own6, f32[2,512,1024]{2,1,0:T(8,128)} %copy-done.17, f32[2,128,1024]{2,1,0:T(8,128)} %copy-done.10, ...), custom_call_target="tpu_custom_call", output_to_operand_aliasing={{0}: (7, {})} | custom-call | flops 1 | bytes 1 | tf_op jit(solution)/shard_map/pallas_call | solution.py:444
  200.6 3.9 %collective-permute-done.18.refs_2_ = f32[2,128,1024]{2,1,0:T(8,128)S(1)} collective-permute-done((f32[2,128,1024]{2,1,0:T(8,128)S(1)}, f32[2,128,1024]{2,1,0:T(8,128)S(1)}, u32[]{:S(2)}, u32[]{:S(2)}) %collective-permute-start.18) | collective-permute-done | bytes 1048608 | tf_op jit(solution)/shard_map/ppermute | solution.py:504
  204.5 1.4 collective-permute-done.19.refs_5_.refs_4_
  205.9 2.5 %shard_map.54 = (f32[2,512,1024]{2,1,0:T(8,128)S(1)}, f32[8,128]{1,0:T(8,128)}) custom-call(s32[5]{0:T(128)} %pad_add_fusion.refs_0_.meta, f32[2,128,1024]{2,1,0:T(8,128)S(1)} %collective-permute-done.17.refs_1_, f32[2,128,1024]{2,1,0:T(8,128)S(1)} %collective-permute-done.18.refs_2_, f32[2,128,1024]{2,1,0:T(8,128)} %copy-done.5, ...), custom_call_target="tpu_custom_call" | custom-call | flops 1 | bytes 1 | tf_op jit(solution)/shard_map/pallas_call | solution.py:74
  208.5 7.1 %collective-permute-done.21.refs_0_ = f32[2,512,1024]{2,1,0:T(8,128)S(1)} collective-permute-done((f32[2,512,1024]{2,1,0:T(8,128)S(1)}, f32[2,512,1024]{2,1,0:T(8,128)S(1)}, u32[]{:S(2)}, u32[]{:S(2)}) %collective-permute-start.21) | collective-permute-done | bytes 4194336 | tf_op jit(solution)/shard_map/ppermute | solution.py:510
  215.6 14.7 %shard_map.55 = (f32[2,2,512,1024]{3,2,1,0:T(8,128)}, f32[8,128]{1,0:T(8,128)}, f32[2,8,128]{2,1,0:T(8,128)}) custom-call(s32[5]{0:T(128)} %pad_add_fusion.refs_0_.meta, bf16[6,512,1024]{2,1,0:T(8,128)(2,1)} %get-tuple-element.45.own6, f32[2,512,1024]{2,1,0:T(8,128)S(1)} %collective-permute-done.21.refs_0_, ...), custom_call_target="tpu_custom_call", output_to_operand_aliasing={{0}: (7, {})} | custom-call | flops 1 | bytes 1 | tf_op jit(solution)/shard_map/pallas_call | solution.py:444
  230.3 0.8 reduce_sum.9
  231.1 1.1 collective-permute-start.22
  232.2 2.4 %collective-permute-done.22 = f32[2]{0:T(128)S(1)} collective-permute-done((f32[2]{0:T(128)S(1)}, f32[2]{0:T(128)S(1)}, u32[]{:S(2)}, u32[]{:S(2)}) %collective-permute-start.22) | collective-permute-done | bytes 40 | tf_op jit(solution)/shard_map/ppermute | solution.py:504
  234.6 0.5 add_bitcast_fusion
  (58 shorter events, 2.2 us)
Async XLA Ops:
  0.6 10.6 %copy-start.19 = (s32[1,2]{1,0:T(1,128)S(1)}, s32[1,2]{1,0:T(1,128)}, u32[]{:S(2)}) copy-start(s32[1,2]{1,0:T(1,128)} %param.3) | copy-start | bytes 28
  0.6 93.9 %collective-permute-start.3 = (f32[2,512,1024]{2,1,0:T(8,128)}, f32[2,512,1024]{2,1,0:T(8,128)}, u32[]{:S(2)}, u32[]{:S(2)}) collective-permute-start(f32[2,512,1024]{2,1,0:T(8,128)} %bitcast.15), channel_id=1, source_target_pairs={{1,0},{0,1},{3,2},{2,3},{5,4},{4,5},{7,6},{6,7},{9,8},{8,9},{11,10... | collective-permute-start | bytes 12582920 | tf_op jit(solution)/shard_map/ppermute | solution.py:504
  5.9 27.6 %collective-permute-start.1 = (f32[2,128,1024]{2,1,0:T(8,128)}, f32[2,128,1024]{2,1,0:T(8,128)S(1)}, u32[]{:S(2)}, u32[]{:S(2)}) collective-permute-start(f32[2,128,1024]{2,1,0:T(8,128)} %get-tuple-element.48), channel_id=1, source_target_pairs={{8,0},{10,2},{12,4},{14,6},{16,8},{18,10},{20,12},{22,14},{24,16},... | collective-permute-start | bytes 3145736 | tf_op jit(solution)/shard_map/ppermute | solution.py:501
  10.8 45.1 %collective-permute-start = (f32[2,128,1024]{2,1,0:T(8,128)S(1)}, f32[2,128,1024]{2,1,0:T(8,128)S(1)}, u32[]{:S(2)}, u32[]{:S(2)}) collective-permute-start(f32[2,128,1024]{2,1,0:T(8,128)S(1)} %get-tuple-element.47), channel_id=1, source_target_pairs={{8,0},{10,2},{12,4},{14,6},{16,8},{18,10},{20,12},{22,14},{24,16},... | collective-permute-start | bytes 3145736 | tf_op jit(solution)/shard_map/ppermute | solution.py:501
  33.4 24.4 %copy-start.2 = (f32[2,128,1024]{2,1,0:T(8,128)}, f32[2,128,1024]{2,1,0:T(8,128)S(1)}, u32[]{:S(2)}) copy-start(f32[2,128,1024]{2,1,0:T(8,128)S(1)} %collective-permute-done.1.refs_1_.refs_7_.refs_3_) | copy-start | bytes 3145732
  35.5 42.8 %collective-permute-start.6 = (f32[2,128,1024]{2,1,0:T(8,128)S(1)}, f32[2,128,1024]{2,1,0:T(8,128)S(1)}, u32[]{:S(2)}, u32[]{:S(2)}) collective-permute-start(f32[2,128,1024]{2,1,0:T(8,128)S(1)} %get-tuple-element.55), channel_id=1, source_target_pairs={{8,0},{10,2},{12,4},{14,6},{16,8},{18,10},{20,12},{22,14},{24,16},... | collective-permute-start | bytes 3145736 | tf_op jit(solution)/shard_map/ppermute | solution.py:501
  39.7 60.6 %collective-permute-start.4 = (f32[2,128,1024]{2,1,0:T(8,128)S(1)}, f32[2,128,1024]{2,1,0:T(8,128)}, u32[]{:S(2)}, u32[]{:S(2)}) collective-permute-start(f32[2,128,1024]{2,1,0:T(8,128)S(1)} %get-tuple-element.53), channel_id=1, source_target_pairs={{4,0},{6,2},{0,4},{2,6},{12,8},{14,10},{8,12},{10,14},{20,16},{22,... | collective-permute-start | bytes 3145736 | tf_op jit(solution)/shard_map/ppermute | solution.py:507
  55.8 23.3 %copy-start.3 = (f32[2,128,1024]{2,1,0:T(8,128)}, f32[2,128,1024]{2,1,0:T(8,128)S(1)}, u32[]{:S(2)}) copy-start(f32[2,128,1024]{2,1,0:T(8,128)S(1)} %collective-permute-done.refs_1_.refs_4_) | copy-start | bytes 3145732
  57.8 42.5 %collective-permute-start.2 = (f32[2,128,1024]{2,1,0:T(8,128)S(1)}, f32[2,128,1024]{2,1,0:T(8,128)S(1)}, u32[]{:S(2)}, u32[]{:S(2)}) collective-permute-start(f32[2,128,1024]{2,1,0:T(8,128)S(1)} %get-tuple-element.52), channel_id=1, source_target_pairs={{8,0},{10,2},{12,4},{14,6},{16,8},{18,10},{20,12},{22,14},{24,16},... | collective-permute-start | bytes 3145736 | tf_op jit(solution)/shard_map/ppermute | solution.py:501
  62.2 39.1 %collective-permute-start.5 = (f32[2,128,1024]{2,1,0:T(8,128)S(1)}, f32[2,128,1024]{2,1,0:T(8,128)S(1)}, u32[]{:S(2)}, u32[]{:S(2)}) collective-permute-start(f32[2,128,1024]{2,1,0:T(8,128)S(1)} %get-tuple-element.54), channel_id=1, source_target_pairs={{4,0},{6,2},{0,4},{2,6},{12,8},{14,10},{8,12},{10,14},{20,16},{22,... | collective-permute-start | bytes 3145736 | tf_op jit(solution)/shard_map/ppermute | solution.py:507
  78.3 22.0 %copy-start.4 = (f32[2,128,1024]{2,1,0:T(8,128)}, f32[2,128,1024]{2,1,0:T(8,128)S(1)}, u32[]{:S(2)}) copy-start(f32[2,128,1024]{2,1,0:T(8,128)S(1)} %collective-permute-done.6.refs_1_.refs_9_.refs_4_) | copy-start | bytes 3145732
  79.1 27.5 %collective-permute-start.7 = (f32[2,128,1024]{2,1,0:T(8,128)S(1)}, f32[2,128,1024]{2,1,0:T(8,128)S(1)}, u32[]{:S(2)}, u32[]{:S(2)}) collective-permute-start(f32[2,128,1024]{2,1,0:T(8,128)S(1)} %get-tuple-element.57), channel_id=1, source_target_pairs={{4,0},{6,2},{0,4},{2,6},{12,8},{14,10},{8,12},{10,14},{20,16},{22,... | collective-permute-start | bytes 3145736 | tf_op jit(solution)/shard_map/ppermute | solution.py:507
  100.3 1.0 copy-start
  101.3 5.3 %copy-start.15 = (f32[2,128,1024]{2,1,0:T(8,128)}, f32[2,128,1024]{2,1,0:T(8,128)S(1)}, u32[]{:S(2)}) copy-start(f32[2,128,1024]{2,1,0:T(8,128)S(1)} %collective-permute-done.5.refs_6_.refs_2_.refs_3_) | copy-start | bytes 3145732
  106.6 1.0 copy-start.18
  107.6 1.2 copy-start.1
  116.8 27.7 %copy-start.11 = (f32[2,128,1024]{2,1,0:T(8,128)}, f32[2,128,1024]{2,1,0:T(8,128)S(1)}, u32[]{:S(2)}) copy-start(f32[2,128,1024]{2,1,0:T(8,128)S(1)} %get-tuple-element.60) | copy-start | bytes 3145732
  116.8 7.6 %collective-permute-start.12 = (f32[2,512,1024]{2,1,0:T(8,128)}, f32[2,512,1024]{2,1,0:T(8,128)}, u32[]{:S(2)}, u32[]{:S(2)}) collective-permute-start(f32[2,512,1024]{2,1,0:T(8,128)} %get-tuple-element.65), channel_id=1, source_target_pairs={{2,0},{0,2},{6,4},{4,6},{10,8},{8,10},{14,12},{12,14},{18,16},{16,... | collective-permute-start | bytes 12582920 | tf_op jit(solution)/shard_map/ppermute | solution.py:510
  116.8 34.5 %collective-permute-start.15 = (f32[2,384,1024]{2,1,0:T(8,128)}, f32[2,384,1024]{2,1,0:T(8,128)}, u32[]{:S(2)}, u32[]{:S(2)}) collective-permute-start(f32[2,384,1024]{2,1,0:T(8,128)} %get-tuple-element.71), channel_id=1, source_target_pairs={{2,0},{0,2},{6,4},{4,6},{10,8},{8,10},{14,12},{12,14},{18,16},{16,... | collective-permute-start | bytes 9437192 | tf_op jit(solution)/shard_map/ppermute | solution.py:510
  117.3 27.1 %collective-permute-start.9 = (f32[2,128,1024]{2,1,0:T(8,128)S(1)}, f32[2,128,1024]{2,1,0:T(8,128)S(1)}, u32[]{:S(2)}, u32[]{:S(2)}) collective-permute-start(f32[2,128,1024]{2,1,0:T(8,128)S(1)} %get-tuple-element.61), channel_id=1, source_target_pairs={{8,0},{10,2},{12,4},{14,6},{16,8},{18,10},{20,12},{22,14},{24,16},... | collective-permute-start | bytes 3145736 | tf_op jit(solution)/shard_map/ppermute | solution.py:501
  117.7 26.8 %collective-permute-start.10 = (f32[2,128,1024]{2,1,0:T(8,128)S(1)}, f32[2,128,1024]{2,1,0:T(8,128)S(1)}, u32[]{:S(2)}, u32[]{:S(2)}) collective-permute-start(f32[2,128,1024]{2,1,0:T(8,128)S(1)} %get-tuple-element.62), channel_id=1, source_target_pairs={{4,0},{6,2},{0,4},{2,6},{12,8},{14,10},{8,12},{10,14},{20,16},{22,... | collective-permute-start | bytes 3145736 | tf_op jit(solution)/shard_map/ppermute | solution.py:507
  119.7 24.8 %collective-permute-start.11 = (f32[2,128,1024]{2,1,0:T(8,128)S(1)}, f32[2,128,1024]{2,1,0:T(8,128)S(1)}, u32[]{:S(2)}, u32[]{:S(2)}) collective-permute-start(f32[2,128,1024]{2,1,0:T(8,128)S(1)} %get-tuple-element.64), channel_id=1, source_target_pairs={{1,0},{0,1},{3,2},{2,3},{5,4},{4,5},{7,6},{6,7},{9,8},{8,9},{11,10... | collective-permute-start | bytes 3145736 | tf_op jit(solution)/shard_map/ppermute | solution.py:504
  144.4 3.7 %copy-start.6 = (f32[2,128,1024]{2,1,0:T(8,128)}, f32[2,128,1024]{2,1,0:T(8,128)S(1)}, u32[]{:S(2)}) copy-start(f32[2,128,1024]{2,1,0:T(8,128)S(1)} %collective-permute-done.9.refs_1_.refs_5_.refs_3_) | copy-start | bytes 3145732
  144.5 3.7 %copy-start.7 = (f32[2,128,1024]{2,1,0:T(8,128)}, f32[2,128,1024]{2,1,0:T(8,128)S(1)}, u32[]{:S(2)}) copy-start(f32[2,128,1024]{2,1,0:T(8,128)S(1)} %collective-permute-done.10.refs_4_.refs_5_.refs_2_) | copy-start | bytes 3145732
  144.5 1.0 copy-start.16
  145.5 2.7 %copy-start.12 = (f32[2,128,1024]{2,1,0:T(8,128)S(1)}, f32[2,128,1024]{2,1,0:T(8,128)}, u32[]{:S(2)}) copy-start(f32[2,128,1024]{2,1,0:T(8,128)} %copy-done.11) | copy-start | bytes 3145732
  148.1 27.6 %copy-start.13 = (f32[2,128,1024]{2,1,0:T(8,128)}, f32[2,128,1024]{2,1,0:T(8,128)S(1)}, u32[]{:S(2)}) copy-start(f32[2,128,1024]{2,1,0:T(8,128)S(1)} %get-tuple-element.76) | copy-start | bytes 3145732
  148.1 3.2 %collective-permute-start.16 = (f32[2,128,1024]{2,1,0:T(8,128)S(1)}, f32[2,128,1024]{2,1,0:T(8,128)S(1)}, u32[]{:S(2)}, u32[]{:S(2)}) collective-permute-start(f32[2,128,1024]{2,1,0:T(8,128)S(1)} %get-tuple-element.72), channel_id=1, source_target_pairs={{2,0},{0,2},{6,4},{4,6},{10,8},{8,10},{14,12},{12,14},{18,16},{16,... | collective-permute-start | bytes 3145736 | tf_op jit(solution)/shard_map/ppermute | solution.py:510
  148.3 27.5 %collective-permute-start.8 = (f32[2,128,1024]{2,1,0:T(8,128)S(1)}, f32[2,128,1024]{2,1,0:T(8,128)S(1)}, u32[]{:S(2)}, u32[]{:S(2)}) collective-permute-start(f32[2,128,1024]{2,1,0:T(8,128)S(1)} %copy-done.12), channel_id=1, source_target_pairs={{8,0},{10,2},{12,4},{14,6},{16,8},{18,10},{20,12},{22,14},{24,16},... | collective-permute-start | bytes 3145736 | tf_op jit(solution)/shard_map/ppermute | solution.py:501
  148.7 27.1 %collective-permute-start.13 = (f32[2,128,1024]{2,1,0:T(8,128)S(1)}, f32[2,128,1024]{2,1,0:T(8,128)S(1)}, u32[]{:S(2)}, u32[]{:S(2)}) collective-permute-start(f32[2,128,1024]{2,1,0:T(8,128)S(1)} %get-tuple-element.68), channel_id=1, source_target_pairs={{4,0},{6,2},{0,4},{2,6},{12,8},{14,10},{8,12},{10,14},{20,16},{22,... | collective-permute-start | bytes 3145736 | tf_op jit(solution)/shard_map/ppermute | solution.py:507
  150.9 24.9 %collective-permute-start.14 = (f32[2,128,1024]{2,1,0:T(8,128)S(1)}, f32[2,128,1024]{2,1,0:T(8,128)}, u32[]{:S(2)}, u32[]{:S(2)}) collective-permute-start(f32[2,128,1024]{2,1,0:T(8,128)S(1)} %get-tuple-element.69), channel_id=1, source_target_pairs={{1,0},{0,1},{3,2},{2,3},{5,4},{4,5},{7,6},{6,7},{9,8},{8,9},{11,10... | collective-permute-start | bytes 3145736 | tf_op jit(solution)/shard_map/ppermute | solution.py:504
  175.7 3.1 %copy-start.5 = (f32[2,128,1024]{2,1,0:T(8,128)}, f32[2,128,1024]{2,1,0:T(8,128)S(1)}, u32[]{:S(2)}) copy-start(f32[2,128,1024]{2,1,0:T(8,128)S(1)} %collective-permute-done.8.refs_1_.refs_3_) | copy-start | bytes 3145732
  175.8 3.1 %copy-start.10 = (f32[2,128,1024]{2,1,0:T(8,128)}, f32[2,128,1024]{2,1,0:T(8,128)S(1)}, u32[]{:S(2)}) copy-start(f32[2,128,1024]{2,1,0:T(8,128)S(1)} %collective-permute-done.13.refs_3_.refs_1_) | copy-start | bytes 3145732
  175.8 3.1 %copy-start.14 = (f32[2,128,1024]{2,1,0:T(8,128)S(1)}, f32[2,128,1024]{2,1,0:T(8,128)}, u32[]{:S(2)}) copy-start(f32[2,128,1024]{2,1,0:T(8,128)} %copy-done.13) | copy-start | bytes 3145732
  178.8 7.2 %collective-permute-start.20 = (f32[2,512,1024]{2,1,0:T(8,128)S(1)}, f32[2,512,1024]{2,1,0:T(8,128)S(1)}, u32[]{:S(2)}, u32[]{:S(2)}) collective-permute-start(f32[2,512,1024]{2,1,0:T(8,128)S(1)} %get-tuple-element.79), channel_id=1, source_target_pairs={{2,0},{0,2},{6,4},{4,6},{10,8},{8,10},{14,12},{12,14},{18,16},{16,... | collective-permute-start | bytes 12582920 | tf_op jit(solution)/shard_map/ppermute | solution.py:510
  178.9 25.6 %collective-permute-start.18 = (f32[2,128,1024]{2,1,0:T(8,128)S(1)}, f32[2,128,1024]{2,1,0:T(8,128)S(1)}, u32[]{:S(2)}, u32[]{:S(2)}) collective-permute-start(f32[2,128,1024]{2,1,0:T(8,128)S(1)} %copy-done.14), channel_id=1, source_target_pairs={{1,0},{0,1},{3,2},{2,3},{5,4},{4,5},{7,6},{6,7},{9,8},{8,9},{11,10... | collective-permute-start | bytes 3145736 | tf_op jit(solution)/shard_map/ppermute | solution.py:504
  180.6 25.3 %collective-permute-start.19 = (f32[2,128,1024]{2,1,0:T(8,128)S(1)}, f32[2,128,1024]{2,1,0:T(8,128)}, u32[]{:S(2)}, u32[]{:S(2)}) collective-permute-start(f32[2,128,1024]{2,1,0:T(8,128)S(1)} %get-tuple-element.77), channel_id=1, source_target_pairs={{8,0},{10,2},{12,4},{14,6},{16,8},{18,10},{20,12},{22,14},{24,16},... | collective-permute-start | bytes 3145736 | tf_op jit(solution)/shard_map/ppermute | solution.py:501
  180.6 25.3 %collective-permute-start.17 = (f32[2,128,1024]{2,1,0:T(8,128)S(1)}, f32[2,128,1024]{2,1,0:T(8,128)S(1)}, u32[]{:S(2)}, u32[]{:S(2)}) collective-permute-start(f32[2,128,1024]{2,1,0:T(8,128)S(1)} %get-tuple-element.75), channel_id=1, source_target_pairs={{4,0},{6,2},{0,4},{2,6},{12,8},{14,10},{8,12},{10,14},{20,16},{22,... | collective-permute-start | bytes 3145736 | tf_op jit(solution)/shard_map/ppermute | solution.py:507
  186.1 2.1 copy-start.17
  204.5 3.9 %copy-start.8 = (f32[2,128,1024]{2,1,0:T(8,128)}, f32[2,128,1024]{2,1,0:T(8,128)S(1)}, u32[]{:S(2)}) copy-start(f32[2,128,1024]{2,1,0:T(8,128)S(1)} %collective-permute-done.18.refs_2_) | copy-start | bytes 3145732
  205.9 2.5 %copy-start.9 = (f32[2,128,1024]{2,1,0:T(8,128)}, f32[2,128,1024]{2,1,0:T(8,128)S(1)}, u32[]{:S(2)}) copy-start(f32[2,128,1024]{2,1,0:T(8,128)S(1)} %collective-permute-done.17.refs_1_) | copy-start | bytes 3145732
  208.4 7.2 %collective-permute-start.21 = (f32[2,512,1024]{2,1,0:T(8,128)S(1)}, f32[2,512,1024]{2,1,0:T(8,128)S(1)}, u32[]{:S(2)}, u32[]{:S(2)}) collective-permute-start(f32[2,512,1024]{2,1,0:T(8,128)S(1)} %get-tuple-element.82), channel_id=1, source_target_pairs={{2,0},{0,2},{6,4},{4,6},{10,8},{8,10},{14,12},{12,14},{18,16},{16,... | collective-permute-start | bytes 12582920 | tf_op jit(solution)/shard_map/ppermute | solution.py:510
  231.1 3.6 %collective-permute-start.22 = (f32[2]{0:T(128)S(1)}, f32[2]{0:T(128)S(1)}, u32[]{:S(2)}, u32[]{:S(2)}) collective-permute-start(f32[2]{0:T(128)S(1)} %broadcast_multiply_fusion), channel_id=1, source_target_pairs={{1,0},{0,1},{3,2},{2,3},{5,4},{4,5},{7,6},{6,7},{9,8},{8,9},{11,10... | collective-permute-start | bytes 32 | tf_op jit(solution)/shard_map/ppermute | solution.py:504

commit v4 on v3

--- a/solution.py
+++ b/solution.py
@@ -13,7 +13,7 @@
 ROUTE_LIMIT = 54 * 1024 * 1024
 TILE = 512
 SPLIT_TILE = 256
-CHUNKS = 4
+CHUNKS = 2
 GATE = pl.CostEstimate(flops=1, bytes_accessed=1, transcendentals=0)
 SMALL = pl.CostEstimate(flops=1, bytes_accessed=1, transcendentals=0)
 TOKEN = jax.ShapeDtypeStruct((8, 128), F32)
@@ -571,7 +571,8 @@
         tasks, after = [], list(written[-1:])
         for kind, other, q in step:
             tasks += [(kind, j, q) for j in (range(1, planes) if other else [0])]
-        after += [got[kind, j, q] for kind, other, q in there for j in (range(1, planes) if other else [0])]
+        waited = [got[kind, j, q] for kind, other, q in there for j in (range(1, planes) if other else [0])]
+        after += [held(x) for x in waited] if planes == 2 else waited
         for kind, g in work:
             if kind == "own":
                 own6, done = split_block(own)

time: 236 us -> 235 us (level)
    unnamed x40 -> x44, local copies, waits for them, and re-layouts: 6.33 us -> 5.17 us
  transfers between devices with their start and end apart: 23 -> 23, of which waited for: 11 -> 12; matrix products, arithmetic and copies ran while one was open for 0% -> 0% of each run, Pallas kernels for 34% -> 34%
where the time goes in v4:
time: 235 us; the launch traced here: 234 us
  Pallas kernels  106 us (45%)
  waiting for transfers between devices  86.2 us (37%)
  starting transfers between devices  33.5 us (14%)
  local copies, waits for them, and re-layouts  5.17 us (2%)
    ppermute x7, waiting for transfers between devices, from_later(): return lax.ppermute(x, 'tm', [((i + 4) % steps, i) for i in range(steps)])  46.1 us
    pallas_call x2, Pallas kernels, both_call(): pl.pallas_call(functools.partial(both_kernel, places, len(sources), f is...  43.6 us
    pallas_call x2, Pallas kernels, more_call(): pl.pallas_call(functools.partial(more_kernel, places, len(sources), len(p...  26.9 us
    pallas_call x9, Pallas kernels, route(): pl.pallas_call(functools.partial(route_kernel, plan, int(chosen), len(arr...  24.1 us
    ppermute x5, waiting for transfers between devices, from_plane(): lax.ppermute(x, 'mode', [((i + shift) % planes, i) for i in range(planes)])  19.9 us
    ppermute x5, waiting for transfers between devices, across_cores(): return lax.ppermute(x, 'tm', [(i ^ 1, i) for i in range(steps)])  15 us
    ppermute x7, starting transfers between devices, from_later(): return lax.ppermute(x, 'tm', [((i + 4) % steps, i) for i in range(steps)])  14 us
    ppermute x6, starting transfers between devices, across_chips(): return lax.ppermute(x, 'tm', [(i ^ 2, i) for i in range(steps)])  11.9 us
  transfers between devices with their start and end apart: 23, of which 12 were waited for; matrix products, arithmetic and copies ran while one was open for 0% of the time, Pallas kernels for 34%

profile of v4, /device:TPU:0, one launch (start us, length us, event | category | flops | bytes accessed | tf_op | source)
XLA Modules:
  0.0 234.1 jit_solution(18288311092841580064)
XLA Ops:
  0.6 3.0 %collective-permute-start.3 = (f32[2,512,1024]{2,1,0:T(8,128)}, f32[2,512,1024]{2,1,0:T(8,128)}, u32[]{:S(2)}, u32[]{:S(2)}) collective-permute-start(f32[2,512,1024]{2,1,0:T(8,128)} %bitcast.15), channel_id=1, source_target_pairs={{1,0},{0,1},{3,2},{2,3},{5,4},{4,5},{7,6},{6,7},{9,8},{8,9},{11,10... | collective-permute-start | bytes 12582920 | tf_op jit(solution)/shard_map/ppermute | solution.py:504
  3.7 2.2 shard_map.42
  5.9 3.7 %collective-permute-start.1 = (f32[2,128,1024]{2,1,0:T(8,128)}, f32[2,128,1024]{2,1,0:T(8,128)S(1)}, u32[]{:S(2)}, u32[]{:S(2)}) collective-permute-start(f32[2,128,1024]{2,1,0:T(8,128)} %get-tuple-element.48), channel_id=1, source_target_pairs={{8,0},{10,2},{12,4},{14,6},{16,8},{18,10},{20,12},{22,14},{24,16},... | collective-permute-start | bytes 3145736 | tf_op jit(solution)/shard_map/ppermute | solution.py:501
  9.5 1.2 shard_map.43
  11.3 0.7 pad_add_fusion.refs_0_.meta
  11.9 5.8 %shard_map.41 = (bf16[6,512,1024]{2,1,0:T(8,128)(2,1)}, f32[8,128]{1,0:T(8,128)}) custom-call(f32[2,512,1024]{2,1,0:T(8,128)} %bitcast.18), custom_call_target="tpu_custom_call" | custom-call | flops 1 | bytes 1 | tf_op jit(solution)/shard_map/pallas_call | solution.py:107
  17.7 15.7 %collective-permute-done.1.refs_1_.refs_7_.refs_3_ = f32[2,128,1024]{2,1,0:T(8,128)S(1)} collective-permute-done((f32[2,128,1024]{2,1,0:T(8,128)}, f32[2,128,1024]{2,1,0:T(8,128)S(1)}, u32[]{:S(2)}, u32[]{:S(2)}) %collective-permute-start.1) | collective-permute-done | bytes 1048608 | tf_op jit(solution)/shard_map/ppermute | solution.py:501
  33.4 2.0 shard_map.44
  35.4 4.2 %collective-permute-start.6 = (f32[2,128,1024]{2,1,0:T(8,128)S(1)}, f32[2,128,1024]{2,1,0:T(8,128)S(1)}, u32[]{:S(2)}, u32[]{:S(2)}) collective-permute-start(f32[2,128,1024]{2,1,0:T(8,128)S(1)} %get-tuple-element.55), channel_id=1, source_target_pairs={{8,0},{10,2},{12,4},{14,6},{16,8},{18,10},{20,12},{22,14},{24,16},... | collective-permute-start | bytes 3145736 | tf_op jit(solution)/shard_map/ppermute | solution.py:501
  39.7 1.7 collective-permute-start.4
  41.4 14.4 %collective-permute-done.refs_1_.refs_4_ = f32[2,128,1024]{2,1,0:T(8,128)S(1)} collective-permute-done((f32[2,128,1024]{2,1,0:T(8,128)S(1)}, f32[2,128,1024]{2,1,0:T(8,128)S(1)}, u32[]{:S(2)}, u32[]{:S(2)}) %collective-permute-start) | collective-permute-done | bytes 1048608 | tf_op jit(solution)/shard_map/ppermute | solution.py:501
  55.8 2.0 shard_map.45
  57.8 4.3 %collective-permute-start.2 = (f32[2,128,1024]{2,1,0:T(8,128)S(1)}, f32[2,128,1024]{2,1,0:T(8,128)S(1)}, u32[]{:S(2)}, u32[]{:S(2)}) collective-permute-start(f32[2,128,1024]{2,1,0:T(8,128)S(1)} %get-tuple-element.52), channel_id=1, source_target_pairs={{8,0},{10,2},{12,4},{14,6},{16,8},{18,10},{20,12},{22,14},{24,16},... | collective-permute-start | bytes 3145736 | tf_op jit(solution)/shard_map/ppermute | solution.py:501
  62.1 1.7 collective-permute-start.5
  63.9 14.4 %collective-permute-done.6.refs_1_.refs_9_.refs_4_ = f32[2,128,1024]{2,1,0:T(8,128)S(1)} collective-permute-done((f32[2,128,1024]{2,1,0:T(8,128)S(1)}, f32[2,128,1024]{2,1,0:T(8,128)S(1)}, u32[]{:S(2)}, u32[]{:S(2)}) %collective-permute-start.6) | collective-permute-done | bytes 1048608 | tf_op jit(solution)/shard_map/ppermute | solution.py:501
  78.3 0.8 shard_map.46
  79.1 2.7 %collective-permute-start.7 = (f32[2,128,1024]{2,1,0:T(8,128)S(1)}, f32[2,128,1024]{2,1,0:T(8,128)S(1)}, u32[]{:S(2)}, u32[]{:S(2)}) collective-permute-start(f32[2,128,1024]{2,1,0:T(8,128)S(1)} %get-tuple-element.57), channel_id=1, source_target_pairs={{4,0},{6,2},{0,4},{2,6},{12,8},{14,10},{8,12},{10,14},{20,16},{22,... | collective-permute-start | bytes 3145736 | tf_op jit(solution)/shard_map/ppermute | solution.py:507
  81.7 12.8 %collective-permute-done.3.x_ref.refs_3_.refs_2_.refs_4_ = f32[2,512,1024]{2,1,0:T(8,128)} collective-permute-done((f32[2,512,1024]{2,1,0:T(8,128)}, f32[2,512,1024]{2,1,0:T(8,128)}, u32[]{:S(2)}, u32[]{:S(2)}) %collective-permute-start.3) | collective-permute-done | bytes 4194336 | tf_op jit(solution)/shard_map/ppermute | solution.py:504
  94.6 5.8 %shard_map.47 = (bf16[6,512,1024]{2,1,0:T(8,128)(2,1)}, f32[8,128]{1,0:T(8,128)}) custom-call(f32[2,512,1024]{2,1,0:T(8,128)} %collective-permute-done.3.x_ref.refs_3_.refs_2_.refs_4_), custom_call_target="tpu_custom_call" | custom-call | flops 1 | bytes 1 | tf_op jit(solution)/shard_map/pallas_call | solution.py:107
  100.4 1.0 copy-done
  101.4 5.2 %collective-permute-done.7.refs_8_.refs_1_ = f32[2,128,1024]{2,1,0:T(8,128)S(1)} collective-permute-done((f32[2,128,1024]{2,1,0:T(8,128)S(1)}, f32[2,128,1024]{2,1,0:T(8,128)S(1)}, u32[]{:S(2)}, u32[]{:S(2)}) %collective-permute-start.7) | collective-permute-done | bytes 1048608 | tf_op jit(solution)/shard_map/ppermute | solution.py:507
  106.6 1.0 copy-done.20
  107.5 1.2 copy-done.1
  108.8 7.7 %shard_map.48 = (f32[2,128,1024]{2,1,0:T(8,128)S(1)}, f32[2,128,1024]{2,1,0:T(8,128)S(1)}, f32[2,128,1024]{2,1,0:T(8,128)S(1)}, f32[2,128,1024]{2,1,0:T(8,128)S(...) custom-call(s32[5]{0:T(128)} %pad_add_fusion.refs_0_.meta, f32[2,128,1024]{2,1,0:T(8,128)S(1)} %copy-done.1, ...), custom_call_target="tpu_custom_call" | custom-call | flops 1 | bytes 1 | tf_op jit(solution)/shard_map/pallas_call | solution.py:74
  117.4 2.0 collective-permute-start.10
  119.8 4.2 %collective-permute-done.12.refs_0_ = f32[2,512,1024]{2,1,0:T(8,128)} collective-permute-done((f32[2,512,1024]{2,1,0:T(8,128)}, f32[2,512,1024]{2,1,0:T(8,128)}, u32[]{:S(2)}, u32[]{:S(2)}) %collective-permute-start.12) | collective-permute-done | bytes 4194336 | tf_op jit(solution)/shard_map/ppermute | solution.py:510
  124.0 20.0 %shard_map.49 = (f32[2,2,512,1024]{3,2,1,0:T(8,128)}, f32[2,2,256,1024]{3,2,1,0:T(8,128)}, f32[8,128]{1,0:T(8,128)}) custom-call(s32[5]{0:T(128)} %pad_add_fusion.refs_0_.meta, bf16[6,512,1024]{2,1,0:T(8,128)(2,1)} %get-tuple-element.45.own6, f32[2,512,1024]{2,1,0:T(8,128)} %collective-permute-done.12.refs_0_, ...), custom_call_target="tpu_custom_call" | custom-call | flops 1 | bytes 1 | tf_op jit(solution)/shard_map/pallas_call | solution.py:398
  144.1 3.0 %shard_map.50 = (f32[2,128,1024]{2,1,0:T(8,128)S(1)}, f32[2,128,1024]{2,1,0:T(8,128)S(1)}, f32[2,128,1024]{2,1,0:T(8,128)S(1)}, f32[2,128,1024]{2,1,0:T(8,128)S(...) custom-call(s32[5]{0:T(128)} %pad_add_fusion.refs_0_.meta, ...), custom_call_target="tpu_custom_call" | custom-call | flops 1 | bytes 1 | tf_op jit(solution)/shard_map/pallas_call | solution.py:74
  147.8 2.2 collective-permute-start.13
  150.0 0.6 collective-permute-start.14
  150.6 23.6 %shard_map.51 = (f32[2,2,512,1024]{3,2,1,0:T(8,128)}, f32[2,2,256,1024]{3,2,1,0:T(8,128)}, f32[8,128]{1,0:T(8,128)}) custom-call(s32[5]{0:T(128)} %pad_add_fusion.refs_0_.meta, bf16[6,512,1024]{2,1,0:T(8,128)(2,1)} %get-tuple-element.45.own6, f32[2,384,1024]{2,1,0:T(8,128)} %collective-permute-done.15.refs_0_, ...), custom_call_target="tpu_custom_call", output_to_operand_aliasing={{0}: (9, {})} | custom-call | flops 1 | bytes 1 | tf_op jit(solution)/shard_map/pallas_call | solution.py:398
  174.3 0.8 collective-permute-done.14.refs_4_.refs_2_
  175.1 2.9 %shard_map.52 = (f32[2,128,1024]{2,1,0:T(8,128)S(1)}, f32[2,512,1024]{2,1,0:T(8,128)S(1)}, f32[8,128]{1,0:T(8,128)}) custom-call(s32[5]{0:T(128)} %pad_add_fusion.refs_0_.meta, f32[2,128,1024]{2,1,0:T(8,128)S(1)} %collective-permute-done.8.refs_1_.refs_3_, f32[2,512,1024]{2,1,0:T(8,128)} %collective-permute-done.3.x_ref.refs_3_.refs_2_.refs_4_, ...), custom_call_target="tpu_custom_call" | custom-call | flops 1 | bytes 1 | tf_op jit(solution)/shard_map/pallas_call | solution.py:74
  178.1 1.3 collective-permute-start.18
  179.3 0.6 collective-permute-start.19
  179.9 1.6 collective-permute-start.17
  181.5 3.7 %collective-permute-done.20.refs_0_ = f32[2,512,1024]{2,1,0:T(8,128)S(1)} collective-permute-done((f32[2,512,1024]{2,1,0:T(8,128)S(1)}, f32[2,512,1024]{2,1,0:T(8,128)S(1)}, u32[]{:S(2)}, u32[]{:S(2)}) %collective-permute-start.20) | collective-permute-done | bytes 4194336 | tf_op jit(solution)/shard_map/ppermute | solution.py:510
  185.2 2.0 copy-done.19
  187.1 12.6 %shard_map.53 = (f32[2,2,512,1024]{3,2,1,0:T(8,128)}, f32[8,128]{1,0:T(8,128)}) custom-call(s32[5]{0:T(128)} %pad_add_fusion.refs_0_.meta, bf16[6,512,1024]{2,1,0:T(8,128)(2,1)} %get-tuple-element.45.own6, f32[2,512,1024]{2,1,0:T(8,128)} %copy-done.19, f32[2,128,1024]{2,1,0:T(8,128)} %copy-done.11, ...), custom_call_target="tpu_custom_call", output_to_operand_aliasing={{0}: (7, {})} | custom-call | flops 1 | bytes 1 | tf_op jit(solution)/shard_map/pallas_call | solution.py:444
  199.7 3.9 %collective-permute-done.18.refs_2_ = f32[2,128,1024]{2,1,0:T(8,128)S(1)} collective-permute-done((f32[2,128,1024]{2,1,0:T(8,128)S(1)}, f32[2,128,1024]{2,1,0:T(8,128)S(1)}, u32[]{:S(2)}, u32[]{:S(2)}) %collective-permute-start.18) | collective-permute-done | bytes 1048608 | tf_op jit(solution)/shard_map/ppermute | solution.py:504
  203.6 1.6 collective-permute-done.19.refs_5_.refs_4_
  205.2 2.4 %shard_map.54 = (f32[2,512,1024]{2,1,0:T(8,128)S(1)}, f32[8,128]{1,0:T(8,128)}) custom-call(s32[5]{0:T(128)} %pad_add_fusion.refs_0_.meta, f32[2,128,1024]{2,1,0:T(8,128)S(1)} %collective-permute-done.17.refs_1_, f32[2,128,1024]{2,1,0:T(8,128)S(1)} %collective-permute-done.18.refs_2_, f32[2,128,1024]{2,1,0:T(8,128)} %copy-done.5, ...), custom_call_target="tpu_custom_call" | custom-call | flops 1 | bytes 1 | tf_op jit(solution)/shard_map/pallas_call | solution.py:74
  207.7 7.1 %collective-permute-done.21.refs_0_ = f32[2,512,1024]{2,1,0:T(8,128)S(1)} collective-permute-done((f32[2,512,1024]{2,1,0:T(8,128)S(1)}, f32[2,512,1024]{2,1,0:T(8,128)S(1)}, u32[]{:S(2)}, u32[]{:S(2)}) %collective-permute-start.21) | collective-permute-done | bytes 4194336 | tf_op jit(solution)/shard_map/ppermute | solution.py:510
  214.9 14.4 %shard_map.55 = (f32[2,2,512,1024]{3,2,1,0:T(8,128)}, f32[8,128]{1,0:T(8,128)}, f32[2,8,128]{2,1,0:T(8,128)}) custom-call(s32[5]{0:T(128)} %pad_add_fusion.refs_0_.meta, bf16[6,512,1024]{2,1,0:T(8,128)(2,1)} %get-tuple-element.45.own6, f32[2,512,1024]{2,1,0:T(8,128)S(1)} %collective-permute-done.21.refs_0_, ...), custom_call_target="tpu_custom_call", output_to_operand_aliasing={{0}: (7, {})} | custom-call | flops 1 | bytes 1 | tf_op jit(solution)/shard_map/pallas_call | solution.py:444
  229.2 0.8 reduce_sum.9
  230.0 1.2 collective-permute-start.22
  231.2 2.4 %collective-permute-done.22 = f32[2]{0:T(128)S(1)} collective-permute-done((f32[2]{0:T(128)S(1)}, f32[2]{0:T(128)S(1)}, u32[]{:S(2)}, u32[]{:S(2)}) %collective-permute-start.22) | collective-permute-done | bytes 40 | tf_op jit(solution)/shard_map/ppermute | solution.py:504
  233.6 0.5 add_bitcast_fusion
  (62 shorter events, 2.8 us)
Async XLA Ops:
  0.6 10.6 %copy-start.21 = (s32[1,2]{1,0:T(1,128)S(1)}, s32[1,2]{1,0:T(1,128)}, u32[]{:S(2)}) copy-start(s32[1,2]{1,0:T(1,128)} %param.3) | copy-start | bytes 28
  0.6 93.9 %collective-permute-start.3 = (f32[2,512,1024]{2,1,0:T(8,128)}, f32[2,512,1024]{2,1,0:T(8,128)}, u32[]{:S(2)}, u32[]{:S(2)}) collective-permute-start(f32[2,512,1024]{2,1,0:T(8,128)} %bitcast.15), channel_id=1, source_target_pairs={{1,0},{0,1},{3,2},{2,3},{5,4},{4,5},{7,6},{6,7},{9,8},{8,9},{11,10... | collective-permute-start | bytes 12582920 | tf_op jit(solution)/shard_map/ppermute | solution.py:504
  5.9 27.6 %collective-permute-start.1 = (f32[2,128,1024]{2,1,0:T(8,128)}, f32[2,128,1024]{2,1,0:T(8,128)S(1)}, u32[]{:S(2)}, u32[]{:S(2)}) collective-permute-start(f32[2,128,1024]{2,1,0:T(8,128)} %get-tuple-element.48), channel_id=1, source_target_pairs={{8,0},{10,2},{12,4},{14,6},{16,8},{18,10},{20,12},{22,14},{24,16},... | collective-permute-start | bytes 3145736 | tf_op jit(solution)/shard_map/ppermute | solution.py:501
  10.7 45.1 %collective-permute-start = (f32[2,128,1024]{2,1,0:T(8,128)S(1)}, f32[2,128,1024]{2,1,0:T(8,128)S(1)}, u32[]{:S(2)}, u32[]{:S(2)}) collective-permute-start(f32[2,128,1024]{2,1,0:T(8,128)S(1)} %get-tuple-element.47), channel_id=1, source_target_pairs={{8,0},{10,2},{12,4},{14,6},{16,8},{18,10},{20,12},{22,14},{24,16},... | collective-permute-start | bytes 3145736 | tf_op jit(solution)/shard_map/ppermute | solution.py:501
  33.4 24.4 %copy-start.2 = (f32[2,128,1024]{2,1,0:T(8,128)}, f32[2,128,1024]{2,1,0:T(8,128)S(1)}, u32[]{:S(2)}) copy-start(f32[2,128,1024]{2,1,0:T(8,128)S(1)} %collective-permute-done.1.refs_1_.refs_7_.refs_3_) | copy-start | bytes 3145732
  35.4 42.8 %collective-permute-start.6 = (f32[2,128,1024]{2,1,0:T(8,128)S(1)}, f32[2,128,1024]{2,1,0:T(8,128)S(1)}, u32[]{:S(2)}, u32[]{:S(2)}) collective-permute-start(f32[2,128,1024]{2,1,0:T(8,128)S(1)} %get-tuple-element.55), channel_id=1, source_target_pairs={{8,0},{10,2},{12,4},{14,6},{16,8},{18,10},{20,12},{22,14},{24,16},... | collective-permute-start | bytes 3145736 | tf_op jit(solution)/shard_map/ppermute | solution.py:501
  39.7 60.7 %collective-permute-start.4 = (f32[2,128,1024]{2,1,0:T(8,128)S(1)}, f32[2,128,1024]{2,1,0:T(8,128)}, u32[]{:S(2)}, u32[]{:S(2)}) collective-permute-start(f32[2,128,1024]{2,1,0:T(8,128)S(1)} %get-tuple-element.53), channel_id=1, source_target_pairs={{4,0},{6,2},{0,4},{2,6},{12,8},{14,10},{8,12},{10,14},{20,16},{22,... | collective-permute-start | bytes 3145736 | tf_op jit(solution)/shard_map/ppermute | solution.py:507
  55.8 23.3 %copy-start.3 = (f32[2,128,1024]{2,1,0:T(8,128)}, f32[2,128,1024]{2,1,0:T(8,128)S(1)}, u32[]{:S(2)}) copy-start(f32[2,128,1024]{2,1,0:T(8,128)S(1)} %collective-permute-done.refs_1_.refs_4_) | copy-start | bytes 3145732
  57.8 42.6 %collective-permute-start.2 = (f32[2,128,1024]{2,1,0:T(8,128)S(1)}, f32[2,128,1024]{2,1,0:T(8,128)S(1)}, u32[]{:S(2)}, u32[]{:S(2)}) collective-permute-start(f32[2,128,1024]{2,1,0:T(8,128)S(1)} %get-tuple-element.52), channel_id=1, source_target_pairs={{8,0},{10,2},{12,4},{14,6},{16,8},{18,10},{20,12},{22,14},{24,16},... | collective-permute-start | bytes 3145736 | tf_op jit(solution)/shard_map/ppermute | solution.py:501
  62.1 39.3 %collective-permute-start.5 = (f32[2,128,1024]{2,1,0:T(8,128)S(1)}, f32[2,128,1024]{2,1,0:T(8,128)S(1)}, u32[]{:S(2)}, u32[]{:S(2)}) collective-permute-start(f32[2,128,1024]{2,1,0:T(8,128)S(1)} %get-tuple-element.54), channel_id=1, source_target_pairs={{4,0},{6,2},{0,4},{2,6},{12,8},{14,10},{8,12},{10,14},{20,16},{22,... | collective-permute-start | bytes 3145736 | tf_op jit(solution)/shard_map/ppermute | solution.py:507
  78.3 22.1 %copy-start.4 = (f32[2,128,1024]{2,1,0:T(8,128)}, f32[2,128,1024]{2,1,0:T(8,128)S(1)}, u32[]{:S(2)}) copy-start(f32[2,128,1024]{2,1,0:T(8,128)S(1)} %collective-permute-done.6.refs_1_.refs_9_.refs_4_) | copy-start | bytes 3145732
  79.1 27.5 %collective-permute-start.7 = (f32[2,128,1024]{2,1,0:T(8,128)S(1)}, f32[2,128,1024]{2,1,0:T(8,128)S(1)}, u32[]{:S(2)}, u32[]{:S(2)}) collective-permute-start(f32[2,128,1024]{2,1,0:T(8,128)S(1)} %get-tuple-element.57), channel_id=1, source_target_pairs={{4,0},{6,2},{0,4},{2,6},{12,8},{14,10},{8,12},{10,14},{20,16},{22,... | collective-permute-start | bytes 3145736 | tf_op jit(solution)/shard_map/ppermute | solution.py:507
  100.4 1.0 copy-start
  101.4 5.2 %copy-start.18 = (f32[2,128,1024]{2,1,0:T(8,128)}, f32[2,128,1024]{2,1,0:T(8,128)S(1)}, u32[]{:S(2)}) copy-start(f32[2,128,1024]{2,1,0:T(8,128)S(1)} %collective-permute-done.5.refs_6_.refs_2_.refs_3_) | copy-start | bytes 3145732
  106.6 1.0 copy-start.20
  107.5 1.2 copy-start.1
  116.4 27.6 %copy-start.12 = (f32[2,128,1024]{2,1,0:T(8,128)}, f32[2,128,1024]{2,1,0:T(8,128)S(1)}, u32[]{:S(2)}) copy-start(f32[2,128,1024]{2,1,0:T(8,128)S(1)} %get-tuple-element.60) | copy-start | bytes 3145732
  116.4 7.6 %collective-permute-start.12 = (f32[2,512,1024]{2,1,0:T(8,128)}, f32[2,512,1024]{2,1,0:T(8,128)}, u32[]{:S(2)}, u32[]{:S(2)}) collective-permute-start(f32[2,512,1024]{2,1,0:T(8,128)} %get-tuple-element.65), channel_id=1, source_target_pairs={{2,0},{0,2},{6,4},{4,6},{10,8},{8,10},{14,12},{12,14},{18,16},{16,... | collective-permute-start | bytes 12582920 | tf_op jit(solution)/shard_map/ppermute | solution.py:510
  116.5 34.1 %collective-permute-start.15 = (f32[2,384,1024]{2,1,0:T(8,128)}, f32[2,384,1024]{2,1,0:T(8,128)}, u32[]{:S(2)}, u32[]{:S(2)}) collective-permute-start(f32[2,384,1024]{2,1,0:T(8,128)} %get-tuple-element.71), channel_id=1, source_target_pairs={{2,0},{0,2},{6,4},{4,6},{10,8},{8,10},{14,12},{12,14},{18,16},{16,... | collective-permute-start | bytes 9437192 | tf_op jit(solution)/shard_map/ppermute | solution.py:510
  117.0 27.0 %collective-permute-start.9 = (f32[2,128,1024]{2,1,0:T(8,128)S(1)}, f32[2,128,1024]{2,1,0:T(8,128)S(1)}, u32[]{:S(2)}, u32[]{:S(2)}) collective-permute-start(f32[2,128,1024]{2,1,0:T(8,128)S(1)} %get-tuple-element.61), channel_id=1, source_target_pairs={{8,0},{10,2},{12,4},{14,6},{16,8},{18,10},{20,12},{22,14},{24,16},... | collective-permute-start | bytes 3145736 | tf_op jit(solution)/shard_map/ppermute | solution.py:501
  117.4 26.7 %collective-permute-start.10 = (f32[2,128,1024]{2,1,0:T(8,128)S(1)}, f32[2,128,1024]{2,1,0:T(8,128)S(1)}, u32[]{:S(2)}, u32[]{:S(2)}) collective-permute-start(f32[2,128,1024]{2,1,0:T(8,128)S(1)} %get-tuple-element.62), channel_id=1, source_target_pairs={{4,0},{6,2},{0,4},{2,6},{12,8},{14,10},{8,12},{10,14},{20,16},{22,... | collective-permute-start | bytes 3145736 | tf_op jit(solution)/shard_map/ppermute | solution.py:507
  119.3 24.8 %collective-permute-start.11 = (f32[2,128,1024]{2,1,0:T(8,128)S(1)}, f32[2,128,1024]{2,1,0:T(8,128)S(1)}, u32[]{:S(2)}, u32[]{:S(2)}) collective-permute-start(f32[2,128,1024]{2,1,0:T(8,128)S(1)} %get-tuple-element.64), channel_id=1, source_target_pairs={{1,0},{0,1},{3,2},{2,3},{5,4},{4,5},{7,6},{6,7},{9,8},{8,9},{11,10... | collective-permute-start | bytes 3145736 | tf_op jit(solution)/shard_map/ppermute | solution.py:504
  144.1 3.1 %copy-start.6 = (f32[2,128,1024]{2,1,0:T(8,128)}, f32[2,128,1024]{2,1,0:T(8,128)S(1)}, u32[]{:S(2)}) copy-start(f32[2,128,1024]{2,1,0:T(8,128)S(1)} %collective-permute-done.9.refs_1_.refs_5_.refs_3_) | copy-start | bytes 3145732
  144.1 3.1 %copy-start.8 = (f32[2,128,1024]{2,1,0:T(8,128)}, f32[2,128,1024]{2,1,0:T(8,128)S(1)}, u32[]{:S(2)}) copy-start(f32[2,128,1024]{2,1,0:T(8,128)S(1)} %collective-permute-done.10.refs_4_.refs_5_.refs_2_) | copy-start | bytes 3145732
  144.1 3.1 %copy-start.7 = (f32[2,128,1024]{2,1,0:T(8,128)}, f32[2,128,1024]{2,1,0:T(8,128)S(1)}, u32[]{:S(2)}) copy-start(f32[2,128,1024]{2,1,0:T(8,128)S(1)} %collective-permute-done.11.refs_7_.refs_6_.refs_4_) | copy-start | bytes 3145732
  144.1 3.3 %copy-start.13 = (f32[2,128,1024]{2,1,0:T(8,128)S(1)}, f32[2,128,1024]{2,1,0:T(8,128)}, u32[]{:S(2)}) copy-start(f32[2,128,1024]{2,1,0:T(8,128)} %copy-done.12) | copy-start | bytes 3145732
  147.2 27.0 %copy-start.14 = (f32[2,128,1024]{2,1,0:T(8,128)}, f32[2,128,1024]{2,1,0:T(8,128)S(1)}, u32[]{:S(2)}) copy-start(f32[2,128,1024]{2,1,0:T(8,128)S(1)} %get-tuple-element.77) | copy-start | bytes 3145732
  147.2 27.0 %copy-start.16 = (f32[2,128,1024]{2,1,0:T(8,128)}, f32[2,128,1024]{2,1,0:T(8,128)S(1)}, u32[]{:S(2)}) copy-start(f32[2,128,1024]{2,1,0:T(8,128)S(1)} %get-tuple-element.76) | copy-start | bytes 3145732
  147.2 3.4 %collective-permute-start.16 = (f32[2,128,1024]{2,1,0:T(8,128)S(1)}, f32[2,128,1024]{2,1,0:T(8,128)S(1)}, u32[]{:S(2)}, u32[]{:S(2)}) collective-permute-start(f32[2,128,1024]{2,1,0:T(8,128)S(1)} %get-tuple-element.72), channel_id=1, source_target_pairs={{2,0},{0,2},{6,4},{4,6},{10,8},{8,10},{14,12},{12,14},{18,16},{16,... | collective-permute-start | bytes 3145736 | tf_op jit(solution)/shard_map/ppermute | solution.py:510
  147.4 26.8 %collective-permute-start.8 = (f32[2,128,1024]{2,1,0:T(8,128)S(1)}, f32[2,128,1024]{2,1,0:T(8,128)S(1)}, u32[]{:S(2)}, u32[]{:S(2)}) collective-permute-start(f32[2,128,1024]{2,1,0:T(8,128)S(1)} %copy-done.13), channel_id=1, source_target_pairs={{8,0},{10,2},{12,4},{14,6},{16,8},{18,10},{20,12},{22,14},{24,16},... | collective-permute-start | bytes 3145736 | tf_op jit(solution)/shard_map/ppermute | solution.py:501
  147.8 26.5 %collective-permute-start.13 = (f32[2,128,1024]{2,1,0:T(8,128)S(1)}, f32[2,128,1024]{2,1,0:T(8,128)S(1)}, u32[]{:S(2)}, u32[]{:S(2)}) collective-permute-start(f32[2,128,1024]{2,1,0:T(8,128)S(1)} %get-tuple-element.68), channel_id=1, source_target_pairs={{4,0},{6,2},{0,4},{2,6},{12,8},{14,10},{8,12},{10,14},{20,16},{22,... | collective-permute-start | bytes 3145736 | tf_op jit(solution)/shard_map/ppermute | solution.py:507
  150.0 25.0 %collective-permute-start.14 = (f32[2,128,1024]{2,1,0:T(8,128)S(1)}, f32[2,128,1024]{2,1,0:T(8,128)}, u32[]{:S(2)}, u32[]{:S(2)}) collective-permute-start(f32[2,128,1024]{2,1,0:T(8,128)S(1)} %get-tuple-element.69), channel_id=1, source_target_pairs={{1,0},{0,1},{3,2},{2,3},{5,4},{4,5},{7,6},{6,7},{9,8},{8,9},{11,10... | collective-permute-start | bytes 3145736 | tf_op jit(solution)/shard_map/ppermute | solution.py:504
  174.2 3.7 %copy-start.5 = (f32[2,128,1024]{2,1,0:T(8,128)}, f32[2,128,1024]{2,1,0:T(8,128)S(1)}, u32[]{:S(2)}) copy-start(f32[2,128,1024]{2,1,0:T(8,128)S(1)} %collective-permute-done.8.refs_1_.refs_3_) | copy-start | bytes 3145732
  174.2 3.7 %copy-start.11 = (f32[2,128,1024]{2,1,0:T(8,128)}, f32[2,128,1024]{2,1,0:T(8,128)S(1)}, u32[]{:S(2)}) copy-start(f32[2,128,1024]{2,1,0:T(8,128)S(1)} %collective-permute-done.13.refs_3_.refs_1_) | copy-start | bytes 3145732
  175.1 3.0 %copy-start.17 = (f32[2,128,1024]{2,1,0:T(8,128)S(1)}, f32[2,128,1024]{2,1,0:T(8,128)}, u32[]{:S(2)}) copy-start(f32[2,128,1024]{2,1,0:T(8,128)} %copy-done.16) | copy-start | bytes 3145732
  175.1 4.3 %copy-start.15 = (f32[2,128,1024]{2,1,0:T(8,128)S(1)}, f32[2,128,1024]{2,1,0:T(8,128)}, u32[]{:S(2)}) copy-start(f32[2,128,1024]{2,1,0:T(8,128)} %copy-done.14) | copy-start | bytes 3145732
  178.0 7.2 %collective-permute-start.20 = (f32[2,512,1024]{2,1,0:T(8,128)S(1)}, f32[2,512,1024]{2,1,0:T(8,128)S(1)}, u32[]{:S(2)}, u32[]{:S(2)}) collective-permute-start(f32[2,512,1024]{2,1,0:T(8,128)S(1)} %get-tuple-element.79), channel_id=1, source_target_pairs={{2,0},{0,2},{6,4},{4,6},{10,8},{8,10},{14,12},{12,14},{18,16},{16,... | collective-permute-start | bytes 12582920 | tf_op jit(solution)/shard_map/ppermute | solution.py:510
  178.1 25.6 %collective-permute-start.18 = (f32[2,128,1024]{2,1,0:T(8,128)S(1)}, f32[2,128,1024]{2,1,0:T(8,128)S(1)}, u32[]{:S(2)}, u32[]{:S(2)}) collective-permute-start(f32[2,128,1024]{2,1,0:T(8,128)S(1)} %copy-done.17), channel_id=1, source_target_pairs={{1,0},{0,1},{3,2},{2,3},{5,4},{4,5},{7,6},{6,7},{9,8},{8,9},{11,10... | collective-permute-start | bytes 3145736 | tf_op jit(solution)/shard_map/ppermute | solution.py:504
  179.3 25.9 %collective-permute-start.19 = (f32[2,128,1024]{2,1,0:T(8,128)S(1)}, f32[2,128,1024]{2,1,0:T(8,128)}, u32[]{:S(2)}, u32[]{:S(2)}) collective-permute-start(f32[2,128,1024]{2,1,0:T(8,128)S(1)} %copy-done.15), channel_id=1, source_target_pairs={{8,0},{10,2},{12,4},{14,6},{16,8},{18,10},{20,12},{22,14},{24,16},... | collective-permute-start | bytes 3145736 | tf_op jit(solution)/shard_map/ppermute | solution.py:501
  179.9 25.3 %collective-permute-start.17 = (f32[2,128,1024]{2,1,0:T(8,128)S(1)}, f32[2,128,1024]{2,1,0:T(8,128)S(1)}, u32[]{:S(2)}, u32[]{:S(2)}) collective-permute-start(f32[2,128,1024]{2,1,0:T(8,128)S(1)} %get-tuple-element.75), channel_id=1, source_target_pairs={{4,0},{6,2},{0,4},{2,6},{12,8},{14,10},{8,12},{10,14},{20,16},{22,... | collective-permute-start | bytes 3145736 | tf_op jit(solution)/shard_map/ppermute | solution.py:507
  185.2 2.0 copy-start.19
  203.6 4.0 %copy-start.9 = (f32[2,128,1024]{2,1,0:T(8,128)}, f32[2,128,1024]{2,1,0:T(8,128)S(1)}, u32[]{:S(2)}) copy-start(f32[2,128,1024]{2,1,0:T(8,128)S(1)} %collective-permute-done.18.refs_2_) | copy-start | bytes 3145732
  205.2 2.4 %copy-start.10 = (f32[2,128,1024]{2,1,0:T(8,128)}, f32[2,128,1024]{2,1,0:T(8,128)S(1)}, u32[]{:S(2)}) copy-start(f32[2,128,1024]{2,1,0:T(8,128)S(1)} %collective-permute-done.17.refs_1_) | copy-start | bytes 3145732
  207.6 7.2 %collective-permute-start.21 = (f32[2,512,1024]{2,1,0:T(8,128)S(1)}, f32[2,512,1024]{2,1,0:T(8,128)S(1)}, u32[]{:S(2)}, u32[]{:S(2)}) collective-permute-start(f32[2,512,1024]{2,1,0:T(8,128)S(1)} %get-tuple-element.82), channel_id=1, source_target_pairs={{2,0},{0,2},{6,4},{4,6},{10,8},{8,10},{14,12},{12,14},{18,16},{16,... | collective-permute-start | bytes 12582920 | tf_op jit(solution)/shard_map/ppermute | solution.py:510
  230.0 3.6 %collective-permute-start.22 = (f32[2]{0:T(128)S(1)}, f32[2]{0:T(128)S(1)}, u32[]{:S(2)}, u32[]{:S(2)}) collective-permute-start(f32[2]{0:T(128)S(1)} %broadcast_multiply_fusion), channel_id=1, source_target_pairs={{1,0},{0,1},{3,2},{2,3},{5,4},{4,5},{7,6},{6,7},{9,8},{8,9},{11,10... | collective-permute-start | bytes 32 | tf_op jit(solution)/shard_map/ppermute | solution.py:504
